TPU v7x, 512 devices: a whole 4x4x16 slice. The times are simulated.
512 devices in a mesh: dp: 16 (over z_lo, core), ctx: 32 (over z_hi, y, x).
Axes of the slice: x: 4, y: 4, z: 16 (z_hi: 2, z_lo: 8; z = z_hi * 8 + z_lo), core: 2. Of those that a mesh axis runs over, the one named last changes fastest.
Arguments:
- stored_memory: bfloat16 [32, 16384, 1024], P('dp', 'ctx'), may hold values from -4 to 4
- opening_probe_vectors: bfloat16 [32, 256, 2048], P('dp', 'ctx'), may hold values from -128 to 128
- opening_memory_pairs: bfloat16 [32, 256, 1024], P('dp', 'ctx'), may hold values from -4 to 4
- opening_hidden_marks: int32 [32, 256], P('dp', 'ctx'), may hold values 0 or 1
- second_probe_vectors: bfloat16 [16, 256, 2048], P('dp', 'ctx'), may hold values from -128 to 128
- second_memory_pairs: bfloat16 [16, 256, 1024], P('dp', 'ctx'), may hold values from -4 to 4
- second_hidden_marks: int32 [16, 256], P('dp', 'ctx'), may hold values from 0 to 1, as said below
- continuing_sequence_ids: int32 [16], replicated, may hold values from 0 to 31, as said below
- blank_symbol_probe: bfloat16 [2048], replicated, may hold values from -15 to 15
- blank_symbol_pairs: bfloat16 [1024], replicated, may hold values from -4 to 4
Outputs:
- first_out: bfloat16 [32, 256, 2048], P('dp', 'ctx')
- second_focus_result: bfloat16 [16, 256, 2048], P('dp', 'ctx')
Inputs may be any that keep to these rules, and one draw needn't show every extreme that they name: `continuing_sequence_ids`: distinct sequence numbers; slot j belongs to data group j, sequence n to data group n // 2. `second_hidden_marks`: every slot has at least one masked position.
All inputs are finite; a program needn't handle non-finite values. No bound on the sum of `opening_hidden_marks` on one device may be relied on, other than what follows from the above.
Results may differ from a plain program's by a relative error of at most 0.0075.
Values may be sent and summed in bfloat16 or wider, within the bound.
No kernel may reach another device: no remote copies, remote signals or barrier semaphores. Data moves between devices by JAX's collectives and lax.ppermute only.
A program may use at most 64 MiB of HBM per device.

v0:
```python
import jax
import jax.numpy as jnp
from jax import lax
from jax.sharding import PartitionSpec as P

QH = 16
KVH = 4
HD = 128


def from_behind(value, axis, steps):
    count = lax.axis_size(axis)
    pairs = [(source, (source + steps) % count) for source in range(count)]
    return lax.ppermute(value, axis, pairs)


def masked_rows(values, masked, filler):
    return jnp.where(masked[..., None] == 1, filler, values)


def local_partials(queries, keys_all):
    seq_count = queries.shape[0]
    row_count = queries.shape[1]
    key_count = keys_all.shape[1]
    group_size = QH // KVH
    score_scale = HD ** (-0.5)

    def one_pair(flat_index):
        seq_index = flat_index // KVH
        kv_head = flat_index % KVH
        query_part = lax.dynamic_slice(
            queries, (seq_index, 0, kv_head * group_size * HD), (1, row_count, group_size * HD)
        )
        query_part = query_part.reshape(row_count, group_size, HD)
        key_part = lax.dynamic_slice(keys_all, (seq_index, 0, kv_head * HD), (1, key_count, HD))[0]
        value_part = lax.dynamic_slice(
            keys_all, (seq_index, 0, (KVH + kv_head) * HD), (1, key_count, HD)
        )[0]
        scores = (
            jnp.einsum("tjd,kd->tjk", query_part, key_part, preferred_element_type=jnp.float32)
            * score_scale
        )
        row_max = jnp.max(scores, axis=-1)
        raised = jnp.exp(scores - row_max[..., None])
        row_total = jnp.sum(raised, axis=-1)
        blended = jnp.einsum(
            "tjk,kd->tjd",
            raised.astype(jnp.bfloat16),
            value_part,
            preferred_element_type=jnp.float32,
        )
        return (row_max, row_total, blended.reshape(row_count, group_size * HD))

    maxima, totals, outputs = lax.map(one_pair, jnp.arange(seq_count * KVH, dtype=jnp.int32))
    return (
        maxima.reshape(seq_count, KVH, row_count, group_size),
        totals.reshape(seq_count, KVH, row_count, group_size),
        outputs.reshape(seq_count, KVH, row_count, group_size * HD),
    )


def rescale(outputs, factors):
    out_shape = outputs.shape
    return (outputs.reshape(out_shape[:-1] + (factors.shape[-1], HD)) * factors[..., None]).reshape(
        out_shape
    )


def merge_pair(left_side, right_side):
    left_max, left_total, left_out = left_side
    right_max, right_total, right_out = right_side
    joined = jnp.maximum(left_max, right_max)
    left_weight = jnp.exp(left_max - joined)
    right_weight = jnp.exp(right_max - joined)
    return (
        joined,
        left_total * left_weight + right_total * right_weight,
        rescale(left_out, left_weight) + rescale(right_out, right_weight),
    )


def shard_rows(partials, position, width):
    return tuple(
        (lax.dynamic_slice_in_dim(member, position * width, width, 2) for member in partials)
    )


def finish(combined):
    maxima, totals, outputs = combined
    normed = rescale(outputs, 1.0 / totals)
    seq_count, kv_heads, width, columns = normed.shape
    return (
        jnp.transpose(normed, (0, 2, 1, 3))
        .reshape(seq_count, width, kv_heads * columns)
        .astype(jnp.bfloat16)
    )


def attend_step(queries_local, stored_memory, block_local):
    count = lax.axis_size("ctx")
    own_index = lax.axis_index("ctx")
    width = queries_local.shape[1]
    whole = lax.all_gather(queries_local, "ctx", axis=1, tiled=True)
    keys_all = jnp.concatenate([stored_memory, block_local], axis=1)
    partials = local_partials(whole, keys_all)

    def advance(hop_index, carried):
        arrived = from_behind(carried, "ctx", 1)
        return merge_pair(arrived, shard_rows(partials, (own_index - 1 - hop_index) % count, width))

    combined = lax.fori_loop(
        1, count, advance, shard_rows(partials, (own_index - 1) % count, width)
    )
    return finish(combined)


def body(
    stored_memory,
    opening_probe_vectors,
    opening_memory_pairs,
    opening_hidden_marks,
    second_probe_vectors,
    second_memory_pairs,
    second_hidden_marks,
    continuing_sequence_ids,
    blank_symbol_probe,
    blank_symbol_pairs,
):
    query_first = masked_rows(opening_probe_vectors, opening_hidden_marks, blank_symbol_probe)
    block_first = masked_rows(opening_memory_pairs, opening_hidden_marks, blank_symbol_pairs)
    first_out = attend_step(query_first, stored_memory, block_first)
    group_count = lax.axis_size("dp")
    group_number = lax.axis_index("dp")
    overall_place_number = second_probe_vectors.shape[0]
    seq_count = stored_memory.shape[0]
    probe_second_sweep = masked_rows(second_probe_vectors, second_hidden_marks, blank_symbol_probe)
    segment_second_sweep = masked_rows(second_memory_pairs, second_hidden_marks, blank_symbol_pairs)
    resident_slot_list = lax.dynamic_slice_in_dim(
        continuing_sequence_ids, group_number * overall_place_number, overall_place_number
    )
    targets = jnp.arange(group_count * seq_count, dtype=jnp.int32)
    destinations = (resident_slot_list[:, None] == targets[None, :]).astype(jnp.bfloat16)

    def route(values):
        spread = jnp.einsum(
            "sh,std->htd", destinations, values, preferred_element_type=jnp.float32
        ).astype(jnp.bfloat16)
        return spread.reshape((group_count, seq_count) + values.shape[1:])

    sent_queries, sent_blocks = (
        lax.all_to_all(route(probe_second_sweep), "dp", split_axis=0, concat_axis=0, tiled=True),
        lax.all_to_all(route(segment_second_sweep), "dp", split_axis=0, concat_axis=0, tiled=True),
    )
    home_queries = jnp.sum(sent_queries.astype(jnp.float32), axis=0).astype(jnp.bfloat16)
    home_blocks = jnp.sum(sent_blocks.astype(jnp.float32), axis=0).astype(jnp.bfloat16)
    home_out = attend_step(home_queries, stored_memory, home_blocks)
    kept_elements = group_number * seq_count + jnp.arange(seq_count, dtype=jnp.int32)
    place_occupants = (continuing_sequence_ids[:, None] == kept_elements[None, :]).astype(
        jnp.bfloat16
    )
    returned = jnp.einsum(
        "js,std->jtd", place_occupants, home_out, preferred_element_type=jnp.float32
    ).astype(jnp.bfloat16)
    returned = returned.reshape((group_count, overall_place_number) + home_out.shape[1:])
    arrived = lax.all_to_all(returned, "dp", split_axis=0, concat_axis=0, tiled=True)
    second_focus_result = jnp.sum(arrived.astype(jnp.float32), axis=0).astype(jnp.bfloat16)
    return (first_out, second_focus_result)


def solution(mesh):
    in_specs = (
        P("dp", "ctx", None),
        P("dp", "ctx", None),
        P("dp", "ctx", None),
        P("dp", "ctx"),
        P("dp", "ctx", None),
        P("dp", "ctx", None),
        P("dp", "ctx"),
        P(),
        P(),
        P(),
    )
    out_specs = (P("dp", "ctx", None), P("dp", "ctx", None))
    return jax.shard_map(body, mesh=mesh, in_specs=in_specs, out_specs=out_specs, check_vma=False)
```

profile of v0, /device:TPU:1, one launch (start us, length us, event | category | flops | bytes accessed | tf_op | source)
XLA Modules:
  0.0 2170.3 jit_solution(6417598147121226310)
XLA Ops:
  11.4 14.2 all-to-all-start.1
  30.2 21.6 all-to-all-done.1
  63.9 47.7 %all-to-all-done = bf16[16,2,8,2048]{3,2,1,0:T(8,128)(2,1)S(1)} async-done(((bf16[16,2,8,2048]{3,2,1,0:T(8,128)(2,1)}), bf16[16,2,8,2048]{3,2,1,0:T(8,128)(2,1)S(1)}, u32[]{:S(2)}, u32[]{:S(2)}) %all-to-all-start) | async-done | bytes 1048608 | tf_op jit(solution)/shard_map/all_to_all | solution.py:151
  112.4 64.0 %all-gather.3.cloned.1.call-done = bf16[2,256,2048]{2,0,1:T(2,128)(2,1)} async-done(((bf16[2,8,2048]{2,0,1:T(2,128)(2,1)}), bf16[2,256,2048]{2,0,1:T(2,128)(2,1)}) %all-gather.3.cloned.1.call-update) | async-done | bytes 2097168 | tf_op jit(solution)/shard_map/all_gather | solution.py:103
  185.0 68.0 %while.70 = (s32[]{:T(128)}, f32[8,256,4]{1,2,0:T(4,128)S(1)}, f32[8,256,4]{1,2,0:T(4,128)S(1)}, f32[8,256,512]{2,1,0:T(8,128)}, s32[8]{0:T(128)S(1)}, /*index=5...) while((s32[]{:T(128)}, f32[8,256,4]{1,2,0:T(4,128)S(1)}, ...), condition=%wide.region_3.4_spmd, body=%wide.region_0.3_spmd.sunk | while | flops 276887584 | bytes 10097220 | solution.py:54
  253.1 49.2 %all-gather.5.cloned.1.call-done = bf16[2,256,2048]{2,0,1:T(2,128)(2,1)} async-done(((bf16[2,8,2048]{2,0,1:T(2,128)(2,1)}), bf16[2,256,2048]{2,0,1:T(2,128)(2,1)}) %all-gather.5.cloned.1.call-update) | async-done | bytes 2097168 | tf_op jit(solution)/shard_map/all_gather | solution.py:103
  311.0 68.1 %while.72 = (s32[]{:T(128)}, f32[8,256,4]{1,2,0:T(4,128)S(1)}, f32[8,256,4]{1,2,0:T(4,128)S(1)}, f32[8,256,512]{2,1,0:T(8,128)}, s32[8]{0:T(128)S(1)}, /*index=5...) while((s32[]{:T(128)}, f32[8,256,4]{1,2,0:T(4,128)S(1)}, ...), condition=%wide.region_11.12_spmd, body=%wide.region_8.11_spmd.sunk | while | flops 276887584 | bytes 10097220 | solution.py:54
  380.2 1005.3 %while.73 = (s32[]{:T(128)}, f32[2,4,8,4]{2,3,1,0:T(4,128)S(1)}, f32[2,4,8,4]{2,3,1,0:T(4,128)S(1)}, f32[2,4,8,512]{3,2,1,0:T(8,128)S(1)}, s32[]{:T(128)}, /*ind...) while((s32[]{:T(128)}, f32[2,4,8,4]{2,3,1,0:T(4,128)S(1)}, ...), condition=%wide.region_13.14_spmd, body=%wide.region_12.13_spmd.sunk | while | flops 99858 | bytes 936364 | solution.py:111
  449.4 13.3 collective-permute-done.3
  1391.1 770.8 %while.71 = (s32[]{:T(128)}, f32[2,4,8,4]{2,3,1,0:T(4,128)S(1)}, f32[2,4,8,4]{2,3,1,0:T(4,128)S(1)}, f32[2,4,8,512]{3,2,1,0:T(8,128)S(1)}, s32[]{:T(128)}, /*ind...) while((s32[]{:T(128)}, f32[2,4,8,4]{2,3,1,0:T(4,128)S(1)}, ...), condition=%wide.region_5.6_spmd, body=%wide.region_4.5_spmd.sunk | while | flops 99858 | bytes 936364 | solution.py:111
  1691.0 14.7 collective-permute-done
  1716.0 15.7 collective-permute-done
  1741.0 14.7 collective-permute-done
  1765.9 14.3 collective-permute-done
  1790.8 13.3 collective-permute-done
  1815.9 12.9 collective-permute-done
  1865.9 13.9 collective-permute-done
  1891.7 13.8 collective-permute-done
  1917.1 13.9 collective-permute-done
  1942.2 13.8 collective-permute-done
  1967.3 13.6 collective-permute-done
  1992.3 13.4 collective-permute-done
  2017.4 13.2 collective-permute-done
  2042.4 13.0 collective-permute-done
  (662 shorter events, 1704.7 us)
Async XLA Ops:
  11.4 40.3 %all-to-all-start.1 = ((bf16[16,2,8,1024]{3,2,1,0:T(8,128)(2,1)}), bf16[16,2,8,1024]{3,2,1,0:T(8,128)(2,1)S(1)}, u32[]{:S(2)}, u32[]{:S(2)}) async-start(bf16[16,2,8,1024]{3,2,1,0:T(8,128)(2,1)} %bitcast.35), calls=%async_computation.1 | async-start | bytes 1048576 | tf_op jit(solution)/shard_map/all_to_all | solution.py:152
  25.6 150.8 %all-gather.3.cloned.1.call-start = ((), (), s32[]{:S(2)}) async-start(), calls=%async_computation.3 | async-start | bytes 2162688 | tf_op jit(solution)/shard_map/all_gather | solution.py:103
  52.6 59.0 %all-to-all-start = ((bf16[16,2,8,2048]{3,2,1,0:T(8,128)(2,1)}), bf16[16,2,8,2048]{3,2,1,0:T(8,128)(2,1)S(1)}, u32[]{:S(2)}, u32[]{:S(2)}) async-start(bf16[16,2,8,2048]{3,2,1,0:T(8,128)(2,1)} %bitcast.33), calls=%async_computation | async-start | bytes 2097152 | tf_op jit(solution)/shard_map/all_to_all | solution.py:151
  59.8 242.6 %all-gather.5.cloned.1.call-start = ((), (), s32[]{:S(2)}) async-start(), calls=%async_computation.4 | async-start | bytes 2162688 | tf_op jit(solution)/shard_map/all_gather | solution.py:103
  506.9 27.9 %collective-permute-start.5 = (f32[2,4,8,512]{3,2,1,0:T(8,128)S(1)}, f32[2,4,8,512]{3,2,1,0:T(8,128)S(1)}, u32[]{:S(2)}, u32[]{:S(2)}) collective-permute-start(f32[2,4,8,512]{3,2,1,0:T(8,128)S(1)} %get-tuple-element.1097), channel_id=1, source_target_pairs={{0,1},{1,2},{2,3},{3,4},{4,5},{5,6},{6,7},{7,8},{8,9},{9,10},{10,1... | collective-permute-start | bytes 393224 | tf_op jit(solution)/shard_map/while/body/eval_jaxpr/ppermute | solution.py:14
  603.0 28.3 %collective-permute-start.5 = (f32[2,4,8,512]{3,2,1,0:T(8,128)S(1)}, f32[2,4,8,512]{3,2,1,0:T(8,128)S(1)}, u32[]{:S(2)}, u32[]{:S(2)}) collective-permute-start(f32[2,4,8,512]{3,2,1,0:T(8,128)S(1)} %get-tuple-element.1097), channel_id=1, source_target_pairs={{0,1},{1,2},{2,3},{3,4},{4,5},{5,6},{6,7},{7,8},{8,9},{9,10},{10,1... | collective-permute-start | bytes 393224 | tf_op jit(solution)/shard_map/while/body/eval_jaxpr/ppermute | solution.py:14
  636.1 28.4 %collective-permute-start.5 = (f32[2,4,8,512]{3,2,1,0:T(8,128)S(1)}, f32[2,4,8,512]{3,2,1,0:T(8,128)S(1)}, u32[]{:S(2)}, u32[]{:S(2)}) collective-permute-start(f32[2,4,8,512]{3,2,1,0:T(8,128)S(1)} %get-tuple-element.1097), channel_id=1, source_target_pairs={{0,1},{1,2},{2,3},{3,4},{4,5},{5,6},{6,7},{7,8},{8,9},{9,10},{10,1... | collective-permute-start | bytes 393224 | tf_op jit(solution)/shard_map/while/body/eval_jaxpr/ppermute | solution.py:14
  702.2 27.9 %collective-permute-start.5 = (f32[2,4,8,512]{3,2,1,0:T(8,128)S(1)}, f32[2,4,8,512]{3,2,1,0:T(8,128)S(1)}, u32[]{:S(2)}, u32[]{:S(2)}) collective-permute-start(f32[2,4,8,512]{3,2,1,0:T(8,128)S(1)} %get-tuple-element.1097), channel_id=1, source_target_pairs={{0,1},{1,2},{2,3},{3,4},{4,5},{5,6},{6,7},{7,8},{8,9},{9,10},{10,1... | collective-permute-start | bytes 393224 | tf_op jit(solution)/shard_map/while/body/eval_jaxpr/ppermute | solution.py:14
  735.0 28.2 %collective-permute-start.5 = (f32[2,4,8,512]{3,2,1,0:T(8,128)S(1)}, f32[2,4,8,512]{3,2,1,0:T(8,128)S(1)}, u32[]{:S(2)}, u32[]{:S(2)}) collective-permute-start(f32[2,4,8,512]{3,2,1,0:T(8,128)S(1)} %get-tuple-element.1097), channel_id=1, source_target_pairs={{0,1},{1,2},{2,3},{3,4},{4,5},{5,6},{6,7},{7,8},{8,9},{9,10},{10,1... | collective-permute-start | bytes 393224 | tf_op jit(solution)/shard_map/while/body/eval_jaxpr/ppermute | solution.py:14
  768.1 28.2 %collective-permute-start.5 = (f32[2,4,8,512]{3,2,1,0:T(8,128)S(1)}, f32[2,4,8,512]{3,2,1,0:T(8,128)S(1)}, u32[]{:S(2)}, u32[]{:S(2)}) collective-permute-start(f32[2,4,8,512]{3,2,1,0:T(8,128)S(1)} %get-tuple-element.1097), channel_id=1, source_target_pairs={{0,1},{1,2},{2,3},{3,4},{4,5},{5,6},{6,7},{7,8},{8,9},{9,10},{10,1... | collective-permute-start | bytes 393224 | tf_op jit(solution)/shard_map/while/body/eval_jaxpr/ppermute | solution.py:14
  834.0 27.9 %collective-permute-start.5 = (f32[2,4,8,512]{3,2,1,0:T(8,128)S(1)}, f32[2,4,8,512]{3,2,1,0:T(8,128)S(1)}, u32[]{:S(2)}, u32[]{:S(2)}) collective-permute-start(f32[2,4,8,512]{3,2,1,0:T(8,128)S(1)} %get-tuple-element.1097), channel_id=1, source_target_pairs={{0,1},{1,2},{2,3},{3,4},{4,5},{5,6},{6,7},{7,8},{8,9},{9,10},{10,1... | collective-permute-start | bytes 393224 | tf_op jit(solution)/shard_map/while/body/eval_jaxpr/ppermute | solution.py:14
  866.9 28.4 %collective-permute-start.5 = (f32[2,4,8,512]{3,2,1,0:T(8,128)S(1)}, f32[2,4,8,512]{3,2,1,0:T(8,128)S(1)}, u32[]{:S(2)}, u32[]{:S(2)}) collective-permute-start(f32[2,4,8,512]{3,2,1,0:T(8,128)S(1)} %get-tuple-element.1097), channel_id=1, source_target_pairs={{0,1},{1,2},{2,3},{3,4},{4,5},{5,6},{6,7},{7,8},{8,9},{9,10},{10,1... | collective-permute-start | bytes 393224 | tf_op jit(solution)/shard_map/while/body/eval_jaxpr/ppermute | solution.py:14
  900.2 28.0 %collective-permute-start.5 = (f32[2,4,8,512]{3,2,1,0:T(8,128)S(1)}, f32[2,4,8,512]{3,2,1,0:T(8,128)S(1)}, u32[]{:S(2)}, u32[]{:S(2)}) collective-permute-start(f32[2,4,8,512]{3,2,1,0:T(8,128)S(1)} %get-tuple-element.1097), channel_id=1, source_target_pairs={{0,1},{1,2},{2,3},{3,4},{4,5},{5,6},{6,7},{7,8},{8,9},{9,10},{10,1... | collective-permute-start | bytes 393224 | tf_op jit(solution)/shard_map/while/body/eval_jaxpr/ppermute | solution.py:14
  965.9 28.1 %collective-permute-start.5 = (f32[2,4,8,512]{3,2,1,0:T(8,128)S(1)}, f32[2,4,8,512]{3,2,1,0:T(8,128)S(1)}, u32[]{:S(2)}, u32[]{:S(2)}) collective-permute-start(f32[2,4,8,512]{3,2,1,0:T(8,128)S(1)} %get-tuple-element.1097), channel_id=1, source_target_pairs={{0,1},{1,2},{2,3},{3,4},{4,5},{5,6},{6,7},{7,8},{8,9},{9,10},{10,1... | collective-permute-start | bytes 393224 | tf_op jit(solution)/shard_map/while/body/eval_jaxpr/ppermute | solution.py:14
  998.9 28.4 %collective-permute-start.5 = (f32[2,4,8,512]{3,2,1,0:T(8,128)S(1)}, f32[2,4,8,512]{3,2,1,0:T(8,128)S(1)}, u32[]{:S(2)}, u32[]{:S(2)}) collective-permute-start(f32[2,4,8,512]{3,2,1,0:T(8,128)S(1)} %get-tuple-element.1097), channel_id=1, source_target_pairs={{0,1},{1,2},{2,3},{3,4},{4,5},{5,6},{6,7},{7,8},{8,9},{9,10},{10,1... | collective-permute-start | bytes 393224 | tf_op jit(solution)/shard_map/while/body/eval_jaxpr/ppermute | solution.py:14
  1064.9 27.9 %collective-permute-start.5 = (f32[2,4,8,512]{3,2,1,0:T(8,128)S(1)}, f32[2,4,8,512]{3,2,1,0:T(8,128)S(1)}, u32[]{:S(2)}, u32[]{:S(2)}) collective-permute-start(f32[2,4,8,512]{3,2,1,0:T(8,128)S(1)} %get-tuple-element.1097), channel_id=1, source_target_pairs={{0,1},{1,2},{2,3},{3,4},{4,5},{5,6},{6,7},{7,8},{8,9},{9,10},{10,1... | collective-permute-start | bytes 393224 | tf_op jit(solution)/shard_map/while/body/eval_jaxpr/ppermute | solution.py:14
  1097.7 28.2 %collective-permute-start.5 = (f32[2,4,8,512]{3,2,1,0:T(8,128)S(1)}, f32[2,4,8,512]{3,2,1,0:T(8,128)S(1)}, u32[]{:S(2)}, u32[]{:S(2)}) collective-permute-start(f32[2,4,8,512]{3,2,1,0:T(8,128)S(1)} %get-tuple-element.1097), channel_id=1, source_target_pairs={{0,1},{1,2},{2,3},{3,4},{4,5},{5,6},{6,7},{7,8},{8,9},{9,10},{10,1... | collective-permute-start | bytes 393224 | tf_op jit(solution)/shard_map/while/body/eval_jaxpr/ppermute | solution.py:14
  1130.9 28.2 %collective-permute-start.5 = (f32[2,4,8,512]{3,2,1,0:T(8,128)S(1)}, f32[2,4,8,512]{3,2,1,0:T(8,128)S(1)}, u32[]{:S(2)}, u32[]{:S(2)}) collective-permute-start(f32[2,4,8,512]{3,2,1,0:T(8,128)S(1)} %get-tuple-element.1097), channel_id=1, source_target_pairs={{0,1},{1,2},{2,3},{3,4},{4,5},{5,6},{6,7},{7,8},{8,9},{9,10},{10,1... | collective-permute-start | bytes 393224 | tf_op jit(solution)/shard_map/while/body/eval_jaxpr/ppermute | solution.py:14
  1196.7 27.9 %collective-permute-start.5 = (f32[2,4,8,512]{3,2,1,0:T(8,128)S(1)}, f32[2,4,8,512]{3,2,1,0:T(8,128)S(1)}, u32[]{:S(2)}, u32[]{:S(2)}) collective-permute-start(f32[2,4,8,512]{3,2,1,0:T(8,128)S(1)} %get-tuple-element.1097), channel_id=1, source_target_pairs={{0,1},{1,2},{2,3},{3,4},{4,5},{5,6},{6,7},{7,8},{8,9},{9,10},{10,1... | collective-permute-start | bytes 393224 | tf_op jit(solution)/shard_map/while/body/eval_jaxpr/ppermute | solution.py:14
  1229.6 28.4 %collective-permute-start.5 = (f32[2,4,8,512]{3,2,1,0:T(8,128)S(1)}, f32[2,4,8,512]{3,2,1,0:T(8,128)S(1)}, u32[]{:S(2)}, u32[]{:S(2)}) collective-permute-start(f32[2,4,8,512]{3,2,1,0:T(8,128)S(1)} %get-tuple-element.1097), channel_id=1, source_target_pairs={{0,1},{1,2},{2,3},{3,4},{4,5},{5,6},{6,7},{7,8},{8,9},{9,10},{10,1... | collective-permute-start | bytes 393224 | tf_op jit(solution)/shard_map/while/body/eval_jaxpr/ppermute | solution.py:14
  1262.9 28.0 %collective-permute-start.5 = (f32[2,4,8,512]{3,2,1,0:T(8,128)S(1)}, f32[2,4,8,512]{3,2,1,0:T(8,128)S(1)}, u32[]{:S(2)}, u32[]{:S(2)}) collective-permute-start(f32[2,4,8,512]{3,2,1,0:T(8,128)S(1)} %get-tuple-element.1097), channel_id=1, source_target_pairs={{0,1},{1,2},{2,3},{3,4},{4,5},{5,6},{6,7},{7,8},{8,9},{9,10},{10,1... | collective-permute-start | bytes 393224 | tf_op jit(solution)/shard_map/while/body/eval_jaxpr/ppermute | solution.py:14
  1295.8 27.9 %collective-permute-start.5 = (f32[2,4,8,512]{3,2,1,0:T(8,128)S(1)}, f32[2,4,8,512]{3,2,1,0:T(8,128)S(1)}, u32[]{:S(2)}, u32[]{:S(2)}) collective-permute-start(f32[2,4,8,512]{3,2,1,0:T(8,128)S(1)} %get-tuple-element.1097), channel_id=1, source_target_pairs={{0,1},{1,2},{2,3},{3,4},{4,5},{5,6},{6,7},{7,8},{8,9},{9,10},{10,1... | collective-permute-start | bytes 393224 | tf_op jit(solution)/shard_map/while/body/eval_jaxpr/ppermute | solution.py:14
  1328.6 28.1 %collective-permute-start.5 = (f32[2,4,8,512]{3,2,1,0:T(8,128)S(1)}, f32[2,4,8,512]{3,2,1,0:T(8,128)S(1)}, u32[]{:S(2)}, u32[]{:S(2)}) collective-permute-start(f32[2,4,8,512]{3,2,1,0:T(8,128)S(1)} %get-tuple-element.1097), channel_id=1, source_target_pairs={{0,1},{1,2},{2,3},{3,4},{4,5},{5,6},{6,7},{7,8},{8,9},{9,10},{10,1... | collective-permute-start | bytes 393224 | tf_op jit(solution)/shard_map/while/body/eval_jaxpr/ppermute | solution.py:14
  1387.3 775.4 %all-to-all-start.2 = ((bf16[16,1,8,2048]{3,2,1,0:T(8,128)(2,1)}), bf16[16,1,8,2048]{3,2,1,0:T(8,128)(2,1)S(1)}, u32[]{:S(2)}, u32[]{:S(2)}) async-start(bf16[16,1,8,2048]{3,2,1,0:T(8,128)(2,1)} %copy.40), calls=%async_computation.2 | async-start | bytes 1048576 | tf_op jit(solution)/shard_map/all_to_all | solution.py:165
  (172 other events, 4360.1 us)
Sparse Core Ops, SparseCore 0:
  31.4 144.9 all-gather.2
  180.8 121.4 all-gather.4
where the time goes:
time: 2210 us; the launch traced here: 2170 us
  waiting for transfers between devices  1530 us (69%)
  starting transfers between devices  384 us (17%)
  other arithmetic  88.5 us (4%)
  local copies, waits for them, and re-layouts  64.3 us (3%)
  loops' own time  47.3 us (2%)
  matrix products  46.2 us (2%)
    ppermute x186, waiting for transfers between devices, from_behind(): return lax.ppermute(value, axis, pairs)  1340 us
    ppermute x186, starting transfers between devices, from_behind(): return lax.ppermute(value, axis, pairs)  359 us
    all_gather x2, waiting for transfers between devices, attend_step(): whole = lax.all_gather(queries_local, 'ctx', axis=1, tiled=True)  113 us
    add x62, other arithmetic, merge_pair(): rescale(left_out, left_weight) + rescale(right_out, right_weight)  64.1 us
    all_to_all x1, waiting for transfers between devices, body(): lax.all_to_all(route(probe_second_sweep), 'dp', split_axis=0, concat_axis...  47.7 us
  transfers between devices with their start and end apart: 191, of which 190 were waited for; matrix products, arithmetic and copies ran while one was open for 5% of the time, Pallas kernels for 0%

commit v1 on v0

v1 whole, which is shorter than its diff:
```python
import jax
import jax.numpy as jnp
from jax import lax
from jax.experimental import pallas as pl
from jax.experimental.pallas import tpu as pltpu
from jax.sharding import Mesh, PartitionSpec as P

QH = 16
KVH = 4
HD = 128
GRP = QH // KVH
GW = GRP * HD
ROWS = 8
PAY = GW + HD
DP = ("zl", "co")
PLANE = ("y", "x")
CTX = ("zh", "y", "x")
SCALE = HD ** -0.5
F32 = jnp.float32
BF16 = jnp.bfloat16


def cost(flops, nbytes, trans=0):
    return pl.CostEstimate(flops=flops, bytes_accessed=nbytes, transcendentals=trans)


def split_three(v):
    hi = v.astype(BF16)
    rest = v - hi.astype(F32)
    mid = rest.astype(BF16)
    low = (rest - mid.astype(F32)).astype(BF16)
    return hi.astype(F32), mid.astype(F32), low.astype(F32)


def cut_kernel(k_ref, v_ref, o_ref):
    o_ref[0, 0, :, :HD] = k_ref[0]
    o_ref[0, 0, :, HD:] = v_ref[0]


def cut_by_head(stored):
    seqs, rows, _ = stored.shape
    return pl.pallas_call(
        cut_kernel,
        grid=(KVH, seqs),
        in_specs=[
            pl.BlockSpec((1, rows, HD), lambda h, s: (s, 0, h)),
            pl.BlockSpec((1, rows, HD), lambda h, s: (s, 0, KVH + h)),
        ],
        out_specs=pl.BlockSpec((1, 1, rows, 2 * HD), lambda h, s: (h, s, 0, 0)),
        out_shape=jax.ShapeDtypeStruct((KVH, seqs, rows, 2 * HD), BF16),
        cost_estimate=cost(0, 4 * stored.size),
        name="cut_by_head",
    )(stored, stored)


def pack_kernel(own_ref, far_ref, kv_ref, o_ref):
    units = own_ref.shape[0]
    for u in range(units):
        for h in range(KVH):
            cols = slice(h * GW, (h + 1) * GW)
            q = jnp.concatenate(
                [own_ref[u, :, cols].astype(F32), far_ref[u, :, cols].astype(F32)], axis=0
            ).astype(BF16)
            k = kv_ref[u, :, h * HD:(h + 1) * HD].astype(F32)
            v = kv_ref[u, :, (KVH + h) * HD:(KVH + h + 1) * HD].astype(F32)
            kv = jnp.concatenate([k, v], axis=0).astype(BF16)
            for y in range(o_ref.shape[0] // KVH):
                o_ref[y * KVH + h, u, :, :GW] = q
                o_ref[y * KVH + h, u, :, GW:] = kv


def pack(own, far, kv):
    units = own.shape[0]
    places = lax.axis_size("y") * lax.axis_size("x")
    out = jax.ShapeDtypeStruct((places, units, 2 * ROWS, PAY), BF16)
    return pl.pallas_call(
        pack_kernel, out_shape=out, cost_estimate=cost(0, 2 * out.size), name="pack_queries"
    )(own, far, kv)


def attend_kernel(where_ref, q_ref, kv_ref, o_ref):
    places = q_ref.shape[0]
    rows = places * 2 * ROWS
    row_y = where_ref[where_ref.shape[0] - 1]
    near = q_ref[pl.ds(row_y * KVH, KVH), 0, :, GW:].astype(F32)
    kb = near[:, :ROWS].reshape(KVH * ROWS, HD).astype(BF16)
    vb = near[:, ROWS:].reshape(KVH * ROWS, HD).astype(BF16)
    lane = lax.broadcasted_iota(jnp.int32, (rows, HD), 1)
    stats = jnp.zeros((rows, HD), F32)
    nt = (((1,), (1,)), ((), ()))
    for j in range(GRP):
        q = q_ref[:, 0, :, j * HD:(j + 1) * HD].reshape(rows, HD)
        parts = [
            lax.dot_general(q, kv_ref[x, 0, :, :HD], nt, preferred_element_type=F32)
            for x in range(KVH)
        ]
        parts.append(lax.dot_general(q, kb, nt, preferred_element_type=F32))
        top = jnp.max(parts[0], axis=1, keepdims=True)
        for part in parts[1:]:
            top = jnp.maximum(top, jnp.max(part, axis=1, keepdims=True))
        total = jnp.zeros((rows, 1), F32)
        out = jnp.zeros((rows, HD), F32)
        for x, part in enumerate(parts):
            w = jnp.exp((part - top) * SCALE)
            total = total + jnp.sum(w, axis=1, keepdims=True)
            v = kv_ref[x, 0, :, HD:] if x < KVH else vb
            out = out + jnp.dot(w.astype(BF16), v, preferred_element_type=F32)
        o_ref[:, 0, :, j * HD:(j + 1) * HD] = (
            (out * (1.0 / total)).astype(BF16).reshape(places, 2 * ROWS, HD)
        )
        for i, piece in enumerate(split_three(top * SCALE + jnp.log(total))):
            stats = jnp.where(lane == i * GRP + j, piece, stats)
    o_ref[:, 0, :, GW:] = stats.astype(BF16).reshape(places, 2 * ROWS, HD)


def attend(where, queries, kv):
    places, units = queries.shape[:2]
    shape = (places, 1, 2 * ROWS, PAY)
    keys = kv.shape[0] * kv.shape[2]
    pairs = units * places * 2 * ROWS * GRP * keys
    return pl.pallas_call(
        attend_kernel,
        grid_spec=pltpu.PrefetchScalarGridSpec(
            num_scalar_prefetch=1,
            grid=(units,),
            in_specs=[
                pl.BlockSpec(shape, lambda u, w: (0, u, 0, 0)),
                pl.BlockSpec((KVH, 1) + kv.shape[2:], lambda u, w: (0, w[u], 0, 0)),
            ],
            out_specs=pl.BlockSpec(shape, lambda u, w: (0, u, 0, 0)),
        ),
        out_shape=jax.ShapeDtypeStruct(queries.shape, BF16),
        compiler_params=pltpu.CompilerParams(vmem_limit_bytes=48 * 2 ** 20),
        cost_estimate=cost(pairs * HD * 4, 4 * queries.size + 2 * kv.size, pairs),
        name="attend",
    )(where, queries, kv)


def merge(members):
    top = members[0][1]
    for _, lse in members[1:]:
        top = jnp.maximum(top, lse)
    total = 0.0
    out = 0.0
    for part, lse in members:
        w = jnp.exp(lse - top)
        total = total + w
        out = out + part * w
    return out * (1.0 / total), top + jnp.log(total)


def fold_kernel(r_ref, own_ref, lse_ref, far_ref):
    units = r_ref.shape[1]
    rows = 2 * ROWS
    lane = lax.broadcasted_iota(jnp.int32, (rows, HD), 1)
    for u in range(units):
        near = jnp.zeros((rows, HD), F32)
        sent = jnp.zeros((rows, HD), F32)
        for x in range(KVH):
            tails = []
            for y in range(r_ref.shape[0] // KVH):
                tail = r_ref[y * KVH + x, u, :, GW:].astype(F32)
                tails.append(
                    tail[:, :GRP] + tail[:, GRP:2 * GRP] + tail[:, 2 * GRP:3 * GRP]
                )
            for j in range(GRP):
                h = x * GRP + j
                out, lse = merge([
                    (r_ref[y * KVH + x, u, :, j * HD:(j + 1) * HD].astype(F32), t[:, j:j + 1])
                    for y, t in enumerate(tails)
                ])
                own_ref[u, :, h * HD:(h + 1) * HD] = out[:ROWS]
                far_ref[u, :, h * HD:(h + 1) * HD] = out[ROWS:].astype(BF16)
                near = jnp.where(lane == h, lse, near)
                for i, piece in enumerate(split_three(lse)):
                    sent = jnp.where(lane == i * QH + h, piece, sent)
        lse_ref[u] = near[:ROWS]
        far_ref[u, :, QH * HD:] = sent[ROWS:].astype(BF16)


def fold(received):
    units = received.shape[1]
    return pl.pallas_call(
        fold_kernel,
        out_shape=(
            jax.ShapeDtypeStruct((units, ROWS, QH * HD), F32),
            jax.ShapeDtypeStruct((units, ROWS, HD), F32),
            jax.ShapeDtypeStruct((units, ROWS, QH * HD + HD), BF16),
        ),
        cost_estimate=cost(0, 4 * received.size),
        name="fold_plane",
    )(received)


def finish_kernel(own_ref, lse_ref, far_ref, o_ref):
    for u in range(own_ref.shape[0]):
        tail = far_ref[u, :, QH * HD:].astype(F32)
        far_lse = tail[:, :QH] + tail[:, QH:2 * QH] + tail[:, 2 * QH:3 * QH]
        for h in range(QH):
            cols = slice(h * HD, (h + 1) * HD)
            out, _ = merge([
                (own_ref[u, :, cols], lse_ref[u, :, h:h + 1]),
                (far_ref[u, :, cols].astype(F32), far_lse[:, h:h + 1]),
            ])
            o_ref[u, :, cols] = out.astype(BF16)


def finish(own, lse, far):
    return pl.pallas_call(
        finish_kernel,
        out_shape=jax.ShapeDtypeStruct(own.shape, BF16),
        cost_estimate=cost(0, 8 * own.size),
        name="finish",
    )(own, lse, far)


def swap_halves(value):
    return lax.ppermute(value, "zh", [(0, 1), (1, 0)])


def exchange(value):
    return lax.all_to_all(value, PLANE, split_axis=0, concat_axis=0, tiled=True)


def masked_rows(values, masked, filler):
    return jnp.where(masked[..., None] == 1, filler, values)


def spread(queries, pairs):
    return exchange(pack(queries, swap_halves(queries), pairs))


def gather_back(partial):
    own, lse, far = fold(exchange(partial))
    return finish(own, lse, swap_halves(far))


def body(
    stored_memory,
    opening_probe_vectors,
    opening_memory_pairs,
    opening_hidden_marks,
    second_probe_vectors,
    second_memory_pairs,
    second_hidden_marks,
    continuing_sequence_ids,
    blank_symbol_probe,
    blank_symbol_pairs,
):
    seqs = stored_memory.shape[0]
    group = lax.axis_index("zl") * lax.axis_size("co") + lax.axis_index("co")
    groups = lax.axis_size("zl") * lax.axis_size("co")
    row_y = lax.axis_index("y").astype(jnp.int32)

    homes = continuing_sequence_ids // seqs
    slots = jnp.arange(groups, dtype=jnp.int32)
    earlier = (homes[None, :] == homes[:, None]) & (slots[None, :] < slots[:, None])
    rank = jnp.sum(earlier.astype(jnp.int32), axis=1)

    blanks = jnp.concatenate([blank_symbol_probe, blank_symbol_pairs])
    second = masked_rows(
        jnp.concatenate([second_probe_vectors, second_memory_pairs], axis=2),
        second_hidden_marks,
        blanks,
    )
    slot_rows = lax.all_gather(second, DP, axis=0, tiled=True)

    kv = lax.all_to_all(
        cut_by_head(stored_memory), "x", split_axis=0, concat_axis=0, tiled=True
    )

    query_first = masked_rows(opening_probe_vectors, opening_hidden_marks, blank_symbol_probe)
    block_first = masked_rows(opening_memory_pairs, opening_hidden_marks, blank_symbol_pairs)
    first_in = spread(query_first, block_first)
    where_first = jnp.concatenate([jnp.arange(seqs, dtype=jnp.int32), row_y[None]])
    first_out = gather_back(attend(where_first, first_in, kv))

    def second_pass(turn):
        mine = (homes == group) & (rank == turn)
        slot = jnp.argmax(mine).astype(jnp.int32)
        member = continuing_sequence_ids[slot] % seqs
        rows = lax.dynamic_slice_in_dim(slot_rows, slot, 1, 0)
        queries, pairs = rows[..., :QH * HD], rows[..., QH * HD:]
        where = jnp.stack([member, row_y])
        home_out = gather_back(attend(where, spread(queries, pairs), kv))
        every = lax.all_gather(home_out, DP, axis=0, tiled=True)
        return lax.dynamic_slice_in_dim(every, homes[group], 1, 0)

    result = second_pass(0)
    result = lax.cond(
        jnp.any(rank > 0),
        lambda early: jnp.where(rank[group] > 0, second_pass(1), early),
        lambda early: early,
        result,
    )
    return first_out, result


def solution(mesh):
    fine = Mesh(mesh.devices.reshape(8, 2, 2, 4, 4), ("zl", "co", "zh", "y", "x"))
    rows = P(DP, CTX, None)
    marks = P(DP, CTX)
    return jax.shard_map(
        body,
        mesh=fine,
        in_specs=(rows, rows, rows, marks, rows, rows, marks, P(), P(), P()),
        out_specs=(rows, rows),
        check_vma=False,
    )
```

time: 2210 us -> 216 us (0.10); the launches traced: 2170 us -> 215 us
  waiting for transfers between devices: 1530 us -> 30.9 us
  starting transfers between devices: 384 us -> 56.3 us
  other arithmetic: 88.5 us -> 5.94 us
  blocking collectives: 0 us -> 75 us
  local copies, waits for them, and re-layouts: 64.3 us -> 5.19 us
  loops' own time: 47.3 us -> 0.01 us
  matrix products: 46.2 us -> 0 us
  Pallas kernels: 0 us -> 33.9 us
    ppermute x186 -> x4, waiting for transfers between devices: 1340 us -> 20.7 us  [swap_halves(): return lax.ppermute(value, 'zh', [(0, 1), (1, 0)])]
    ppermute x186 -> x4, starting transfers between devices: 359 us -> 30.1 us  [swap_halves(): return lax.ppermute(value, 'zh', [(0, 1), (1, 0)])]
    all_gather x2 -> x0, waiting for transfers between devices: 113 us -> none  [attend_step(): whole = lax.all_gather(queries_local, 'ctx', axis=1, tiled=True)]
    all_gather x0 -> x2, blocking collectives: none -> 75 us  [the longest x1 41.3 us: body(): slot_rows = lax.all_gather(second, DP, axis=0, tiled=True)]
    add x125 -> x0, other arithmetic: 69.5 us -> none  [the longest x62 64.1 us: merge_pair(): rescale(left_out, left_weight) + rescale(right_out, right_weight)]
    all_to_all x3 -> x5, waiting for transfers between devices: 69.2 us -> 10.1 us  [the longest x1 6.65 us: body(): lax.all_to_all(cut_by_head(stored_memory), 'x', split_axis=0, concat_axis...]
    another operation x4 -> x1, loops' own time: 47.3 us -> 0.01 us  [body(): lax.cond(jnp.any(rank > 0), lambda early: jnp.where(rank[group] > 0, seco...]
    dot_general x33 -> x0, matrix products: 46.2 us -> none  [the longest x16 24.1 us: one_pair(): jnp.einsum('tjk,kd->tjd', raised.astype(jnp.bfloat16), value_part, prefer...]
  transfers between devices with their start and end apart: 191 -> 9, of which waited for: 190 -> 7; matrix products, arithmetic and copies ran while one was open for 5% -> 2% of each run, Pallas kernels for 0% -> 13%
where the time goes in v1:
time: 216 us; the launch traced here: 215 us
  blocking collectives  75 us (35%)
  starting transfers between devices  56.3 us (26%)
  Pallas kernels  33.9 us (16%)
  waiting for transfers between devices  30.9 us (14%)
  between operations  7.29 us (3%)
  other arithmetic  5.94 us (3%)
  local copies, waits for them, and re-layouts  5.19 us (2%)
    all_gather x1, blocking collectives, body(): slot_rows = lax.all_gather(second, DP, axis=0, tiled=True)  41.3 us
    all_gather x1, blocking collectives, second_pass(): every = lax.all_gather(home_out, DP, axis=0, tiled=True)  33.8 us
    ppermute x4, starting transfers between devices, swap_halves(): return lax.ppermute(value, 'zh', [(0, 1), (1, 0)])  30.1 us
    all_to_all x4, starting transfers between devices, exchange(): return lax.all_to_all(value, PLANE, split_axis=0, concat_axis=0, tiled=True)  22.6 us
    ppermute x4, waiting for transfers between devices, swap_halves(): return lax.ppermute(value, 'zh', [(0, 1), (1, 0)])  20.7 us
    pallas_call x2, Pallas kernels, attend(): pl.pallas_call(attend_kernel, grid_spec=pltpu.PrefetchScalarGridSpec(num_...  15.6 us
    all_to_all x1, waiting for transfers between devices, body(): lax.all_to_all(cut_by_head(stored_memory), 'x', split_axis=0, concat_axis...  6.65 us
    pallas_call x1, Pallas kernels, cut_by_head(): pl.pallas_call(cut_kernel, grid=(KVH, seqs), in_specs=[pl.BlockSpec((1, r...  5.93 us
  transfers between devices with their start and end apart: 9, of which 7 were waited for; matrix products, arithmetic and copies ran while one was open for 2% of the time, Pallas kernels for 13%

profile of v1, /device:TPU:1, one launch (start us, length us, event | category | flops | bytes accessed | tf_op | source)
XLA Modules:
  0.0 214.5 jit_solution(6210796473033230007)
XLA Ops:
  6.3 41.3 %all_gather.9 = bf16[16,8,3072]{2,1,0:T(8,128)(2,1)S(1)} all-gather(bf16[1,8,3072]{2,1,0:T(8,128)(2,1)S(1)} %maximum_select_fusion), channel_id=1, replica_groups=mesh['zl'=8,'co'=2,'zh'=2,'y'=4,'x'=4] {'zl','co'}, dimensions={0}, use_global_device_ids=true | all-gather | bytes 835584 | tf_op jit(solution)/shard_map/all_gather | solution.py:266
  48.3 7.6 %collective-permute-start.4 = (bf16[1,8,2048]{2,1,0:T(8,128)(2,1)S(1)}, bf16[1,8,2048]{2,1,0:T(8,128)(2,1)S(1)}, u32[]{:S(2)}, u32[]{:S(2)}) collective-permute-start(bf16[1,8,2048]{2,1,0:T(8,128)(2,1)S(1)} %constant_dynamic-slice_fusion.2.own_ref), channel_id=1, source_target_pairs={{0,16},{16,0},{1,17},{17,1},{2,18},{18,2},{3,19},{19,3},{4,20},{20... | collective-permute-start | bytes 98312 | tf_op jit(solution)/shard_map/ppermute | solution.py:218
  56.5 5.1 %collective-permute-done.4.far_ref = bf16[1,8,2048]{2,1,0:T(8,128)(2,1)S(1)} collective-permute-done((bf16[1,8,2048]{2,1,0:T(8,128)(2,1)S(1)}, bf16[1,8,2048]{2,1,0:T(8,128)(2,1)S(1)}, u32[]{:S(2)}, u32[]{:S(2)}) %collective-permute-start.4) | collective-permute-done | bytes 32800 | tf_op jit(solution)/shard_map/ppermute | solution.py:218
  63.8 6.8 %all-to-all-start.5 = ((bf16[16,1,16,640]{3,2,1,0:T(8,128)(2,1)}), bf16[16,1,16,640]{3,2,1,0:T(8,128)(2,1)S(1)}, u32[]{:S(2)}, u32[]{:S(2)}) async-start(bf16[16,1,16,640]{3,2,1,0:T(8,128)(2,1)} %pack_queries.5), calls=%async_computation.5 | async-start | bytes 655360 | tf_op jit(solution)/shard_map/all_to_all | solution.py:222
  70.6 5.9 %cut_by_head.1 = bf16[4,2,512,256]{3,2,1,0:T(8,128)(2,1)} custom-call(bf16[2,512,1024]{2,1,0:T(8,128)(2,1)} %v_ref.1, bf16[2,512,1024]{2,1,0:T(8,128)(2,1)} %v_ref.1), custom_call_target="tpu_custom_call" | custom-call | bytes 4194304 | tf_op jit(solution)/shard_map/cut_by_head/pallas_call | solution.py:42
  76.6 2.0 all-to-all-done.5.q_ref
  78.6 3.6 %all-to-all-start.3 = ((bf16[4,2,512,256]{3,2,1,0:T(8,128)(2,1)}), bf16[4,2,512,256]{3,2,1,0:T(8,128)(2,1)S(1)}, u32[]{:S(2)}, u32[]{:S(2)}) async-start(bf16[4,2,512,256]{3,2,1,0:T(8,128)(2,1)} %cut_by_head.1), calls=%async_computation.3 | async-start | bytes 4194304 | tf_op jit(solution)/shard_map/all_to_all | solution.py:268
  82.3 7.5 %collective-permute-start.2 = (bf16[2,8,2048]{2,1,0:T(8,128)(2,1)S(1)}, bf16[2,8,2048]{2,1,0:T(8,128)(2,1)S(1)}, u32[]{:S(2)}, u32[]{:S(2)}) collective-permute-start(bf16[2,8,2048]{2,1,0:T(8,128)(2,1)S(1)} %broadcast_select_fusion.own_ref), channel_id=1, source_target_pairs={{0,16},{16,0},{1,17},{17,1},{2,18},{18,2},{3,19},{19,3},{4,20},{20... | collective-permute-start | bytes 196616 | tf_op jit(solution)/shard_map/ppermute | solution.py:218
  90.6 6.2 %collective-permute-done.2.far_ref = bf16[2,8,2048]{2,1,0:T(8,128)(2,1)S(1)} collective-permute-done((bf16[2,8,2048]{2,1,0:T(8,128)(2,1)S(1)}, bf16[2,8,2048]{2,1,0:T(8,128)(2,1)S(1)}, u32[]{:S(2)}, u32[]{:S(2)}) %collective-permute-start.2) | collective-permute-done | bytes 65568 | tf_op jit(solution)/shard_map/ppermute | solution.py:218
  97.4 1.8 pack_queries.4
  99.2 6.7 %all-to-all-done.3.kv_ref = bf16[4,2,512,256]{3,2,1,0:T(8,128)(2,1)S(1)} async-done(((bf16[4,2,512,256]{3,2,1,0:T(8,128)(2,1)}), bf16[4,2,512,256]{3,2,1,0:T(8,128)(2,1)S(1)}, u32[]{:S(2)}, u32[]{:S(2)}) %all-to-all-start.3) | async-done | bytes 2097184 | tf_op jit(solution)/shard_map/all_to_all | solution.py:268
  105.8 4.0 %all-to-all-start.2 = ((bf16[16,2,16,640]{3,2,1,0:T(8,128)(2,1)}), bf16[16,2,16,640]{3,2,1,0:T(8,128)(2,1)S(1)}, u32[]{:S(2)}, u32[]{:S(2)}) async-start(bf16[16,2,16,640]{3,2,1,0:T(8,128)(2,1)} %pack_queries.4), calls=%async_computation.2 | async-start | bytes 1310720 | tf_op jit(solution)/shard_map/all_to_all | solution.py:222
  112.4 5.5 %attend.5 = bf16[16,1,16,640]{3,2,1,0:T(8,128)(2,1)} custom-call(s32[2]{0:T(128)S(1)} %pad_add_fusion.2.where_ref, bf16[16,1,16,640]{3,2,1,0:T(8,128)(2,1)S(1)} %all-to-all-done.5.q_ref, bf16[4,2,512,256]{3,2,1,0:T(8,128)(2,1)S(1)} %all-to-all-done.3.kv_ref), custom_call_target="tpu_custom_call" | custom-call | flops 1073741824 | bytes 2752512 | tf_op jit(solution)/shard_map/attend/pallas_call | solution.py:121
  119.5 5.1 %all-to-all-start.6 = ((bf16[16,1,16,640]{3,2,1,0:T(8,128)(2,1)}), bf16[16,1,16,640]{3,2,1,0:T(8,128)(2,1)S(1)}, u32[]{:S(2)}, u32[]{:S(2)}) async-start(bf16[16,1,16,640]{3,2,1,0:T(8,128)(2,1)} %attend.5), calls=%async_computation.6 | async-start | bytes 655360 | tf_op jit(solution)/shard_map/all_to_all | solution.py:222
  124.7 10.0 %attend.4 = bf16[16,2,16,640]{3,2,1,0:T(8,128)(2,1)} custom-call(s32[3]{0:T(128)S(1)} %pad_add_fusion.1.where_ref, bf16[16,2,16,640]{3,2,1,0:T(8,128)(2,1)S(1)} %all-to-all-done.2.q_ref, bf16[4,2,512,256]{3,2,1,0:T(8,128)(2,1)S(1)} %all-to-all-done.3.kv_ref), custom_call_target="tpu_custom_call" | custom-call | flops 2147483648 | bytes 3407872 | tf_op jit(solution)/shard_map/attend/pallas_call | solution.py:121
  134.8 6.7 %all-to-all-start.4 = ((bf16[16,2,16,640]{3,2,1,0:T(8,128)(2,1)}), bf16[16,2,16,640]{3,2,1,0:T(8,128)(2,1)S(1)}, u32[]{:S(2)}, u32[]{:S(2)}) async-start(bf16[16,2,16,640]{3,2,1,0:T(8,128)(2,1)} %attend.4), calls=%async_computation.4 | async-start | bytes 1310720 | tf_op jit(solution)/shard_map/all_to_all | solution.py:222
  141.4 2.3 %fold_plane.5 = (f32[1,8,2048]{2,1,0:T(8,128)}, f32[1,8,128]{2,1,0:T(8,128)}, bf16[1,8,2176]{2,1,0:T(8,128)(2,1)}) custom-call(bf16[16,1,16,640]{3,2,1,0:T(8,128)(2,1)} %copy-done.1), custom_call_target="tpu_custom_call" | custom-call | bytes 655360 | tf_op jit(solution)/shard_map/fold_plane/pallas_call | solution.py:183
  143.7 7.5 %collective-permute-start.5 = (bf16[1,8,2176]{2,1,0:T(8,128)(2,1)}, bf16[1,8,2176]{2,1,0:T(8,128)(2,1)S(1)}, u32[]{:S(2)}, u32[]{:S(2)}) collective-permute-start(bf16[1,8,2176]{2,1,0:T(8,128)(2,1)} %get-tuple-element.47), channel_id=1, source_target_pairs={{0,16},{16,0},{1,17},{17,1},{2,18},{18,2},{3,19},{19,3},{4,20},{20... | collective-permute-start | bytes 104456 | tf_op jit(solution)/shard_map/ppermute | solution.py:218
  155.0 2.3 %collective-permute-done.5.far_ref = bf16[1,8,2176]{2,1,0:T(8,128)(2,1)S(1)} collective-permute-done((bf16[1,8,2176]{2,1,0:T(8,128)(2,1)}, bf16[1,8,2176]{2,1,0:T(8,128)(2,1)S(1)}, u32[]{:S(2)}, u32[]{:S(2)}) %collective-permute-start.5) | collective-permute-done | bytes 34848 | tf_op jit(solution)/shard_map/ppermute | solution.py:218
  159.6 33.8 %all_gather.10 = bf16[16,8,2048]{2,1,0:T(8,128)(2,1)S(1)} all-gather(bf16[1,8,2048]{2,1,0:T(8,128)(2,1)} %finish.5), channel_id=1, replica_groups=mesh['zl'=8,'co'=2,'zh'=2,'y'=4,'x'=4] {'zl','co'}, dimensions={0}, use_global_device_ids=true | all-gather | bytes 557056 | tf_op jit(solution)/shard_map/all_gather | solution.py:286
  194.3 3.2 %fold_plane.4 = (f32[2,8,2048]{2,1,0:T(8,128)}, f32[2,8,128]{2,1,0:T(8,128)}, bf16[2,8,2176]{2,1,0:T(8,128)(2,1)}) custom-call(bf16[16,2,16,640]{3,2,1,0:T(8,128)(2,1)} %copy-done), custom_call_target="tpu_custom_call" | custom-call | bytes 1310720 | tf_op jit(solution)/shard_map/fold_plane/pallas_call | solution.py:183
  197.5 7.4 %collective-permute-start.3 = (bf16[2,8,2176]{2,1,0:T(8,128)(2,1)}, bf16[2,8,2176]{2,1,0:T(8,128)(2,1)S(1)}, u32[]{:S(2)}, u32[]{:S(2)}) collective-permute-start(bf16[2,8,2176]{2,1,0:T(8,128)(2,1)} %get-tuple-element.43), channel_id=1, source_target_pairs={{0,16},{16,0},{1,17},{17,1},{2,18},{18,2},{3,19},{19,3},{4,20},{20... | collective-permute-start | bytes 208904 | tf_op jit(solution)/shard_map/ppermute | solution.py:218
  205.0 7.1 %collective-permute-done.3.far_ref = bf16[2,8,2176]{2,1,0:T(8,128)(2,1)S(1)} collective-permute-done((bf16[2,8,2176]{2,1,0:T(8,128)(2,1)}, bf16[2,8,2176]{2,1,0:T(8,128)(2,1)S(1)}, u32[]{:S(2)}, u32[]{:S(2)}) %collective-permute-start.3) | collective-permute-done | bytes 69664 | tf_op jit(solution)/shard_map/ppermute | solution.py:218
  212.6 1.9 finish.4
  (56 shorter events, 15.9 us)
Async XLA Ops:
  47.6 29.0 %copy-start.2 = (bf16[16,8,3072]{2,1,0:T(8,128)(2,1)}, bf16[16,8,3072]{2,1,0:T(8,128)(2,1)S(1)}, u32[]{:S(2)}) copy-start(bf16[16,8,3072]{2,1,0:T(8,128)(2,1)S(1)} %all_gather.9) | copy-start | bytes 2359300
  48.2 13.4 %copy-start.5 = (bf16[1,8,2048]{2,1,0:T(8,128)(2,1)}, bf16[1,8,2048]{2,1,0:T(8,128)(2,1)S(1)}, u32[]{:S(2)}) copy-start(bf16[1,8,2048]{2,1,0:T(8,128)(2,1)S(1)} %constant_dynamic-slice_fusion.2.own_ref) | copy-start | bytes 98308
  48.3 13.4 %collective-permute-start.4 = (bf16[1,8,2048]{2,1,0:T(8,128)(2,1)S(1)}, bf16[1,8,2048]{2,1,0:T(8,128)(2,1)S(1)}, u32[]{:S(2)}, u32[]{:S(2)}) collective-permute-start(bf16[1,8,2048]{2,1,0:T(8,128)(2,1)S(1)} %constant_dynamic-slice_fusion.2.own_ref), channel_id=1, source_target_pairs={{0,16},{16,0},{1,17},{17,1},{2,18},{18,2},{3,19},{19,3},{4,20},{20... | collective-permute-start | bytes 98312 | tf_op jit(solution)/shard_map/ppermute | solution.py:218
  61.6 0.6 copy-start.12
  63.8 14.8 %all-to-all-start.5 = ((bf16[16,1,16,640]{3,2,1,0:T(8,128)(2,1)}), bf16[16,1,16,640]{3,2,1,0:T(8,128)(2,1)S(1)}, u32[]{:S(2)}, u32[]{:S(2)}) async-start(bf16[16,1,16,640]{3,2,1,0:T(8,128)(2,1)} %pack_queries.5), calls=%async_computation.5 | async-start | bytes 655360 | tf_op jit(solution)/shard_map/all_to_all | solution.py:222
  76.6 5.6 %copy-start.18 = (s32[2,8]{1,0:T(2,128)S(1)}, s32[2,8]{1,0:T(2,128)}, u32[]{:S(2)}) copy-start(s32[2,8]{1,0:T(2,128)} %param.15) | copy-start | bytes 196
  76.6 5.7 %copy-start.9 = (bf16[2,8,2048]{2,1,0:T(8,128)(2,1)S(1)}, bf16[2,8,2048]{2,1,0:T(8,128)(2,1)}, u32[]{:S(2)}) copy-start(bf16[2,8,2048]{2,1,0:T(8,128)(2,1)} %param.13) | copy-start | bytes 196612
  76.6 5.7 %copy-start.15 = (bf16[2048]{0:T(1024)(128)(2,1)S(1)}, bf16[2048]{0:T(1024)(128)(2,1)}, u32[]{:S(2)}) copy-start(bf16[2048]{0:T(1024)(128)(2,1)} %param.20) | copy-start | bytes 12292
  76.6 13.3 %copy-start.14 = (bf16[2,8,1024]{2,1,0:T(8,128)(2,1)S(1)}, bf16[2,8,1024]{2,1,0:T(8,128)(2,1)}, u32[]{:S(2)}) copy-start(bf16[2,8,1024]{2,1,0:T(8,128)(2,1)} %param.14) | copy-start | bytes 98308
  76.6 13.3 %copy-start.16 = (bf16[1024]{0:T(1024)(128)(2,1)S(1)}, bf16[1024]{0:T(1024)(128)(2,1)}, u32[]{:S(2)}) copy-start(bf16[1024]{0:T(1024)(128)(2,1)} %param.21) | copy-start | bytes 6148
  78.6 27.2 %all-to-all-start.3 = ((bf16[4,2,512,256]{3,2,1,0:T(8,128)(2,1)}), bf16[4,2,512,256]{3,2,1,0:T(8,128)(2,1)S(1)}, u32[]{:S(2)}, u32[]{:S(2)}) async-start(bf16[4,2,512,256]{3,2,1,0:T(8,128)(2,1)} %cut_by_head.1), calls=%async_computation.3 | async-start | bytes 4194304 | tf_op jit(solution)/shard_map/all_to_all | solution.py:268
  82.2 27.6 %copy-start.17 = (s32[16]{0:T(128)S(1)}, s32[16]{0:T(128)}, u32[]{:S(2)}) copy-start(s32[16]{0:T(128)} %param.19) | copy-start | bytes 196
  82.3 14.4 %copy-start.3 = (bf16[2,8,2048]{2,1,0:T(8,128)(2,1)}, bf16[2,8,2048]{2,1,0:T(8,128)(2,1)S(1)}, u32[]{:S(2)}) copy-start(bf16[2,8,2048]{2,1,0:T(8,128)(2,1)S(1)} %broadcast_select_fusion.own_ref) | copy-start | bytes 196612
  82.3 14.4 %collective-permute-start.2 = (bf16[2,8,2048]{2,1,0:T(8,128)(2,1)S(1)}, bf16[2,8,2048]{2,1,0:T(8,128)(2,1)S(1)}, u32[]{:S(2)}, u32[]{:S(2)}) collective-permute-start(bf16[2,8,2048]{2,1,0:T(8,128)(2,1)S(1)} %broadcast_select_fusion.own_ref), channel_id=1, source_target_pairs={{0,16},{16,0},{1,17},{17,1},{2,18},{18,2},{3,19},{19,3},{4,20},{20... | collective-permute-start | bytes 196616 | tf_op jit(solution)/shard_map/ppermute | solution.py:218
  96.8 0.6 copy-start.8
  105.8 13.7 %all-to-all-start.2 = ((bf16[16,2,16,640]{3,2,1,0:T(8,128)(2,1)}), bf16[16,2,16,640]{3,2,1,0:T(8,128)(2,1)S(1)}, u32[]{:S(2)}, u32[]{:S(2)}) async-start(bf16[16,2,16,640]{3,2,1,0:T(8,128)(2,1)} %pack_queries.4), calls=%async_computation.2 | async-start | bytes 1310720 | tf_op jit(solution)/shard_map/all_to_all | solution.py:222
  119.5 15.3 %all-to-all-start.6 = ((bf16[16,1,16,640]{3,2,1,0:T(8,128)(2,1)}), bf16[16,1,16,640]{3,2,1,0:T(8,128)(2,1)S(1)}, u32[]{:S(2)}, u32[]{:S(2)}) async-start(bf16[16,1,16,640]{3,2,1,0:T(8,128)(2,1)} %attend.5), calls=%async_computation.6 | async-start | bytes 655360 | tf_op jit(solution)/shard_map/all_to_all | solution.py:222
  134.8 6.7 %copy-start.1 = (bf16[16,1,16,640]{3,2,1,0:T(8,128)(2,1)}, bf16[16,1,16,640]{3,2,1,0:T(8,128)(2,1)S(1)}, u32[]{:S(2)}) copy-start(bf16[16,1,16,640]{3,2,1,0:T(8,128)(2,1)S(1)} %all-to-all-done.6.r_ref) | copy-start | bytes 983044
  134.8 58.6 %all-to-all-start.4 = ((bf16[16,2,16,640]{3,2,1,0:T(8,128)(2,1)}), bf16[16,2,16,640]{3,2,1,0:T(8,128)(2,1)S(1)}, u32[]{:S(2)}, u32[]{:S(2)}) async-start(bf16[16,2,16,640]{3,2,1,0:T(8,128)(2,1)} %attend.4), calls=%async_computation.4 | async-start | bytes 1310720 | tf_op jit(solution)/shard_map/all_to_all | solution.py:222
  143.7 13.6 %collective-permute-start.5 = (bf16[1,8,2176]{2,1,0:T(8,128)(2,1)}, bf16[1,8,2176]{2,1,0:T(8,128)(2,1)S(1)}, u32[]{:S(2)}, u32[]{:S(2)}) collective-permute-start(bf16[1,8,2176]{2,1,0:T(8,128)(2,1)} %get-tuple-element.47), channel_id=1, source_target_pairs={{0,16},{16,0},{1,17},{17,1},{2,18},{18,2},{3,19},{19,3},{4,20},{20... | collective-permute-start | bytes 104456 | tf_op jit(solution)/shard_map/ppermute | solution.py:218
  193.4 0.8 copy-start
  197.5 14.5 %collective-permute-start.3 = (bf16[2,8,2176]{2,1,0:T(8,128)(2,1)}, bf16[2,8,2176]{2,1,0:T(8,128)(2,1)S(1)}, u32[]{:S(2)}, u32[]{:S(2)}) collective-permute-start(bf16[2,8,2176]{2,1,0:T(8,128)(2,1)} %get-tuple-element.43), channel_id=1, source_target_pairs={{0,16},{16,0},{1,17},{17,1},{2,18},{18,2},{3,19},{19,3},{4,20},{20... | collective-permute-start | bytes 208904 | tf_op jit(solution)/shard_map/ppermute | solution.py:218
  204.9 9.6 %copy-start.4 = (bf16[1,8,2048]{2,1,0:T(8,128)(2,1)}, bf16[1,8,2048]{2,1,0:T(8,128)(2,1)S(1)}, u32[]{:S(2)}) copy-start(bf16[1,8,2048]{2,1,0:T(8,128)(2,1)S(1)} %get-tuple-element.48) | copy-start | bytes 98308
  212.0 0.6 copy-start.7
  (1 other events, 0.6 us)

commit v2 on v1

v2 whole, which is shorter than its diff:
```python
import functools

import jax
import jax.numpy as jnp
from jax import lax
from jax.experimental import pallas as pl
from jax.experimental.pallas import tpu as pltpu
from jax.sharding import Mesh, PartitionSpec as P

QH = 16
KVH = 4
HD = 128
GRP = QH // KVH
GW = GRP * HD
ROWS = 8
PAY = GW + HD
DP = ("zl", "co")
PLANE = ("y", "x")
CTX = ("zh", "y", "x")
SCALE = HD ** -0.5
F32 = jnp.float32
BF16 = jnp.bfloat16


def cost(flops, nbytes, trans=0):
    return pl.CostEstimate(flops=flops, bytes_accessed=nbytes, transcendentals=trans)


def params(mib):
    return pltpu.CompilerParams(vmem_limit_bytes=mib * 2 ** 20)


def shape(dims, dtype=BF16):
    return jax.ShapeDtypeStruct(dims, dtype)


def in_smem():
    return pl.BlockSpec(memory_space=pltpu.SMEM)


def in_vmem():
    return pl.BlockSpec(memory_space=pltpu.VMEM)


def split_three(v):
    hi = v.astype(BF16)
    rest = v - hi.astype(F32)
    mid = rest.astype(BF16)
    low = (rest - mid.astype(F32)).astype(BF16)
    return hi.astype(F32), mid.astype(F32), low.astype(F32)


SLOT, OTHER, MEMBER, HOME, HOME_OTHER = 0, 2, 4, 6, 7


def plan_kernel(seqs, ids_ref, o_ref):
    count = ids_ref.shape[0]
    core = lax.axis_index("co")
    group = lax.axis_index("zl") * lax.axis_size("co") + core
    other = group + 1 - 2 * core
    for where, place in ((group, SLOT), (other, OTHER)):
        seen = jnp.int32(0)
        slot = [jnp.int32(0), jnp.int32(0)]
        member = [jnp.int32(0), jnp.int32(0)]
        for j in range(count):
            one = ids_ref[j]
            home = lax.div(one, jnp.int32(seqs))
            hit = home == where
            for turn in range(2):
                now = hit & (seen == turn)
                slot[turn] = jnp.where(now, j, slot[turn])
                member[turn] = jnp.where(now, one - home * seqs, member[turn])
            seen = seen + hit.astype(jnp.int32)
        for turn in range(2):
            o_ref[place + turn] = slot[turn]
            if place == SLOT:
                o_ref[MEMBER + turn] = member[turn]
    o_ref[HOME] = lax.div(ids_ref[group], jnp.int32(seqs))
    o_ref[HOME_OTHER] = lax.div(ids_ref[other], jnp.int32(seqs))


def make_plan(ids, seqs):
    return pl.pallas_call(
        functools.partial(plan_kernel, seqs),
        in_specs=[in_smem()],
        out_specs=in_smem(),
        out_shape=shape((8,), jnp.int32),
        compiler_params=params(1),
        cost_estimate=cost(0, 128),
        name="plan",
    )(ids)


def head_of(y, x):
    return 2 * (y & 1) + (x & 1)


def own_head():
    return head_of(lax.axis_index("y"), lax.axis_index("x"))


def cut_kernel(s_ref, *outs):
    here = own_head()
    for d, out in enumerate(outs):
        head = jnp.bitwise_xor(here, d)
        for part in range(2):
            start = pl.multiple_of((part * KVH + head) * HD, HD)
            for n in range(out.shape[0]):
                out[n, :, part * HD:(part + 1) * HD] = s_ref[n, :, pl.ds(start, HD)]


def cut_by_head(stored):
    seqs, rows, _ = stored.shape
    return pl.pallas_call(
        cut_kernel,
        out_shape=[shape((seqs, rows, 2 * HD))] * KVH,
        compiler_params=params(12),
        cost_estimate=cost(0, 4 * stored.size),
        name="cut_by_head",
    )(stored)


def send_kernel(*refs):
    given, o_ref, held, sem = refs[:5], refs[5], refs[6:11], refs[11]
    copies = [pltpu.make_async_copy(a, b, sem.at[n]) for n, (a, b) in enumerate(zip(given, held))]
    for copy in copies:
        copy.start()
    for copy in copies:
        copy.wait()
    q_ref, kv_ref, mark_ref, bq_ref, bkv_ref = held
    square = (ROWS, ROWS)
    eye = lax.broadcasted_iota(jnp.int32, square, 0) == lax.broadcasted_iota(jnp.int32, square, 1)
    marks = jnp.broadcast_to(mark_ref[...], square)
    column = jnp.sum(jnp.where(eye, marks, 0).astype(F32), axis=1, keepdims=True)
    hidden = jnp.broadcast_to(column == 1.0, (ROWS, HD))
    for blank, values, first in ((bq_ref, q_ref, 0), (bkv_ref, kv_ref, q_ref.shape[2] // 2)):
        half = values.shape[2] // 2
        for c in range(2):
            value = jnp.concatenate(
                [
                    jnp.where(
                        hidden,
                        jnp.broadcast_to(blank[i:i + 1].astype(F32), (ROWS, HD)),
                        values[0, :, i * HD:(i + 1) * HD].astype(F32),
                    )
                    for i in range(c * half // HD, (c + 1) * half // HD)
                ],
                axis=1,
            ).astype(BF16)
            for chip in range(o_ref.shape[0] // 2):
                o_ref[2 * chip + c, :, first:first + half] = value


def send_slots(q, kv, marks, blank_q, blank_kv):
    groups = lax.axis_size("zl") * lax.axis_size("co")
    out = shape((groups, ROWS, (q.shape[2] + kv.shape[2]) // 2))
    given = (q, kv, marks, blank_q.reshape(-1, HD), blank_kv.reshape(-1, HD))
    return pl.pallas_call(
        send_kernel,
        in_specs=[pl.BlockSpec(memory_space=pltpu.HBM)] * len(given),
        out_specs=in_vmem(),
        out_shape=out,
        scratch_shapes=[pltpu.VMEM(value.shape, value.dtype) for value in given]
        + [pltpu.SemaphoreType.DMA((len(given),))],
        compiler_params=params(4),
        cost_estimate=cost(0, 2 * out.size),
        name="send_slots",
    )(*given)


def pick_kernel(entry, plan_ref, halves_ref, o_ref):
    o_ref[0] = halves_ref[plan_ref[entry]]


def pick(plan, halves, entry):
    return pl.pallas_call(
        functools.partial(pick_kernel, entry),
        in_specs=[in_smem(), in_vmem()],
        out_specs=in_vmem(),
        out_shape=shape((1,) + halves.shape[1:]),
        compiler_params=params(2),
        cost_estimate=cost(0, 4 * halves.size),
        name="pick",
    )(plan, halves)


def join_kernel(entry, given, plan_ref, halves_ref, got_ref, *refs):
    aheads, outs = refs[:given], refs[given:]
    kept = halves_ref[plan_ref[entry]]
    got = got_ref[0]
    low = lax.axis_index("co") == 0
    first = 0
    for n, out in enumerate(outs):
        last = out.shape[0] - 1
        if given:
            out[:last] = aheads[n][...]
        half = out.shape[2] // 2
        cols = slice(first, first + half)

        @pl.when(low)
        def _(out=out, last=last, half=half, cols=cols):
            out[last, :, :half] = kept[:, cols]
            out[last, :, half:] = got[:, cols]

        @pl.when(jnp.logical_not(low))
        def _(out=out, last=last, half=half, cols=cols):
            out[last, :, :half] = got[:, cols]
            out[last, :, half:] = kept[:, cols]

        first += half


def join(plan, halves, got, entry, widths, *aheads):
    units = 1 + (aheads[0].shape[0] if aheads else 0)
    return pl.pallas_call(
        functools.partial(join_kernel, entry, len(aheads)),
        in_specs=[in_smem()] + [in_vmem()] * (2 + len(aheads)),
        out_specs=[in_vmem()] * len(widths),
        out_shape=[shape((units, ROWS, width)) for width in widths],
        compiler_params=params(2),
        cost_estimate=cost(0, 4 * halves.size),
        name="join",
    )(plan, halves, got, *aheads)


def pack_kernel(own_ref, far_ref, kv_ref, o_ref):
    width = lax.axis_size("x")
    for u in range(own_ref.shape[0]):
        for h in range(KVH):
            cols = slice(h * GW, (h + 1) * GW)
            q = jnp.concatenate(
                [own_ref[u, :, cols].astype(F32), far_ref[u, :, cols].astype(F32)], axis=0
            ).astype(BF16)
            k = kv_ref[u, :, h * HD:(h + 1) * HD].astype(F32)
            v = kv_ref[u, :, (KVH + h) * HD:(KVH + h + 1) * HD].astype(F32)
            kv = jnp.concatenate([k, v], axis=0).astype(BF16)
            for place in range(o_ref.shape[0]):
                if head_of(place // width, place % width) == h:
                    o_ref[place, u, :, :GW] = q
                    o_ref[place, u, :, GW:] = kv


def pack(own, far, kv):
    places = lax.axis_size("y") * lax.axis_size("x")
    out = shape((places, own.shape[0], 2 * ROWS, PAY))
    return pl.pallas_call(
        pack_kernel,
        out_shape=out,
        compiler_params=params(6),
        cost_estimate=cost(0, 2 * out.size),
        name="pack_queries",
    )(own, far, kv)


def attend_kernel(plan_ref, q_ref, *refs):
    kv_refs, o_ref = refs[:KVH], refs[KVH]
    places = q_ref.shape[0]
    rows = places * 2 * ROWS
    y, x = lax.axis_index("y"), lax.axis_index("x")
    corner = (y - (y & 1)) * lax.axis_size("x") + x - (x & 1)
    near = [
        q_ref[corner + dy * lax.axis_size("x") + dx, 0, :, GW:].astype(F32)
        for dy in range(2)
        for dx in range(2)
    ]
    kb = jnp.concatenate([rows_of[:ROWS] for rows_of in near], axis=0).astype(BF16)
    vb = jnp.concatenate([rows_of[ROWS:] for rows_of in near], axis=0).astype(BF16)
    lane = lax.broadcasted_iota(jnp.int32, (rows, HD), 1)
    stats = jnp.zeros((rows, HD), F32)
    nt = (((1,), (1,)), ((), ()))
    for j in range(GRP):
        q = q_ref[:, 0, :, j * HD:(j + 1) * HD].reshape(rows, HD)
        parts = [
            lax.dot_general(q, kv_refs[x][0, :, :HD], nt, preferred_element_type=F32)
            for x in range(KVH)
        ]
        parts.append(lax.dot_general(q, kb, nt, preferred_element_type=F32))
        top = jnp.max(parts[0], axis=1, keepdims=True)
        for part in parts[1:]:
            top = jnp.maximum(top, jnp.max(part, axis=1, keepdims=True))
        total = jnp.zeros((rows, 1), F32)
        out = jnp.zeros((rows, HD), F32)
        for x, part in enumerate(parts):
            w = jnp.exp((part - top) * SCALE)
            total = total + jnp.sum(w, axis=1, keepdims=True)
            v = kv_refs[x][0, :, HD:] if x < KVH else vb
            out = out + jnp.dot(w.astype(BF16), v, preferred_element_type=F32)
        o_ref[:, 0, :, j * HD:(j + 1) * HD] = (
            (out * (1.0 / total)).astype(BF16).reshape(places, 2 * ROWS, HD)
        )
        for i, piece in enumerate(split_three(top * SCALE + jnp.log(total))):
            stats = jnp.where(lane == i * GRP + j, piece, stats)
    o_ref[:, 0, :, GW:] = stats.astype(BF16).reshape(places, 2 * ROWS, HD)


def attend(plan, queries, kv, first, units, member):
    places = queries.shape[0]
    dims = (places, 1, 2 * ROWS, PAY)
    keys = pl.BlockSpec((1,) + kv[0].shape[1:], lambda u, w: (member(u, w), 0, 0))
    pairs = units * places * 2 * ROWS * GRP * KVH * kv[0].shape[1]
    return pl.pallas_call(
        attend_kernel,
        grid_spec=pltpu.PrefetchScalarGridSpec(
            num_scalar_prefetch=1,
            grid=(units,),
            in_specs=[pl.BlockSpec(dims, lambda u, w: (0, first + u, 0, 0))] + [keys] * KVH,
            out_specs=pl.BlockSpec(dims, lambda u, w: (0, u, 0, 0)),
        ),
        out_shape=shape((places, units) + dims[2:]),
        compiler_params=params(24),
        cost_estimate=cost(pairs * HD * 4, 4 * queries.size + 8 * kv[0].size, pairs),
        name="attend",
    )(plan, queries, *kv)


def merge(members):
    top = members[0][1]
    for _, lse in members[1:]:
        top = jnp.maximum(top, lse)
    total = 0.0
    out = 0.0
    for part, lse in members:
        w = jnp.exp(lse - top)
        total = total + w
        out = out + part * w
    return out * (1.0 / total), top + jnp.log(total)


def fold_kernel(r_ref, own_ref, lse_ref, far_ref):
    units = r_ref.shape[1]
    rows = 2 * ROWS
    width = lax.axis_size("x")
    places = [
        [p for p in range(r_ref.shape[0]) if head_of(p // width, p % width) == h]
        for h in range(KVH)
    ]
    lane = lax.broadcasted_iota(jnp.int32, (rows, HD), 1)
    for u in range(units):
        near = jnp.zeros((rows, HD), F32)
        sent = jnp.zeros((rows, HD), F32)
        for x in range(KVH):
            tails = []
            for place in places[x]:
                tail = r_ref[place, u, :, GW:].astype(F32)
                tails.append(
                    tail[:, :GRP] + tail[:, GRP:2 * GRP] + tail[:, 2 * GRP:3 * GRP]
                )
            for j in range(GRP):
                h = x * GRP + j
                out, lse = merge([
                    (r_ref[place, u, :, j * HD:(j + 1) * HD].astype(F32), t[:, j:j + 1])
                    for place, t in zip(places[x], tails)
                ])
                own_ref[u, :, h * HD:(h + 1) * HD] = out[:ROWS]
                far_ref[u, :, h * HD:(h + 1) * HD] = out[ROWS:].astype(BF16)
                near = jnp.where(lane == h, lse, near)
                for i, piece in enumerate(split_three(lse)):
                    sent = jnp.where(lane == i * QH + h, piece, sent)
        lse_ref[u] = near[:ROWS]
        far_ref[u, :, QH * HD:] = sent[ROWS:].astype(BF16)


def fold(received):
    units = received.shape[1]
    return pl.pallas_call(
        fold_kernel,
        out_shape=(
            jax.ShapeDtypeStruct((units, ROWS, QH * HD), F32),
            jax.ShapeDtypeStruct((units, ROWS, HD), F32),
            jax.ShapeDtypeStruct((units, ROWS, QH * HD + HD), BF16),
        ),
        compiler_params=params(6),
        cost_estimate=cost(0, 4 * received.size),
        name="fold_plane",
    )(received)


def finish_kernel(sending, own_ref, lse_ref, far_ref, o_ref):
    half = QH // 2
    for u in range(own_ref.shape[0]):
        tail = far_ref[u, :, QH * HD:].astype(F32)
        far_lse = tail[:, :QH] + tail[:, QH:2 * QH] + tail[:, 2 * QH:3 * QH]
        for h in range(QH):
            cols = slice(h * HD, (h + 1) * HD)
            out, _ = merge([
                (own_ref[u, :, cols], lse_ref[u, :, h:h + 1]),
                (far_ref[u, :, cols].astype(F32), far_lse[:, h:h + 1]),
            ])
            out = out.astype(BF16)
            if sending:
                part = h % half
                for chip in range(o_ref.shape[0] // 2):
                    o_ref[2 * chip + h // half, :, part * HD:(part + 1) * HD] = out
            else:
                o_ref[u, :, cols] = out


def finish(own, lse, far, sending=False):
    out = shape(own.shape)
    if sending:
        out = shape((lax.axis_size("zl") * lax.axis_size("co"), ROWS, QH * HD // 2))
    return pl.pallas_call(
        functools.partial(finish_kernel, sending),
        out_shape=out,
        compiler_params=params(4),
        cost_estimate=cost(0, 8 * own.size),
        name="finish",
    )(own, lse, far)


def swap(value, axis):
    return lax.ppermute(value, axis, [(0, 1), (1, 0)])


def exchange(value, axes):
    return lax.all_to_all(value, axes, split_axis=0, concat_axis=0, tiled=True)


def across(value, d):
    width = lax.axis_size("x")
    steps = (d & 1) + width * (d >> 1)
    return lax.ppermute(value, PLANE, [(i, i ^ steps) for i in range(width * lax.axis_size("y"))])


def after(value, *earlier):
    return lax.optimization_barrier((value,) + earlier)[0]


def masked_rows(values, masked, filler):
    return jnp.where(masked[..., None] == 1, filler, values)


def body(
    stored_memory,
    opening_probe_vectors,
    opening_memory_pairs,
    opening_hidden_marks,
    second_probe_vectors,
    second_memory_pairs,
    second_hidden_marks,
    continuing_sequence_ids,
    blank_symbol_probe,
    blank_symbol_pairs,
):
    seqs = stored_memory.shape[0]
    wide, pair = QH * HD, 2 * KVH * HD
    plan = make_plan(continuing_sequence_ids, seqs)
    slot_halves = exchange(
        send_slots(
            second_probe_vectors,
            second_memory_pairs,
            second_hidden_marks,
            blank_symbol_probe,
            blank_symbol_pairs,
        ),
        DP,
    )
    pieces = cut_by_head(stored_memory)
    kv = [pieces[0]] + [across(piece, d) for d, piece in enumerate(pieces) if d]

    query_first = masked_rows(opening_probe_vectors, opening_hidden_marks, blank_symbol_probe)
    block_first = masked_rows(opening_memory_pairs, opening_hidden_marks, blank_symbol_pairs)

    homes = continuing_sequence_ids // seqs
    slots = jnp.arange(homes.shape[0], dtype=jnp.int32)
    earlier = (homes[None, :] == homes[:, None]) & (slots[None, :] < slots[:, None])
    waits = jnp.any(earlier, axis=1)

    def second_queries(turn, halves, *aheads):
        got = swap(pick(plan, halves, OTHER + turn), "co")
        return join(plan, halves, got, SLOT + turn, (wide, pair), *aheads)

    def second_member(turn):
        return lambda unit, plan_ref: plan_ref[MEMBER + turn]

    def hand_back(home_halves):
        back = exchange(home_halves, DP)
        got = swap(pick(plan, back, HOME_OTHER), "co")
        return join(plan, back, got, HOME, (wide,))[0]

    def last_pass(early):
        queries, pairs = second_queries(1, slot_halves)
        second_in = exchange(pack(queries, swap(queries, "zh"), pairs), PLANE)
        second_part = attend(plan, second_in, kv, 0, 1, second_member(1))
        own, lse, far = fold(exchange(second_part, PLANE))
        late = hand_back(finish(own, lse, swap(far, "zh"), True))
        group = lax.axis_index("zl") * lax.axis_size("co") + lax.axis_index("co")
        return jnp.where(waits[group], late, early)

    queries, pairs = second_queries(
        0, after(slot_halves, kv[1], kv[2]), query_first, block_first
    )
    far = swap(queries, "zh")
    everything = exchange(pack(queries, after(far, kv[3]), pairs), PLANE)
    second_part = attend(plan, everything, kv, seqs, 1, second_member(0))
    first_part = attend(plan, everything, kv, 0, seqs, lambda unit, plan_ref: unit)
    second_back = exchange(second_part, PLANE)
    first_back = exchange(after(first_part, second_back), PLANE)
    own, lse, far = fold(second_back)
    home_out = finish(own, lse, swap(far, "zh"), True)
    own_first, lse_first, far_first = fold(first_back)
    result = hand_back(after(home_out, first_back))
    first_out = finish(own_first, lse_first, swap(far_first, "zh"))
    result = lax.cond(jnp.any(waits), last_pass, lambda early: early, result)
    return first_out, result


def solution(mesh):
    fine = Mesh(mesh.devices.reshape(8, 2, 2, 4, 4), ("zl", "co", "zh", "y", "x"))
    rows = P(DP, CTX, None)
    marks = P(DP, CTX)
    return jax.shard_map(
        body,
        mesh=fine,
        in_specs=(rows, rows, rows, marks, rows, rows, marks, P(), P(), P()),
        out_specs=(rows, rows),
        check_vma=False,
    )
```

time: 216 us -> 181 us (0.84)
  blocking collectives: 75 us -> 21.1 us
  starting transfers between devices: 56.3 us -> 81.4 us
  waiting for transfers between devices: 30.9 us -> 44 us
  Pallas kernels: 33.9 us -> 25.7 us
  between operations: 7.29 us -> 1.58 us
  other arithmetic: 5.94 us -> 0.88 us
    all_gather x2 -> x0, blocking collectives: 75 us -> none  [the longest x1 41.3 us: body(): slot_rows = lax.all_gather(second, DP, axis=0, tiled=True)]
    all_to_all x0 -> x1, blocking collectives: none -> 21.1 us  [exchange(): return lax.all_to_all(value, axes, split_axis=0, concat_axis=0, tiled=True)]
    all_to_all x5 -> x4, starting transfers between devices: 26.2 us -> 44.1 us  [exchange(): return lax.all_to_all(value, axes, split_axis=0, concat_axis=0, tiled=True)]
    ppermute x4 -> x8, waiting for transfers between devices: 20.7 us -> 32.5 us  [the longest x3 19.6 us: across(): lax.ppermute(value, PLANE, [(i, i ^ steps) for i in range(width * lax.axi...]
    ppermute x4 -> x8, starting transfers between devices: 30.1 us -> 37.3 us  [the longest x5 28.9 us: swap(): return lax.ppermute(value, axis, [(0, 1), (1, 0)])]
    pallas_call x5 -> x10, Pallas kernels: 12.8 us -> 6.95 us  [the longest x2 1.87 us: finish(): pl.pallas_call(functools.partial(finish_kernel, sending), out_shape=out,...]
    pallas_call x2, Pallas kernels: 5.56 us -> 2.17 us  [fold(): pl.pallas_call(fold_kernel, out_shape=(jax.ShapeDtypeStruct((units, ROWS,...]
    unnamed x32 -> x28, local copies, waits for them, and re-layouts: 3.38 us -> 5.73 us
  transfers between devices with their start and end apart: 9 -> 12, of which waited for: 7 -> 6; matrix products, arithmetic and copies ran while one was open for 2% -> 0% of each run, Pallas kernels for 13% -> 10%
where the time goes in v2:
time: 181 us; the launch traced here: 180 us
  starting transfers between devices  81.4 us (45%)
  waiting for transfers between devices  44 us (24%)
  Pallas kernels  25.7 us (14%)
  blocking collectives  21.1 us (12%)
  local copies, waits for them, and re-layouts  5.73 us (3%)
    all_to_all x4, starting transfers between devices, exchange(): return lax.all_to_all(value, axes, split_axis=0, concat_axis=0, tiled=True)  44.1 us
    ppermute x5, starting transfers between devices, swap(): return lax.ppermute(value, axis, [(0, 1), (1, 0)])  28.9 us
    all_to_all x1, blocking collectives, exchange(): return lax.all_to_all(value, axes, split_axis=0, concat_axis=0, tiled=True)  21.1 us
    ppermute x3, waiting for transfers between devices, across(): lax.ppermute(value, PLANE, [(i, i ^ steps) for i in range(width * lax.axi...  19.6 us
    pallas_call x2, Pallas kernels, attend(): pl.pallas_call(attend_kernel, grid_spec=pltpu.PrefetchScalarGridSpec(num_...  16.6 us
    ppermute x5, waiting for transfers between devices, swap(): return lax.ppermute(value, axis, [(0, 1), (1, 0)])  12.9 us
    all_to_all x4, waiting for transfers between devices, exchange(): return lax.all_to_all(value, axes, split_axis=0, concat_axis=0, tiled=True)  11.5 us
    ppermute x3, starting transfers between devices, across(): lax.ppermute(value, PLANE, [(i, i ^ steps) for i in range(width * lax.axi...  8.4 us
  transfers between devices with their start and end apart: 12, of which 6 were waited for; matrix products, arithmetic and copies ran while one was open for 0% of the time, Pallas kernels for 10%

profile of v2, /device:TPU:1, one launch (start us, length us, event | category | flops | bytes accessed | tf_op | source)
XLA Modules:
  0.0 180.3 jit_solution(9585968046463940097)
XLA Ops:
  4.2 1.0 send_slots.1
  5.2 14.1 %all-to-all-start.3 = ((bf16[16,8,1536]{2,1,0:T(8,128)(2,1)}), bf16[16,8,1536]{2,1,0:T(8,128)(2,1)S(1)}, u32[]{:S(2)}, u32[]{:S(2)}) async-start(bf16[16,8,1536]{2,1,0:T(8,128)(2,1)} %send_slots.1), calls=%async_computation.3 | async-start | bytes 786432 | tf_op jit(solution)/shard_map/all_to_all | solution.py:416
  19.2 1.6 copy-done
  21.4 3.1 %collective-permute-start.4 = (bf16[2,512,256]{2,1,0:T(8,128)(2,1)S(1)}, bf16[2,512,256]{2,1,0:T(8,128)(2,1)S(1)}, u32[]{:S(2)}, u32[]{:S(2)}) collective-permute-start(bf16[2,512,256]{2,1,0:T(8,128)(2,1)S(1)} %get-tuple-element.53), channel_id=1, source_target_pairs={{0,1},{1,0},{2,3},{3,2},{4,5},{5,4},{6,7},{7,6},{8,9},{9,8},{10,11... | collective-permute-start | bytes 1572872 | tf_op jit(solution)/shard_map/ppermute | solution.py:422
  24.5 3.2 %collective-permute-start.5 = (bf16[2,512,256]{2,1,0:T(8,128)(2,1)S(1)}, bf16[2,512,256]{2,1,0:T(8,128)(2,1)S(1)}, u32[]{:S(2)}, u32[]{:S(2)}) collective-permute-start(bf16[2,512,256]{2,1,0:T(8,128)(2,1)S(1)} %get-tuple-element.54), channel_id=1, source_target_pairs={{0,4},{1,5},{2,6},{3,7},{4,0},{5,1},{6,2},{7,3},{8,12},{9,13},{10,... | collective-permute-start | bytes 1572872 | tf_op jit(solution)/shard_map/ppermute | solution.py:422
  27.7 2.0 %collective-permute-start.8 = (bf16[2,512,256]{2,1,0:T(8,128)(2,1)S(1)}, bf16[2,512,256]{2,1,0:T(8,128)(2,1)S(1)}, u32[]{:S(2)}, u32[]{:S(2)}) collective-permute-start(bf16[2,512,256]{2,1,0:T(8,128)(2,1)S(1)} %get-tuple-element.57), channel_id=1, source_target_pairs={{0,5},{1,4},{2,7},{3,6},{4,1},{5,0},{6,3},{7,2},{8,13},{9,12},{10,... | collective-permute-start | bytes 1572872 | tf_op jit(solution)/shard_map/ppermute | solution.py:422
  29.9 1.3 plan.1.plan_ref
  31.2 5.6 %collective-permute-done.4.refs_1_ = bf16[2,512,256]{2,1,0:T(8,128)(2,1)S(1)} collective-permute-done((bf16[2,512,256]{2,1,0:T(8,128)(2,1)S(1)}, bf16[2,512,256]{2,1,0:T(8,128)(2,1)S(1)}, u32[]{:S(2)}, u32[]{:S(2)}) %collective-permute-start.4) | collective-permute-done | bytes 524320 | tf_op jit(solution)/shard_map/ppermute | solution.py:422
  36.7 14.0 %collective-permute-done.5.refs_2_ = bf16[2,512,256]{2,1,0:T(8,128)(2,1)S(1)} collective-permute-done((bf16[2,512,256]{2,1,0:T(8,128)(2,1)S(1)}, bf16[2,512,256]{2,1,0:T(8,128)(2,1)S(1)}, u32[]{:S(2)}, u32[]{:S(2)}) %collective-permute-start.5) | collective-permute-done | bytes 524320 | tf_op jit(solution)/shard_map/ppermute | solution.py:422
  51.3 3.1 %collective-permute-start.6 = (bf16[1,8,1536]{2,1,0:T(8,128)(2,1)S(1)}, bf16[1,8,1536]{2,1,0:T(8,128)(2,1)S(1)}, u32[]{:S(2)}, u32[]{:S(2)}) collective-permute-start(bf16[1,8,1536]{2,1,0:T(8,128)(2,1)S(1)} %pick.6), channel_id=1, source_target_pairs={{0,32},{32,0},{1,33},{33,1},{2,34},{34,2},{3,35},{35,3},{4,36},{36... | collective-permute-start | bytes 73736 | tf_op jit(solution)/shard_map/ppermute | solution.py:412
  55.9 7.9 %collective-permute-start.7 = (bf16[3,8,2048]{2,1,0:T(8,128)(2,1)S(1)}, bf16[3,8,2048]{2,1,0:T(8,128)(2,1)S(1)}, u32[]{:S(2)}, u32[]{:S(2)}) collective-permute-start(bf16[3,8,2048]{2,1,0:T(8,128)(2,1)S(1)} %get-tuple-element.56.own_ref), channel_id=1, source_target_pairs={{0,16},{16,0},{1,17},{17,1},{2,18},{18,2},{3,19},{19,3},{4,20},{20... | collective-permute-start | bytes 294920 | tf_op jit(solution)/shard_map/ppermute | solution.py:412
  63.8 6.7 %collective-permute-done.7.far_ref = bf16[3,8,2048]{2,1,0:T(8,128)(2,1)S(1)} collective-permute-done((bf16[3,8,2048]{2,1,0:T(8,128)(2,1)S(1)}, bf16[3,8,2048]{2,1,0:T(8,128)(2,1)S(1)}, u32[]{:S(2)}, u32[]{:S(2)}) %collective-permute-start.7) | collective-permute-done | bytes 98336 | tf_op jit(solution)/shard_map/ppermute | solution.py:412
  70.6 21.1 %all_to_all.40.q_ref = bf16[16,3,16,640]{3,2,1,0:T(8,128)(2,1)S(1)} all-to-all(bf16[16,3,16,640]{3,2,1,0:T(8,128)(2,1)S(1)} %pack_queries.3), channel_id=1, replica_groups=mesh['zl'=8,'co'=2,'zh'=2,'y'=4,'x'=4] {'y','x'}, dimensions={0} | all-to-all | bytes 1966080 | tf_op jit(solution)/shard_map/all_to_all | solution.py:416
  91.7 5.6 %attend.5 = bf16[16,1,16,640]{3,2,1,0:T(8,128)(2,1)} custom-call(s32[8]{0:T(128)S(1)} %plan.1.plan_ref, bf16[16,3,16,640]{3,2,1,0:T(8,128)(2,1)S(1)} %all_to_all.40.q_ref, bf16[2,512,256]{2,1,0:T(8,128)(2,1)S(1)} %get-tuple-element.60.refs_0_, bf16[2,512,256]{2,1,0:T(8,128)(2,1)S(1)} %collective-permute-done.4.refs_1_, ...), custom_call_target="tpu_custom_call" | custom-call | flops 1073741824 | bytes 4063232 | tf_op jit(solution)/shard_map/attend/pallas_call | solution.py:301
  97.3 3.5 %all-to-all-start.5 = ((bf16[16,1,16,640]{3,2,1,0:T(8,128)(2,1)}), bf16[16,1,16,640]{3,2,1,0:T(8,128)(2,1)S(1)}, u32[]{:S(2)}, u32[]{:S(2)}) async-start(bf16[16,1,16,640]{3,2,1,0:T(8,128)(2,1)} %attend.5), calls=%async_computation.5 | async-start | bytes 655360 | tf_op jit(solution)/shard_map/all_to_all | solution.py:416
  100.9 10.9 %attend.4 = bf16[16,2,16,640]{3,2,1,0:T(8,128)(2,1)} custom-call(s32[8]{0:T(128)S(1)} %plan.1.plan_ref, bf16[16,3,16,640]{3,2,1,0:T(8,128)(2,1)S(1)} %all_to_all.40.q_ref, bf16[2,512,256]{2,1,0:T(8,128)(2,1)S(1)} %get-tuple-element.60.refs_0_, bf16[2,512,256]{2,1,0:T(8,128)(2,1)S(1)} %collective-permute-done.4.refs_1_, ...), custom_call_target="tpu_custom_call" | custom-call | flops 2147483648 | bytes 4063232 | tf_op jit(solution)/shard_map/attend/pallas_call | solution.py:301
  111.8 6.6 %all-to-all-start.6 = ((bf16[16,2,16,640]{3,2,1,0:T(8,128)(2,1)}), bf16[16,2,16,640]{3,2,1,0:T(8,128)(2,1)S(1)}, u32[]{:S(2)}, u32[]{:S(2)}) async-start(bf16[16,2,16,640]{3,2,1,0:T(8,128)(2,1)} %attend.4), calls=%async_computation.6 | async-start | bytes 1310720 | tf_op jit(solution)/shard_map/all_to_all | solution.py:416
  119.1 7.9 %collective-permute-start.10 = (bf16[1,8,2176]{2,1,0:T(8,128)(2,1)S(1)}, bf16[1,8,2176]{2,1,0:T(8,128)(2,1)S(1)}, u32[]{:S(2)}, u32[]{:S(2)}) collective-permute-start(bf16[1,8,2176]{2,1,0:T(8,128)(2,1)S(1)} %get-tuple-element.67), channel_id=1, source_target_pairs={{0,16},{16,0},{1,17},{17,1},{2,18},{18,2},{3,19},{19,3},{4,20},{20... | collective-permute-start | bytes 104456 | tf_op jit(solution)/shard_map/ppermute | solution.py:412
  127.1 5.4 %collective-permute-done.10.far_ref = bf16[1,8,2176]{2,1,0:T(8,128)(2,1)S(1)} collective-permute-done((bf16[1,8,2176]{2,1,0:T(8,128)(2,1)S(1)}, bf16[1,8,2176]{2,1,0:T(8,128)(2,1)S(1)}, u32[]{:S(2)}, u32[]{:S(2)}) %collective-permute-start.10) | collective-permute-done | bytes 34848 | tf_op jit(solution)/shard_map/ppermute | solution.py:412
  133.4 19.9 %all-to-all-start.7 = ((bf16[16,8,1024]{2,1,0:T(8,128)(2,1)}), bf16[16,8,1024]{2,1,0:T(8,128)(2,1)S(1)}, u32[]{:S(2)}, u32[]{:S(2)}) async-start(bf16[16,8,1024]{2,1,0:T(8,128)(2,1)} %finish.5), calls=%async_computation.7 | async-start | bytes 524288 | tf_op jit(solution)/shard_map/all_to_all | solution.py:416
  153.4 1.5 fold_plane.4
  154.9 8.0 %collective-permute-start.9 = (bf16[2,8,2176]{2,1,0:T(8,128)(2,1)S(1)}, bf16[2,8,2176]{2,1,0:T(8,128)(2,1)S(1)}, u32[]{:S(2)}, u32[]{:S(2)}) collective-permute-start(bf16[2,8,2176]{2,1,0:T(8,128)(2,1)S(1)} %get-tuple-element.64), channel_id=1, source_target_pairs={{0,16},{16,0},{1,17},{17,1},{2,18},{18,2},{3,19},{19,3},{4,20},{20... | collective-permute-start | bytes 208904 | tf_op jit(solution)/shard_map/ppermute | solution.py:412
  162.8 11.5 %all-to-all-done.7.halves_ref = bf16[16,8,1024]{2,1,0:T(8,128)(2,1)S(1)} async-done(((bf16[16,8,1024]{2,1,0:T(8,128)(2,1)}), bf16[16,8,1024]{2,1,0:T(8,128)(2,1)S(1)}, u32[]{:S(2)}, u32[]{:S(2)}) %all-to-all-start.7) | async-done | bytes 262176 | tf_op jit(solution)/shard_map/all_to_all | solution.py:416
  174.9 1.9 %collective-permute-start.11 = (bf16[1,8,1024]{2,1,0:T(8,128)(2,1)S(1)}, bf16[1,8,1024]{2,1,0:T(8,128)(2,1)S(1)}, u32[]{:S(2)}, u32[]{:S(2)}) collective-permute-start(bf16[1,8,1024]{2,1,0:T(8,128)(2,1)S(1)} %pick.7), channel_id=1, source_target_pairs={{0,32},{32,0},{1,33},{33,1},{2,34},{34,2},{3,35},{35,3},{4,36},{36... | collective-permute-start | bytes 49160 | tf_op jit(solution)/shard_map/ppermute | solution.py:412
  (49 shorter events, 11.2 us)
Async XLA Ops:
  0.6 53.8 %copy-start.6 = (bf16[1024]{0:T(1024)(128)(2,1)S(1)}, bf16[1024]{0:T(1024)(128)(2,1)}, u32[]{:S(2)}) copy-start(bf16[1024]{0:T(1024)(128)(2,1)} %param.21) | copy-start | bytes 6148
  0.6 29.1 %copy-start.13 = (s32[2,8]{1,0:T(2,128)S(1)}, s32[2,8]{1,0:T(2,128)}, u32[]{:S(2)}) copy-start(s32[2,8]{1,0:T(2,128)} %param.15) | copy-start | bytes 196
  0.7 29.2 %copy-start.8 = (s32[16]{0:T(128)S(1)}, s32[16]{0:T(128)}, u32[]{:S(2)}) copy-start(s32[16]{0:T(128)} %ids_ref.1) | copy-start | bytes 196
  0.7 0.8 copy-start.1
  1.4 0.7 copy-start.2
  2.1 0.7 copy-start.4
  2.8 0.7 copy-start.5
  4.2 25.6 %copy-start.3 = (bf16[2048]{0:T(1024)(128)(2,1)S(1)}, bf16[2048]{0:T(1024)(128)(2,1)}, u32[]{:S(2)}) copy-start(bf16[2048]{0:T(1024)(128)(2,1)} %param.20) | copy-start | bytes 12292
  4.2 25.6 %copy-start.10 = (bf16[2,8,2048]{2,1,0:T(8,128)(2,1)S(1)}, bf16[2,8,2048]{2,1,0:T(8,128)(2,1)}, u32[]{:S(2)}) copy-start(bf16[2,8,2048]{2,1,0:T(8,128)(2,1)} %param.13) | copy-start | bytes 196612
  4.2 50.3 %copy-start.11 = (bf16[2,8,1024]{2,1,0:T(8,128)(2,1)S(1)}, bf16[2,8,1024]{2,1,0:T(8,128)(2,1)}, u32[]{:S(2)}) copy-start(bf16[2,8,1024]{2,1,0:T(8,128)(2,1)} %param.14) | copy-start | bytes 98308
  5.2 45.6 %all-to-all-start.3 = ((bf16[16,8,1536]{2,1,0:T(8,128)(2,1)}), bf16[16,8,1536]{2,1,0:T(8,128)(2,1)S(1)}, u32[]{:S(2)}, u32[]{:S(2)}) async-start(bf16[16,8,1536]{2,1,0:T(8,128)(2,1)} %send_slots.1), calls=%async_computation.3 | async-start | bytes 786432 | tf_op jit(solution)/shard_map/all_to_all | solution.py:416
  19.2 1.6 copy-start
  21.4 15.4 %collective-permute-start.4 = (bf16[2,512,256]{2,1,0:T(8,128)(2,1)S(1)}, bf16[2,512,256]{2,1,0:T(8,128)(2,1)S(1)}, u32[]{:S(2)}, u32[]{:S(2)}) collective-permute-start(bf16[2,512,256]{2,1,0:T(8,128)(2,1)S(1)} %get-tuple-element.53), channel_id=1, source_target_pairs={{0,1},{1,0},{2,3},{3,2},{4,5},{5,4},{6,7},{7,6},{8,9},{9,8},{10,11... | collective-permute-start | bytes 1572872 | tf_op jit(solution)/shard_map/ppermute | solution.py:422
  24.5 26.3 %collective-permute-start.5 = (bf16[2,512,256]{2,1,0:T(8,128)(2,1)S(1)}, bf16[2,512,256]{2,1,0:T(8,128)(2,1)S(1)}, u32[]{:S(2)}, u32[]{:S(2)}) collective-permute-start(bf16[2,512,256]{2,1,0:T(8,128)(2,1)S(1)} %get-tuple-element.54), channel_id=1, source_target_pairs={{0,4},{1,5},{2,6},{3,7},{4,0},{5,1},{6,2},{7,3},{8,12},{9,13},{10,... | collective-permute-start | bytes 1572872 | tf_op jit(solution)/shard_map/ppermute | solution.py:422
  27.7 36.1 %collective-permute-start.8 = (bf16[2,512,256]{2,1,0:T(8,128)(2,1)S(1)}, bf16[2,512,256]{2,1,0:T(8,128)(2,1)S(1)}, u32[]{:S(2)}, u32[]{:S(2)}) collective-permute-start(bf16[2,512,256]{2,1,0:T(8,128)(2,1)S(1)} %get-tuple-element.57), channel_id=1, source_target_pairs={{0,5},{1,4},{2,7},{3,6},{4,1},{5,0},{6,3},{7,2},{8,13},{9,12},{10,... | collective-permute-start | bytes 1572872 | tf_op jit(solution)/shard_map/ppermute | solution.py:422
  51.3 3.9 %collective-permute-start.6 = (bf16[1,8,1536]{2,1,0:T(8,128)(2,1)S(1)}, bf16[1,8,1536]{2,1,0:T(8,128)(2,1)S(1)}, u32[]{:S(2)}, u32[]{:S(2)}) collective-permute-start(bf16[1,8,1536]{2,1,0:T(8,128)(2,1)S(1)} %pick.6), channel_id=1, source_target_pairs={{0,32},{32,0},{1,33},{33,1},{2,34},{34,2},{3,35},{35,3},{4,36},{36... | collective-permute-start | bytes 73736 | tf_op jit(solution)/shard_map/ppermute | solution.py:412
  55.9 14.6 %collective-permute-start.7 = (bf16[3,8,2048]{2,1,0:T(8,128)(2,1)S(1)}, bf16[3,8,2048]{2,1,0:T(8,128)(2,1)S(1)}, u32[]{:S(2)}, u32[]{:S(2)}) collective-permute-start(bf16[3,8,2048]{2,1,0:T(8,128)(2,1)S(1)} %get-tuple-element.56.own_ref), channel_id=1, source_target_pairs={{0,16},{16,0},{1,17},{17,1},{2,18},{18,2},{3,19},{19,3},{4,20},{20... | collective-permute-start | bytes 294920 | tf_op jit(solution)/shard_map/ppermute | solution.py:412
  63.8 33.5 %copy-start.12 = (bf16[2,512,256]{2,1,0:T(8,128)(2,1)}, bf16[2,512,256]{2,1,0:T(8,128)(2,1)S(1)}, u32[]{:S(2)}) copy-start(bf16[2,512,256]{2,1,0:T(8,128)(2,1)S(1)} %collective-permute-done.8.refs_3_) | copy-start | bytes 1572868
  97.3 14.5 %all-to-all-start.5 = ((bf16[16,1,16,640]{3,2,1,0:T(8,128)(2,1)}), bf16[16,1,16,640]{3,2,1,0:T(8,128)(2,1)S(1)}, u32[]{:S(2)}, u32[]{:S(2)}) async-start(bf16[16,1,16,640]{3,2,1,0:T(8,128)(2,1)} %attend.5), calls=%async_computation.5 | async-start | bytes 655360 | tf_op jit(solution)/shard_map/all_to_all | solution.py:416
  111.8 21.6 %all-to-all-start.6 = ((bf16[16,2,16,640]{3,2,1,0:T(8,128)(2,1)}), bf16[16,2,16,640]{3,2,1,0:T(8,128)(2,1)S(1)}, u32[]{:S(2)}, u32[]{:S(2)}) async-start(bf16[16,2,16,640]{3,2,1,0:T(8,128)(2,1)} %attend.4), calls=%async_computation.6 | async-start | bytes 1310720 | tf_op jit(solution)/shard_map/all_to_all | solution.py:416
  119.1 13.4 %collective-permute-start.10 = (bf16[1,8,2176]{2,1,0:T(8,128)(2,1)S(1)}, bf16[1,8,2176]{2,1,0:T(8,128)(2,1)S(1)}, u32[]{:S(2)}, u32[]{:S(2)}) collective-permute-start(bf16[1,8,2176]{2,1,0:T(8,128)(2,1)S(1)} %get-tuple-element.67), channel_id=1, source_target_pairs={{0,16},{16,0},{1,17},{17,1},{2,18},{18,2},{3,19},{19,3},{4,20},{20... | collective-permute-start | bytes 104456 | tf_op jit(solution)/shard_map/ppermute | solution.py:412
  133.4 40.9 %all-to-all-start.7 = ((bf16[16,8,1024]{2,1,0:T(8,128)(2,1)}), bf16[16,8,1024]{2,1,0:T(8,128)(2,1)S(1)}, u32[]{:S(2)}, u32[]{:S(2)}) async-start(bf16[16,8,1024]{2,1,0:T(8,128)(2,1)} %finish.5), calls=%async_computation.7 | async-start | bytes 524288 | tf_op jit(solution)/shard_map/all_to_all | solution.py:416
  154.9 23.3 %collective-permute-start.9 = (bf16[2,8,2176]{2,1,0:T(8,128)(2,1)S(1)}, bf16[2,8,2176]{2,1,0:T(8,128)(2,1)S(1)}, u32[]{:S(2)}, u32[]{:S(2)}) collective-permute-start(bf16[2,8,2176]{2,1,0:T(8,128)(2,1)S(1)} %get-tuple-element.64), channel_id=1, source_target_pairs={{0,16},{16,0},{1,17},{17,1},{2,18},{18,2},{3,19},{19,3},{4,20},{20... | collective-permute-start | bytes 208904 | tf_op jit(solution)/shard_map/ppermute | solution.py:412
  174.9 4.2 %collective-permute-start.11 = (bf16[1,8,1024]{2,1,0:T(8,128)(2,1)S(1)}, bf16[1,8,1024]{2,1,0:T(8,128)(2,1)S(1)}, u32[]{:S(2)}, u32[]{:S(2)}) collective-permute-start(bf16[1,8,1024]{2,1,0:T(8,128)(2,1)S(1)} %pick.7), channel_id=1, source_target_pairs={{0,32},{32,0},{1,33},{33,1},{2,34},{34,2},{3,35},{35,3},{4,36},{36... | collective-permute-start | bytes 49160 | tf_op jit(solution)/shard_map/ppermute | solution.py:412
  (2 other events, 1.3 us)

commit v3 on v2

--- a/solution.py
+++ b/solution.py
@@ -18,6 +18,7 @@
 PLANE = ("y", "x")
 CTX = ("zh", "y", "x")
 SCALE = HD ** -0.5
+LOG2E = 1.4426950408889634
 F32 = jnp.float32
 BF16 = jnp.bfloat16
 
@@ -50,7 +51,7 @@
     return hi.astype(F32), mid.astype(F32), low.astype(F32)
 
 
-SLOT, OTHER, MEMBER, HOME, HOME_OTHER = 0, 2, 4, 6, 7
+SLOT, OTHER, MEMBER, HOME, HOME_OTHER, SHARED, WAITS = 0, 2, 4, 6, 7, 8, 9
 
 
 def plan_kernel(seqs, ids_ref, o_ref):
@@ -75,6 +76,15 @@
             o_ref[place + turn] = slot[turn]
             if place == SLOT:
                 o_ref[MEMBER + turn] = member[turn]
+    taken, shared, waits = jnp.int32(0), jnp.int32(0), jnp.int32(0)
+    for j in range(count):
+        bit = lax.shift_left(jnp.int32(1), lax.div(ids_ref[j], jnp.int32(seqs)))
+        second = ((taken & bit) != 0).astype(jnp.int32)
+        shared = shared | second
+        waits = jnp.where(group == j, second, waits)
+        taken = taken | bit
+    o_ref[SHARED] = shared
+    o_ref[WAITS] = waits
     o_ref[HOME] = lax.div(ids_ref[group], jnp.int32(seqs))
     o_ref[HOME_OTHER] = lax.div(ids_ref[other], jnp.int32(seqs))
 
@@ -84,7 +94,7 @@
         functools.partial(plan_kernel, seqs),
         in_specs=[in_smem()],
         out_specs=in_smem(),
-        out_shape=shape((8,), jnp.int32),
+        out_shape=shape((10,), jnp.int32),
         compiler_params=params(1),
         cost_estimate=cost(0, 128),
         name="plan",
@@ -162,32 +172,30 @@
         out_shape=out,
         scratch_shapes=[pltpu.VMEM(value.shape, value.dtype) for value in given]
         + [pltpu.SemaphoreType.DMA((len(given),))],
-        compiler_params=params(4),
         cost_estimate=cost(0, 2 * out.size),
         name="send_slots",
     )(*given)
 
 
-def pick_kernel(entry, plan_ref, halves_ref, o_ref):
-    o_ref[0] = halves_ref[plan_ref[entry]]
-
-
-def pick(plan, halves, entry):
-    return pl.pallas_call(
-        functools.partial(pick_kernel, entry),
+def pick_kernel(entries, plan_ref, halves_ref, *outs):
+    for entry, out in zip(entries, outs):
+        out[0] = halves_ref[plan_ref[entry]]
+
+
+def pick(plan, halves, entries):
+    return pl.pallas_call(
+        functools.partial(pick_kernel, entries),
         in_specs=[in_smem(), in_vmem()],
-        out_specs=in_vmem(),
-        out_shape=shape((1,) + halves.shape[1:]),
+        out_specs=[in_vmem()] * len(entries),
+        out_shape=[shape((1,) + halves.shape[1:])] * len(entries),
         compiler_params=params(2),
         cost_estimate=cost(0, 4 * halves.size),
         name="pick",
     )(plan, halves)
 
 
-def join_kernel(entry, given, plan_ref, halves_ref, got_ref, *refs):
+def join_kernel(given, kept_ref, got_ref, *refs):
     aheads, outs = refs[:given], refs[given:]
-    kept = halves_ref[plan_ref[entry]]
-    got = got_ref[0]
     low = lax.axis_index("co") == 0
     first = 0
     for n, out in enumerate(outs):
@@ -199,28 +207,26 @@
 
         @pl.when(low)
         def _(out=out, last=last, half=half, cols=cols):
-            out[last, :, :half] = kept[:, cols]
-            out[last, :, half:] = got[:, cols]
+            out[last, :, :half] = kept_ref[0, :, cols]
+            out[last, :, half:] = got_ref[0, :, cols]
 
         @pl.when(jnp.logical_not(low))
         def _(out=out, last=last, half=half, cols=cols):
-            out[last, :, :half] = got[:, cols]
-            out[last, :, half:] = kept[:, cols]
+            out[last, :, :half] = got_ref[0, :, cols]
+            out[last, :, half:] = kept_ref[0, :, cols]
 
         first += half
 
 
-def join(plan, halves, got, entry, widths, *aheads):
+def join(kept, got, widths, *aheads):
     units = 1 + (aheads[0].shape[0] if aheads else 0)
     return pl.pallas_call(
-        functools.partial(join_kernel, entry, len(aheads)),
-        in_specs=[in_smem()] + [in_vmem()] * (2 + len(aheads)),
-        out_specs=[in_vmem()] * len(widths),
+        functools.partial(join_kernel, len(aheads)),
         out_shape=[shape((units, ROWS, width)) for width in widths],
         compiler_params=params(2),
-        cost_estimate=cost(0, 4 * halves.size),
+        cost_estimate=cost(0, 8 * kept.size),
         name="join",
-    )(plan, halves, got, *aheads)
+    )(kept, got, *aheads)
 
 
 def pack_kernel(own_ref, far_ref, kv_ref, o_ref):
@@ -252,62 +258,58 @@
     )(own, far, kv)
 
 
-def attend_kernel(plan_ref, q_ref, *refs):
-    kv_refs, o_ref = refs[:KVH], refs[KVH]
-    places = q_ref.shape[0]
+def attend_kernel(first, members, plan_ref, q_ref, *refs):
+    kv_refs, o_ref, k_all, v_all = refs[:KVH], refs[KVH], refs[KVH + 1], refs[KVH + 2]
+    places, units = o_ref.shape[:2]
     rows = places * 2 * ROWS
+    span = kv_refs[0].shape[1]
+    cached = KVH * span
     y, x = lax.axis_index("y"), lax.axis_index("x")
-    corner = (y - (y & 1)) * lax.axis_size("x") + x - (x & 1)
-    near = [
-        q_ref[corner + dy * lax.axis_size("x") + dx, 0, :, GW:].astype(F32)
-        for dy in range(2)
-        for dx in range(2)
-    ]
-    kb = jnp.concatenate([rows_of[:ROWS] for rows_of in near], axis=0).astype(BF16)
-    vb = jnp.concatenate([rows_of[ROWS:] for rows_of in near], axis=0).astype(BF16)
+    width = lax.axis_size("x")
+    corner = (y - (y & 1)) * width + x - (x & 1)
     lane = lax.broadcasted_iota(jnp.int32, (rows, HD), 1)
-    stats = jnp.zeros((rows, HD), F32)
-    nt = (((1,), (1,)), ((), ()))
-    for j in range(GRP):
-        q = q_ref[:, 0, :, j * HD:(j + 1) * HD].reshape(rows, HD)
-        parts = [
-            lax.dot_general(q, kv_refs[x][0, :, :HD], nt, preferred_element_type=F32)
-            for x in range(KVH)
+    v_all[:, HD:] = jnp.ones((cached + KVH * ROWS, HD), BF16)
+    for u in range(units):
+        member = members[u](plan_ref)
+        for n, kv_ref in enumerate(kv_refs):
+            k_all[n * span:(n + 1) * span] = kv_ref[member, :, :HD]
+            v_all[n * span:(n + 1) * span, :HD] = kv_ref[member, :, HD:]
+        near = [
+            q_ref[corner + dy * width + dx, first + u, :, GW:].astype(F32)
+            for dy in range(2)
+            for dx in range(2)
         ]
-        parts.append(lax.dot_general(q, kb, nt, preferred_element_type=F32))
-        top = jnp.max(parts[0], axis=1, keepdims=True)
-        for part in parts[1:]:
-            top = jnp.maximum(top, jnp.max(part, axis=1, keepdims=True))
-        total = jnp.zeros((rows, 1), F32)
-        out = jnp.zeros((rows, HD), F32)
-        for x, part in enumerate(parts):
-            w = jnp.exp((part - top) * SCALE)
-            total = total + jnp.sum(w, axis=1, keepdims=True)
-            v = kv_refs[x][0, :, HD:] if x < KVH else vb
-            out = out + jnp.dot(w.astype(BF16), v, preferred_element_type=F32)
-        o_ref[:, 0, :, j * HD:(j + 1) * HD] = (
-            (out * (1.0 / total)).astype(BF16).reshape(places, 2 * ROWS, HD)
-        )
-        for i, piece in enumerate(split_three(top * SCALE + jnp.log(total))):
-            stats = jnp.where(lane == i * GRP + j, piece, stats)
-    o_ref[:, 0, :, GW:] = stats.astype(BF16).reshape(places, 2 * ROWS, HD)
-
-
-def attend(plan, queries, kv, first, units, member):
-    places = queries.shape[0]
-    dims = (places, 1, 2 * ROWS, PAY)
-    keys = pl.BlockSpec((1,) + kv[0].shape[1:], lambda u, w: (member(u, w), 0, 0))
-    pairs = units * places * 2 * ROWS * GRP * KVH * kv[0].shape[1]
-    return pl.pallas_call(
-        attend_kernel,
-        grid_spec=pltpu.PrefetchScalarGridSpec(
-            num_scalar_prefetch=1,
-            grid=(units,),
-            in_specs=[pl.BlockSpec(dims, lambda u, w: (0, first + u, 0, 0))] + [keys] * KVH,
-            out_specs=pl.BlockSpec(dims, lambda u, w: (0, u, 0, 0)),
-        ),
-        out_shape=shape((places, units) + dims[2:]),
-        compiler_params=params(24),
+        k_all[cached:] = jnp.concatenate([part[:ROWS] for part in near], axis=0).astype(BF16)
+        v_all[cached:, :HD] = jnp.concatenate([part[ROWS:] for part in near], axis=0).astype(BF16)
+        stats = jnp.zeros((rows, HD), F32)
+        for j in range(GRP):
+            cols = slice(j * HD, (j + 1) * HD)
+            q = q_ref[:, first + u, :, cols].reshape(rows, HD)
+            scores = lax.dot_general(
+                q, k_all[...], (((1,), (1,)), ((), ())), preferred_element_type=F32
+            )
+            top = jnp.max(scores, axis=1, keepdims=True)
+            w = jnp.exp2((scores - top) * (SCALE * LOG2E))
+            both = jnp.dot(w.astype(BF16), v_all[...], preferred_element_type=F32)
+            total = both[:, HD:]
+            out = both[:, :HD] * (1.0 / total)
+            o_ref[:, u, :, cols] = out.astype(BF16).reshape(places, 2 * ROWS, HD)
+            for i, piece in enumerate(split_three(top * SCALE + jnp.log(total))):
+                stats = jnp.where(lane == i * GRP + j, piece, stats)
+        o_ref[:, u, :, GW:] = stats.astype(BF16).reshape(places, 2 * ROWS, HD)
+
+
+def attend(plan, queries, kv, first, members):
+    places, units = queries.shape[0], len(members)
+    keys = KVH * (kv[0].shape[1] + ROWS)
+    pairs = units * places * 2 * ROWS * GRP * keys
+    return pl.pallas_call(
+        functools.partial(attend_kernel, first, members),
+        in_specs=[in_smem()] + [in_vmem()] * (1 + KVH),
+        out_specs=in_vmem(),
+        out_shape=shape((places, units) + queries.shape[2:]),
+        scratch_shapes=[pltpu.VMEM((keys, HD), BF16), pltpu.VMEM((keys, 2 * HD), BF16)],
+        compiler_params=params(20),
         cost_estimate=cost(pairs * HD * 4, 4 * queries.size + 8 * kv[0].size, pairs),
         name="attend",
     )(plan, queries, *kv)
@@ -461,48 +463,42 @@
     query_first = masked_rows(opening_probe_vectors, opening_hidden_marks, blank_symbol_probe)
     block_first = masked_rows(opening_memory_pairs, opening_hidden_marks, blank_symbol_pairs)
 
-    homes = continuing_sequence_ids // seqs
-    slots = jnp.arange(homes.shape[0], dtype=jnp.int32)
-    earlier = (homes[None, :] == homes[:, None]) & (slots[None, :] < slots[:, None])
-    waits = jnp.any(earlier, axis=1)
-
-    def second_queries(turn, halves, *aheads):
-        got = swap(pick(plan, halves, OTHER + turn), "co")
-        return join(plan, halves, got, SLOT + turn, (wide, pair), *aheads)
+    def second_queries(turn, *aheads):
+        kept, lent = pick(plan, slot_halves, (SLOT + turn, OTHER + turn))
+        return join(kept, swap(lent, "co"), (wide, pair), *aheads)
 
     def second_member(turn):
-        return lambda unit, plan_ref: plan_ref[MEMBER + turn]
-
-    def hand_back(home_halves):
-        back = exchange(home_halves, DP)
-        got = swap(pick(plan, back, HOME_OTHER), "co")
-        return join(plan, back, got, HOME, (wide,))[0]
+        return lambda plan_ref: plan_ref[MEMBER + turn]
+
+    def hand_back(home_halves, *earlier):
+        back = after(exchange(home_halves, DP), *earlier)
+        kept, lent = pick(plan, back, (HOME, HOME_OTHER))
+        return kept, swap(lent, "co")
 
     def last_pass(early):
-        queries, pairs = second_queries(1, slot_halves)
+        queries, pairs = second_queries(1)
         second_in = exchange(pack(queries, swap(queries, "zh"), pairs), PLANE)
-        second_part = attend(plan, second_in, kv, 0, 1, second_member(1))
+        second_part = attend(plan, second_in, kv, 0, [second_member(1)])
         own, lse, far = fold(exchange(second_part, PLANE))
         late = hand_back(finish(own, lse, swap(far, "zh"), True))
-        group = lax.axis_index("zl") * lax.axis_size("co") + lax.axis_index("co")
-        return jnp.where(waits[group], late, early)
-
-    queries, pairs = second_queries(
-        0, after(slot_halves, kv[1], kv[2]), query_first, block_first
-    )
+        return tuple(jnp.where(plan[WAITS] > 0, new, old) for new, old in zip(late, early))
+
+    queries, pairs = second_queries(0, query_first, block_first)
     far = swap(queries, "zh")
-    everything = exchange(pack(queries, after(far, kv[3]), pairs), PLANE)
-    second_part = attend(plan, everything, kv, seqs, 1, second_member(0))
-    first_part = attend(plan, everything, kv, 0, seqs, lambda unit, plan_ref: unit)
+    everything = exchange(pack(queries, after(far, *kv[1:]), pairs), PLANE)
+
+    second_part = attend(plan, everything, kv, seqs, [second_member(0)])
+    first_part = attend(plan, everything, kv, 0, [lambda plan_ref, n=n: n for n in range(seqs)])
     second_back = exchange(second_part, PLANE)
     first_back = exchange(after(first_part, second_back), PLANE)
     own, lse, far = fold(second_back)
     home_out = finish(own, lse, swap(far, "zh"), True)
     own_first, lse_first, far_first = fold(first_back)
-    result = hand_back(after(home_out, first_back))
     first_out = finish(own_first, lse_first, swap(far_first, "zh"))
-    result = lax.cond(jnp.any(waits), last_pass, lambda early: early, result)
-    return first_out, result
+    shared = plan[SHARED] > 0
+    halves = hand_back(after(home_out, first_back), first_out, shared)
+    halves = lax.cond(shared, last_pass, lambda early: early, halves)
+    return first_out, join(*halves, (wide,))[0]
 
 
 def solution(mesh):

time: 181 us -> 160 us (0.88); the launches traced: 180 us -> 157 us
  waiting for transfers between devices: 44 us -> 29.3 us
  local copies, waits for them, and re-layouts: 5.73 us -> 2.19 us
  blocking collectives: 21.1 us -> 18.1 us
    ppermute x3, waiting for transfers between devices: 19.6 us -> 0.01 us  [across(): lax.ppermute(value, PLANE, [(i, i ^ steps) for i in range(width * lax.axi...]
    ppermute x5, starting transfers between devices: 28.9 us -> 36.8 us  [swap(): return lax.ppermute(value, axis, [(0, 1), (1, 0)])]
    all_to_all x4, starting transfers between devices: 44.1 us -> 36.6 us  [exchange(): return lax.all_to_all(value, axes, split_axis=0, concat_axis=0, tiled=True)]
    unnamed x28 -> x14, local copies, waits for them, and re-layouts: 5.73 us -> 1.61 us
    all_to_all x1, blocking collectives: 21.1 us -> 18.1 us  [exchange(): return lax.all_to_all(value, axes, split_axis=0, concat_axis=0, tiled=True)]
    ppermute x5, waiting for transfers between devices: 12.9 us -> 15.6 us  [swap(): return lax.ppermute(value, axis, [(0, 1), (1, 0)])]
    pallas_call x6, Pallas kernels: 18.8 us -> 16.2 us  [the longest x2 14.5 us: attend(): pl.pallas_call(functools.partial(attend_kernel, first, members), in_specs...]
    all_to_all x4, waiting for transfers between devices: 11.5 us -> 13.7 us  [exchange(): return lax.all_to_all(value, axes, split_axis=0, concat_axis=0, tiled=True)]
  transfers between devices with their start and end apart: 12 -> 12, of which waited for: 6 -> 7; matrix products, arithmetic and copies ran while one was open for 0% -> 0% of each run, Pallas kernels for 10% -> 10%
where the time goes in v3:
time: 160 us; the launch traced here: 157 us
  starting transfers between devices  81.8 us (51%)
  waiting for transfers between devices  29.3 us (18%)
  Pallas kernels  23.9 us (15%)
  blocking collectives  18.1 us (11%)
  local copies, waits for them, and re-layouts  2.19 us (1%)
    ppermute x5, starting transfers between devices, swap(): return lax.ppermute(value, axis, [(0, 1), (1, 0)])  36.8 us
    all_to_all x4, starting transfers between devices, exchange(): return lax.all_to_all(value, axes, split_axis=0, concat_axis=0, tiled=True)  36.6 us
    all_to_all x1, blocking collectives, exchange(): return lax.all_to_all(value, axes, split_axis=0, concat_axis=0, tiled=True)  18.1 us
    ppermute x5, waiting for transfers between devices, swap(): return lax.ppermute(value, axis, [(0, 1), (1, 0)])  15.6 us
    pallas_call x2, Pallas kernels, attend(): pl.pallas_call(functools.partial(attend_kernel, first, members), in_specs...  14.5 us
    all_to_all x4, waiting for transfers between devices, exchange(): return lax.all_to_all(value, axes, split_axis=0, concat_axis=0, tiled=True)  13.7 us
    ppermute x3, starting transfers between devices, across(): lax.ppermute(value, PLANE, [(i, i ^ steps) for i in range(width * lax.axi...  8.4 us
  transfers between devices with their start and end apart: 12, of which 7 were waited for; matrix products, arithmetic and copies ran while one was open for 0% of the time, Pallas kernels for 10%

profile of v3, /device:TPU:1, one launch (start us, length us, event | category | flops | bytes accessed | tf_op | source)
XLA Modules:
  0.0 157.1 jit_solution(10378849612092709270)
XLA Ops:
  0.7 1.7 %send_slots.1 = bf16[16,8,1536]{2,1,0:T(8,128)(2,1)} custom-call(bf16[1,8,2048]{2,1,0:T(8,128)(2,1)} %refs_0_.1, bf16[1,8,1024]{2,1,0:T(8,128)(2,1)} %refs_1_.1, s32[1,8]{1,0:T(1,128)} %refs_2_.1, bf16[16,128]{1,0:T(8,128)(2,1)} %bitcast.4, bf16[8,128]{1,0:T(8,128)(2,1)} %bitcast.5), custom_call_target="tpu_custom_call" | custom-call | bytes 393216 | tf_op jit(solution)/shard_map/send_slots/pallas_call | solution.py:168
  2.4 14.1 %all-to-all-start.3 = ((bf16[16,8,1536]{2,1,0:T(8,128)(2,1)}), bf16[16,8,1536]{2,1,0:T(8,128)(2,1)S(1)}, u32[]{:S(2)}, u32[]{:S(2)}) async-start(bf16[16,8,1536]{2,1,0:T(8,128)(2,1)} %send_slots.1), calls=%async_computation.3 | async-start | bytes 786432 | tf_op jit(solution)/shard_map/all_to_all | solution.py:418
  16.5 1.6 %copy-done = bf16[2,512,1024]{2,1,0:T(8,128)(2,1)S(1)} copy-done((bf16[2,512,1024]{2,1,0:T(8,128)(2,1)S(1)}, bf16[2,512,1024]{2,1,0:T(8,128)(2,1)}, u32[]{:S(2)}) %copy-start) | copy-done | bytes 2097176
  18.6 3.1 %collective-permute-start.6 = (bf16[2,512,256]{2,1,0:T(8,128)(2,1)S(1)}, bf16[2,512,256]{2,1,0:T(8,128)(2,1)S(1)}, u32[]{:S(2)}, u32[]{:S(2)}) collective-permute-start(bf16[2,512,256]{2,1,0:T(8,128)(2,1)S(1)} %get-tuple-element.64), channel_id=1, source_target_pairs={{0,1},{1,0},{2,3},{3,2},{4,5},{5,4},{6,7},{7,6},{8,9},{9,8},{10,11... | collective-permute-start | bytes 1572872 | tf_op jit(solution)/shard_map/ppermute | solution.py:424
  21.7 3.2 %collective-permute-start.7 = (bf16[2,512,256]{2,1,0:T(8,128)(2,1)S(1)}, bf16[2,512,256]{2,1,0:T(8,128)(2,1)}, u32[]{:S(2)}, u32[]{:S(2)}) collective-permute-start(bf16[2,512,256]{2,1,0:T(8,128)(2,1)S(1)} %get-tuple-element.65), channel_id=1, source_target_pairs={{0,4},{1,5},{2,6},{3,7},{4,0},{5,1},{6,2},{7,3},{8,12},{9,13},{10,... | collective-permute-start | bytes 1572872 | tf_op jit(solution)/shard_map/ppermute | solution.py:424
  24.9 2.0 %collective-permute-start.8 = (bf16[2,512,256]{2,1,0:T(8,128)(2,1)S(1)}, bf16[2,512,256]{2,1,0:T(8,128)(2,1)}, u32[]{:S(2)}, u32[]{:S(2)}) collective-permute-start(bf16[2,512,256]{2,1,0:T(8,128)(2,1)S(1)} %get-tuple-element.66), channel_id=1, source_target_pairs={{0,5},{1,4},{2,7},{3,6},{4,1},{5,0},{6,3},{7,2},{8,13},{9,12},{10,... | collective-permute-start | bytes 1572872 | tf_op jit(solution)/shard_map/ppermute | solution.py:424
  27.1 1.3 plan.1.plan_ref
  28.5 9.6 %all-to-all-done.3.halves_ref = bf16[16,8,1536]{2,1,0:T(8,128)(2,1)S(1)} async-done(((bf16[16,8,1536]{2,1,0:T(8,128)(2,1)}), bf16[16,8,1536]{2,1,0:T(8,128)(2,1)S(1)}, u32[]{:S(2)}, u32[]{:S(2)}) %all-to-all-start.3) | async-done | bytes 393248 | tf_op jit(solution)/shard_map/all_to_all | solution.py:418
  38.6 1.9 %collective-permute-start.4 = (bf16[1,8,1536]{2,1,0:T(8,128)(2,1)S(1)}, bf16[1,8,1536]{2,1,0:T(8,128)(2,1)S(1)}, u32[]{:S(2)}, u32[]{:S(2)}) collective-permute-start(bf16[1,8,1536]{2,1,0:T(8,128)(2,1)S(1)} %get-tuple-element.62), channel_id=1, source_target_pairs={{0,32},{32,0},{1,33},{33,1},{2,34},{34,2},{3,35},{35,3},{4,36},{36... | collective-permute-start | bytes 73736 | tf_op jit(solution)/shard_map/ppermute | solution.py:414
  41.7 7.9 %collective-permute-start.5 = (bf16[3,8,2048]{2,1,0:T(8,128)(2,1)S(1)}, bf16[3,8,2048]{2,1,0:T(8,128)(2,1)S(1)}, u32[]{:S(2)}, u32[]{:S(2)}) collective-permute-start(bf16[3,8,2048]{2,1,0:T(8,128)(2,1)S(1)} %get-tuple-element.63.own_ref), channel_id=1, source_target_pairs={{0,16},{16,0},{1,17},{17,1},{2,18},{18,2},{3,19},{19,3},{4,20},{20... | collective-permute-start | bytes 294920 | tf_op jit(solution)/shard_map/ppermute | solution.py:414
  49.7 6.9 %collective-permute-done.5.far_ref = bf16[3,8,2048]{2,1,0:T(8,128)(2,1)S(1)} collective-permute-done((bf16[3,8,2048]{2,1,0:T(8,128)(2,1)S(1)}, bf16[3,8,2048]{2,1,0:T(8,128)(2,1)S(1)}, u32[]{:S(2)}, u32[]{:S(2)}) %collective-permute-start.5) | collective-permute-done | bytes 98336 | tf_op jit(solution)/shard_map/ppermute | solution.py:414
  56.6 18.1 %all_to_all.39.q_ref = bf16[16,3,16,640]{3,2,1,0:T(8,128)(2,1)S(1)} all-to-all(bf16[16,3,16,640]{3,2,1,0:T(8,128)(2,1)S(1)} %pack_queries.3), channel_id=1, replica_groups=mesh['zl'=8,'co'=2,'zh'=2,'y'=4,'x'=4] {'y','x'}, dimensions={0} | all-to-all | bytes 1966080 | tf_op jit(solution)/shard_map/all_to_all | solution.py:418
  74.8 5.8 %attend.5 = bf16[16,1,16,640]{3,2,1,0:T(8,128)(2,1)} custom-call(s32[10]{0:T(128)S(1)} %plan.1.plan_ref, bf16[16,3,16,640]{3,2,1,0:T(8,128)(2,1)S(1)} %all_to_all.39.q_ref, bf16[2,512,256]{2,1,0:T(8,128)(2,1)S(1)} %get-tuple-element.69.refs_0_, bf16[2,512,256]{2,1,0:T(8,128)(2,1)S(1)} %collective-permute-done.6.refs_1_, ...), custom_call_target="tpu_custom_call" | custom-call | flops 1090519040 | bytes 4063232 | tf_op jit(solution)/shard_map/attend/pallas_call | solution.py:306
  80.5 3.7 %all-to-all-start.5 = ((bf16[16,1,16,640]{3,2,1,0:T(8,128)(2,1)}), bf16[16,1,16,640]{3,2,1,0:T(8,128)(2,1)S(1)}, u32[]{:S(2)}, u32[]{:S(2)}) async-start(bf16[16,1,16,640]{3,2,1,0:T(8,128)(2,1)} %attend.5), calls=%async_computation.5 | async-start | bytes 655360 | tf_op jit(solution)/shard_map/all_to_all | solution.py:418
  84.2 8.8 %attend.4 = bf16[16,2,16,640]{3,2,1,0:T(8,128)(2,1)} custom-call(s32[10]{0:T(128)S(1)} %plan.1.plan_ref, bf16[16,3,16,640]{3,2,1,0:T(8,128)(2,1)S(1)} %all_to_all.39.q_ref, bf16[2,512,256]{2,1,0:T(8,128)(2,1)S(1)} %get-tuple-element.69.refs_0_, bf16[2,512,256]{2,1,0:T(8,128)(2,1)S(1)} %collective-permute-done.6.refs_1_, ...), custom_call_target="tpu_custom_call" | custom-call | flops 2181038080 | bytes 4063232 | tf_op jit(solution)/shard_map/attend/pallas_call | solution.py:306
  93.0 6.4 %all-to-all-start.6 = ((bf16[16,2,16,640]{3,2,1,0:T(8,128)(2,1)}), bf16[16,2,16,640]{3,2,1,0:T(8,128)(2,1)S(1)}, u32[]{:S(2)}, u32[]{:S(2)}) async-start(bf16[16,2,16,640]{3,2,1,0:T(8,128)(2,1)} %attend.4), calls=%async_computation.6 | async-start | bytes 1310720 | tf_op jit(solution)/shard_map/all_to_all | solution.py:418
  100.1 17.1 %collective-permute-start.10 = (bf16[1,8,2176]{2,1,0:T(8,128)(2,1)S(1)}, bf16[1,8,2176]{2,1,0:T(8,128)(2,1)S(1)}, u32[]{:S(2)}, u32[]{:S(2)}) collective-permute-start(bf16[1,8,2176]{2,1,0:T(8,128)(2,1)S(1)} %get-tuple-element.76), channel_id=1, source_target_pairs={{0,16},{16,0},{1,17},{17,1},{2,18},{18,2},{3,19},{19,3},{4,20},{20... | collective-permute-start | bytes 104456 | tf_op jit(solution)/shard_map/ppermute | solution.py:414
  117.2 1.3 collective-permute-done.10.far_ref
  119.5 12.4 %all-to-all-start.7 = ((bf16[16,8,1024]{2,1,0:T(8,128)(2,1)}), bf16[16,8,1024]{2,1,0:T(8,128)(2,1)S(1)}, u32[]{:S(2)}, u32[]{:S(2)}) async-start(bf16[16,8,1024]{2,1,0:T(8,128)(2,1)} %finish.5), calls=%async_computation.7 | async-start | bytes 524288 | tf_op jit(solution)/shard_map/all_to_all | solution.py:418
  131.9 1.5 fold_plane.4
  133.4 8.0 %collective-permute-start.9 = (bf16[2,8,2176]{2,1,0:T(8,128)(2,1)S(1)}, bf16[2,8,2176]{2,1,0:T(8,128)(2,1)S(1)}, u32[]{:S(2)}, u32[]{:S(2)}) collective-permute-start(bf16[2,8,2176]{2,1,0:T(8,128)(2,1)S(1)} %get-tuple-element.73), channel_id=1, source_target_pairs={{0,16},{16,0},{1,17},{17,1},{2,18},{18,2},{3,19},{19,3},{4,20},{20... | collective-permute-start | bytes 208904 | tf_op jit(solution)/shard_map/ppermute | solution.py:414
  142.6 5.2 %collective-permute-done.9.far_ref = bf16[2,8,2176]{2,1,0:T(8,128)(2,1)S(1)} collective-permute-done((bf16[2,8,2176]{2,1,0:T(8,128)(2,1)S(1)}, bf16[2,8,2176]{2,1,0:T(8,128)(2,1)S(1)}, u32[]{:S(2)}, u32[]{:S(2)}) %collective-permute-start.9) | collective-permute-done | bytes 69664 | tf_op jit(solution)/shard_map/ppermute | solution.py:414
  148.7 4.2 %all-to-all-done.7.halves_ref = bf16[16,8,1024]{2,1,0:T(8,128)(2,1)S(1)} async-done(((bf16[16,8,1024]{2,1,0:T(8,128)(2,1)}), bf16[16,8,1024]{2,1,0:T(8,128)(2,1)S(1)}, u32[]{:S(2)}, u32[]{:S(2)}) %all-to-all-start.7) | async-done | bytes 262176 | tf_op jit(solution)/shard_map/all_to_all | solution.py:418
  153.4 1.9 %collective-permute-start.11 = (bf16[1,8,1024]{2,1,0:T(8,128)(2,1)S(1)}, bf16[1,8,1024]{2,1,0:T(8,128)(2,1)S(1)}, u32[]{:S(2)}, u32[]{:S(2)}) collective-permute-start(bf16[1,8,1024]{2,1,0:T(8,128)(2,1)S(1)} %get-tuple-element.80), channel_id=1, source_target_pairs={{0,32},{32,0},{1,33},{33,1},{2,34},{34,2},{3,35},{35,3},{4,36},{36... | collective-permute-start | bytes 49160 | tf_op jit(solution)/shard_map/ppermute | solution.py:414
  (34 shorter events, 7.9 us)
Async XLA Ops:
  0.6 26.4 %copy-start.4 = (bf16[2048]{0:T(1024)(128)(2,1)S(1)}, bf16[2048]{0:T(1024)(128)(2,1)}, u32[]{:S(2)}) copy-start(bf16[2048]{0:T(1024)(128)(2,1)} %param.20) | copy-start | bytes 12292
  0.6 39.9 %copy-start.5 = (bf16[1024]{0:T(1024)(128)(2,1)S(1)}, bf16[1024]{0:T(1024)(128)(2,1)}, u32[]{:S(2)}) copy-start(bf16[1024]{0:T(1024)(128)(2,1)} %param.21) | copy-start | bytes 6148
  0.7 26.4 %copy-start.6 = (s32[2,8]{1,0:T(2,128)S(1)}, s32[2,8]{1,0:T(2,128)}, u32[]{:S(2)}) copy-start(s32[2,8]{1,0:T(2,128)} %param.15) | copy-start | bytes 196
  0.7 26.4 %copy-start.2 = (bf16[2,8,2048]{2,1,0:T(8,128)(2,1)S(1)}, bf16[2,8,2048]{2,1,0:T(8,128)(2,1)}, u32[]{:S(2)}) copy-start(bf16[2,8,2048]{2,1,0:T(8,128)(2,1)} %param.13) | copy-start | bytes 196612
  0.7 26.5 %copy-start.1 = (s32[16]{0:T(128)S(1)}, s32[16]{0:T(128)}, u32[]{:S(2)}) copy-start(s32[16]{0:T(128)} %ids_ref.1) | copy-start | bytes 196
  0.7 39.9 %copy-start.3 = (bf16[2,8,1024]{2,1,0:T(8,128)(2,1)S(1)}, bf16[2,8,1024]{2,1,0:T(8,128)(2,1)}, u32[]{:S(2)}) copy-start(bf16[2,8,1024]{2,1,0:T(8,128)(2,1)} %param.14) | copy-start | bytes 98308
  2.4 35.7 %all-to-all-start.3 = ((bf16[16,8,1536]{2,1,0:T(8,128)(2,1)}), bf16[16,8,1536]{2,1,0:T(8,128)(2,1)S(1)}, u32[]{:S(2)}, u32[]{:S(2)}) async-start(bf16[16,8,1536]{2,1,0:T(8,128)(2,1)} %send_slots.1), calls=%async_computation.3 | async-start | bytes 786432 | tf_op jit(solution)/shard_map/all_to_all | solution.py:418
  16.4 1.6 %copy-start = (bf16[2,512,1024]{2,1,0:T(8,128)(2,1)S(1)}, bf16[2,512,1024]{2,1,0:T(8,128)(2,1)}, u32[]{:S(2)}) copy-start(bf16[2,512,1024]{2,1,0:T(8,128)(2,1)} %s_ref.1) | copy-start | bytes 6291460
  18.6 31.1 %collective-permute-start.6 = (bf16[2,512,256]{2,1,0:T(8,128)(2,1)S(1)}, bf16[2,512,256]{2,1,0:T(8,128)(2,1)S(1)}, u32[]{:S(2)}, u32[]{:S(2)}) collective-permute-start(bf16[2,512,256]{2,1,0:T(8,128)(2,1)S(1)} %get-tuple-element.64), channel_id=1, source_target_pairs={{0,1},{1,0},{2,3},{3,2},{4,5},{5,4},{6,7},{7,6},{8,9},{9,8},{10,11... | collective-permute-start | bytes 1572872 | tf_op jit(solution)/shard_map/ppermute | solution.py:424
  21.7 27.9 %collective-permute-start.7 = (bf16[2,512,256]{2,1,0:T(8,128)(2,1)S(1)}, bf16[2,512,256]{2,1,0:T(8,128)(2,1)}, u32[]{:S(2)}, u32[]{:S(2)}) collective-permute-start(bf16[2,512,256]{2,1,0:T(8,128)(2,1)S(1)} %get-tuple-element.65), channel_id=1, source_target_pairs={{0,4},{1,5},{2,6},{3,7},{4,0},{5,1},{6,2},{7,3},{8,12},{9,13},{10,... | collective-permute-start | bytes 1572872 | tf_op jit(solution)/shard_map/ppermute | solution.py:424
  24.9 24.7 %collective-permute-start.8 = (bf16[2,512,256]{2,1,0:T(8,128)(2,1)S(1)}, bf16[2,512,256]{2,1,0:T(8,128)(2,1)}, u32[]{:S(2)}, u32[]{:S(2)}) collective-permute-start(bf16[2,512,256]{2,1,0:T(8,128)(2,1)S(1)} %get-tuple-element.66), channel_id=1, source_target_pairs={{0,5},{1,4},{2,7},{3,6},{4,1},{5,0},{6,3},{7,2},{8,13},{9,12},{10,... | collective-permute-start | bytes 1572872 | tf_op jit(solution)/shard_map/ppermute | solution.py:424
  38.6 3.1 %collective-permute-start.4 = (bf16[1,8,1536]{2,1,0:T(8,128)(2,1)S(1)}, bf16[1,8,1536]{2,1,0:T(8,128)(2,1)S(1)}, u32[]{:S(2)}, u32[]{:S(2)}) collective-permute-start(bf16[1,8,1536]{2,1,0:T(8,128)(2,1)S(1)} %get-tuple-element.62), channel_id=1, source_target_pairs={{0,32},{32,0},{1,33},{33,1},{2,34},{34,2},{3,35},{35,3},{4,36},{36... | collective-permute-start | bytes 73736 | tf_op jit(solution)/shard_map/ppermute | solution.py:414
  41.7 14.9 %collective-permute-start.5 = (bf16[3,8,2048]{2,1,0:T(8,128)(2,1)S(1)}, bf16[3,8,2048]{2,1,0:T(8,128)(2,1)S(1)}, u32[]{:S(2)}, u32[]{:S(2)}) collective-permute-start(bf16[3,8,2048]{2,1,0:T(8,128)(2,1)S(1)} %get-tuple-element.63.own_ref), channel_id=1, source_target_pairs={{0,16},{16,0},{1,17},{17,1},{2,18},{18,2},{3,19},{19,3},{4,20},{20... | collective-permute-start | bytes 294920 | tf_op jit(solution)/shard_map/ppermute | solution.py:414
  80.5 12.5 %all-to-all-start.5 = ((bf16[16,1,16,640]{3,2,1,0:T(8,128)(2,1)}), bf16[16,1,16,640]{3,2,1,0:T(8,128)(2,1)S(1)}, u32[]{:S(2)}, u32[]{:S(2)}) async-start(bf16[16,1,16,640]{3,2,1,0:T(8,128)(2,1)} %attend.5), calls=%async_computation.5 | async-start | bytes 655360 | tf_op jit(solution)/shard_map/all_to_all | solution.py:418
  93.0 26.5 %all-to-all-start.6 = ((bf16[16,2,16,640]{3,2,1,0:T(8,128)(2,1)}), bf16[16,2,16,640]{3,2,1,0:T(8,128)(2,1)S(1)}, u32[]{:S(2)}, u32[]{:S(2)}) async-start(bf16[16,2,16,640]{3,2,1,0:T(8,128)(2,1)} %attend.4), calls=%async_computation.6 | async-start | bytes 1310720 | tf_op jit(solution)/shard_map/all_to_all | solution.py:418
  100.1 18.4 %collective-permute-start.10 = (bf16[1,8,2176]{2,1,0:T(8,128)(2,1)S(1)}, bf16[1,8,2176]{2,1,0:T(8,128)(2,1)S(1)}, u32[]{:S(2)}, u32[]{:S(2)}) collective-permute-start(bf16[1,8,2176]{2,1,0:T(8,128)(2,1)S(1)} %get-tuple-element.76), channel_id=1, source_target_pairs={{0,16},{16,0},{1,17},{17,1},{2,18},{18,2},{3,19},{19,3},{4,20},{20... | collective-permute-start | bytes 104456 | tf_op jit(solution)/shard_map/ppermute | solution.py:414
  119.5 33.4 %all-to-all-start.7 = ((bf16[16,8,1024]{2,1,0:T(8,128)(2,1)}), bf16[16,8,1024]{2,1,0:T(8,128)(2,1)S(1)}, u32[]{:S(2)}, u32[]{:S(2)}) async-start(bf16[16,8,1024]{2,1,0:T(8,128)(2,1)} %finish.5), calls=%async_computation.7 | async-start | bytes 524288 | tf_op jit(solution)/shard_map/all_to_all | solution.py:418
  133.4 14.4 %collective-permute-start.9 = (bf16[2,8,2176]{2,1,0:T(8,128)(2,1)S(1)}, bf16[2,8,2176]{2,1,0:T(8,128)(2,1)S(1)}, u32[]{:S(2)}, u32[]{:S(2)}) collective-permute-start(bf16[2,8,2176]{2,1,0:T(8,128)(2,1)S(1)} %get-tuple-element.73), channel_id=1, source_target_pairs={{0,16},{16,0},{1,17},{17,1},{2,18},{18,2},{3,19},{19,3},{4,20},{20... | collective-permute-start | bytes 208904 | tf_op jit(solution)/shard_map/ppermute | solution.py:414
  153.4 3.1 %collective-permute-start.11 = (bf16[1,8,1024]{2,1,0:T(8,128)(2,1)S(1)}, bf16[1,8,1024]{2,1,0:T(8,128)(2,1)S(1)}, u32[]{:S(2)}, u32[]{:S(2)}) collective-permute-start(bf16[1,8,1024]{2,1,0:T(8,128)(2,1)S(1)} %get-tuple-element.80), channel_id=1, source_target_pairs={{0,32},{32,0},{1,33},{33,1},{2,34},{34,2},{3,35},{35,3},{4,36},{36... | collective-permute-start | bytes 49160 | tf_op jit(solution)/shard_map/ppermute | solution.py:414

commit v4 on v3

--- a/solution.py
+++ b/solution.py
@@ -13,7 +13,6 @@
 GRP = QH // KVH
 GW = GRP * HD
 ROWS = 8
-PAY = GW + HD
 DP = ("zl", "co")
 PLANE = ("y", "x")
 CTX = ("zh", "y", "x")
@@ -109,25 +108,29 @@
     return head_of(lax.axis_index("y"), lax.axis_index("x"))
 
 
-def cut_kernel(s_ref, *outs):
+def cut_kernel(s_ref, b_ref, *outs):
     here = own_head()
+    seqs, rows, _ = s_ref.shape
     for d, out in enumerate(outs):
         head = jnp.bitwise_xor(here, d)
         for part in range(2):
-            start = pl.multiple_of((part * KVH + head) * HD, HD)
-            for n in range(out.shape[0]):
-                out[n, :, part * HD:(part + 1) * HD] = s_ref[n, :, pl.ds(start, HD)]
-
-
-def cut_by_head(stored):
+            columns = pl.ds(pl.multiple_of((part * KVH + head) * HD, HD), HD)
+            cols = slice(part * HD, (part + 1) * HD)
+            for n in range(seqs):
+                out[n * rows:(n + 1) * rows, cols] = s_ref[n, :, columns]
+            blocks = [b_ref[n, :, columns].astype(F32) for n in range(seqs)]
+            out[seqs * rows:, cols] = jnp.concatenate(blocks, axis=0).astype(BF16)
+
+
+def cut_by_head(stored, blocks):
     seqs, rows, _ = stored.shape
     return pl.pallas_call(
         cut_kernel,
-        out_shape=[shape((seqs, rows, 2 * HD))] * KVH,
+        out_shape=[shape((seqs * (rows + ROWS), 2 * HD))] * KVH,
         compiler_params=params(12),
         cost_estimate=cost(0, 4 * stored.size),
         name="cut_by_head",
-    )(stored)
+    )(stored, blocks)
 
 
 def send_kernel(*refs):
@@ -200,7 +203,7 @@
     first = 0
     for n, out in enumerate(outs):
         last = out.shape[0] - 1
-        if given:
+        if n < given:
             out[:last] = aheads[n][...]
         half = out.shape[2] // 2
         cols = slice(first, first + half)
@@ -219,10 +222,10 @@
 
 
 def join(kept, got, widths, *aheads):
-    units = 1 + (aheads[0].shape[0] if aheads else 0)
+    ahead = [value.shape[0] for value in aheads] + [0] * (len(widths) - len(aheads))
     return pl.pallas_call(
         functools.partial(join_kernel, len(aheads)),
-        out_shape=[shape((units, ROWS, width)) for width in widths],
+        out_shape=[shape((units + 1, ROWS, width)) for units, width in zip(ahead, widths)],
         compiler_params=params(2),
         cost_estimate=cost(0, 8 * kept.size),
         name="join",
@@ -231,24 +234,28 @@
 
 def pack_kernel(own_ref, far_ref, kv_ref, o_ref):
     width = lax.axis_size("x")
-    for u in range(own_ref.shape[0]):
-        for h in range(KVH):
-            cols = slice(h * GW, (h + 1) * GW)
-            q = jnp.concatenate(
+    units = own_ref.shape[0]
+    for h in range(KVH):
+        cols = slice(h * GW, (h + 1) * GW)
+        values = [
+            jnp.concatenate(
                 [own_ref[u, :, cols].astype(F32), far_ref[u, :, cols].astype(F32)], axis=0
             ).astype(BF16)
-            k = kv_ref[u, :, h * HD:(h + 1) * HD].astype(F32)
-            v = kv_ref[u, :, (KVH + h) * HD:(KVH + h + 1) * HD].astype(F32)
-            kv = jnp.concatenate([k, v], axis=0).astype(BF16)
-            for place in range(o_ref.shape[0]):
-                if head_of(place // width, place % width) == h:
-                    o_ref[place, u, :, :GW] = q
-                    o_ref[place, u, :, GW:] = kv
+            for u in range(units)
+        ]
+        k = kv_ref[0, :, h * HD:(h + 1) * HD].astype(F32)
+        v = kv_ref[0, :, (KVH + h) * HD:(KVH + h + 1) * HD].astype(F32)
+        kv = jnp.concatenate([k, v], axis=0).astype(BF16)
+        for place in range(o_ref.shape[0]):
+            if head_of(place // width, place % width) == h:
+                for u, value in enumerate(values):
+                    o_ref[place, :, u * GW:(u + 1) * GW] = value
+                o_ref[place, :, units * GW:] = kv
 
 
 def pack(own, far, kv):
     places = lax.axis_size("y") * lax.axis_size("x")
-    out = shape((places, own.shape[0], 2 * ROWS, PAY))
+    out = shape((places, 2 * ROWS, own.shape[0] * GW + HD))
     return pl.pallas_call(
         pack_kernel,
         out_shape=out,
@@ -258,33 +265,40 @@
     )(own, far, kv)
 
 
-def attend_kernel(first, members, plan_ref, q_ref, *refs):
+def attend_kernel(members, seqs, plan_ref, q_ref, *refs):
     kv_refs, o_ref, k_all, v_all = refs[:KVH], refs[KVH], refs[KVH + 1], refs[KVH + 2]
-    places, units = o_ref.shape[:2]
+    places, units = o_ref.shape[0], len(members)
     rows = places * 2 * ROWS
-    span = kv_refs[0].shape[1]
+    span = kv_refs[0].shape[0] // seqs - ROWS
     cached = KVH * span
     y, x = lax.axis_index("y"), lax.axis_index("x")
     width = lax.axis_size("x")
     corner = (y - (y & 1)) * width + x - (x & 1)
     lane = lax.broadcasted_iota(jnp.int32, (rows, HD), 1)
+    stats = jnp.zeros((rows, HD), F32)
     v_all[:, HD:] = jnp.ones((cached + KVH * ROWS, HD), BF16)
-    for u in range(units):
-        member = members[u](plan_ref)
+    for u, member in enumerate(members):
+        if isinstance(member, int):
+            blocks = [kv_ref[seqs * span:].astype(F32) for kv_ref in kv_refs]
+            own = slice(member * ROWS, (member + 1) * ROWS)
+            near = [(block[own, :HD], block[own, HD:]) for block in blocks]
+            start = member * span
+        else:
+            blocks = [
+                q_ref[corner + dy * width + dx, :, units * GW:].astype(F32)
+                for dy in range(2)
+                for dx in range(2)
+            ]
+            near = [(block[:ROWS], block[ROWS:]) for block in blocks]
+            start = pl.multiple_of(member(plan_ref) * span, span)
         for n, kv_ref in enumerate(kv_refs):
-            k_all[n * span:(n + 1) * span] = kv_ref[member, :, :HD]
-            v_all[n * span:(n + 1) * span, :HD] = kv_ref[member, :, HD:]
-        near = [
-            q_ref[corner + dy * width + dx, first + u, :, GW:].astype(F32)
-            for dy in range(2)
-            for dx in range(2)
-        ]
-        k_all[cached:] = jnp.concatenate([part[:ROWS] for part in near], axis=0).astype(BF16)
-        v_all[cached:, :HD] = jnp.concatenate([part[ROWS:] for part in near], axis=0).astype(BF16)
-        stats = jnp.zeros((rows, HD), F32)
+            k_all[n * span:(n + 1) * span] = kv_ref[pl.ds(start, span), :HD]
+            v_all[n * span:(n + 1) * span, :HD] = kv_ref[pl.ds(start, span), HD:]
+        k_all[cached:] = jnp.concatenate([k for k, _ in near], axis=0).astype(BF16)
+        v_all[cached:, :HD] = jnp.concatenate([v for _, v in near], axis=0).astype(BF16)
         for j in range(GRP):
-            cols = slice(j * HD, (j + 1) * HD)
-            q = q_ref[:, first + u, :, cols].reshape(rows, HD)
+            cols = slice(u * GW + j * HD, u * GW + (j + 1) * HD)
+            q = q_ref[:, :, cols].reshape(rows, HD)
             scores = lax.dot_general(
                 q, k_all[...], (((1,), (1,)), ((), ())), preferred_element_type=F32
             )
@@ -293,21 +307,21 @@
             both = jnp.dot(w.astype(BF16), v_all[...], preferred_element_type=F32)
             total = both[:, HD:]
             out = both[:, :HD] * (1.0 / total)
-            o_ref[:, u, :, cols] = out.astype(BF16).reshape(places, 2 * ROWS, HD)
+            o_ref[:, :, cols] = out.astype(BF16).reshape(places, 2 * ROWS, HD)
             for i, piece in enumerate(split_three(top * SCALE + jnp.log(total))):
-                stats = jnp.where(lane == i * GRP + j, piece, stats)
-        o_ref[:, u, :, GW:] = stats.astype(BF16).reshape(places, 2 * ROWS, HD)
-
-
-def attend(plan, queries, kv, first, members):
+                stats = jnp.where(lane == (3 * u + i) * GRP + j, piece, stats)
+    o_ref[:, :, units * GW:] = stats.astype(BF16).reshape(places, 2 * ROWS, HD)
+
+
+def attend(plan, queries, kv, members, seqs):
     places, units = queries.shape[0], len(members)
-    keys = KVH * (kv[0].shape[1] + ROWS)
+    keys = KVH * (kv[0].shape[0] // seqs)
     pairs = units * places * 2 * ROWS * GRP * keys
     return pl.pallas_call(
-        functools.partial(attend_kernel, first, members),
+        functools.partial(attend_kernel, members, seqs),
         in_specs=[in_smem()] + [in_vmem()] * (1 + KVH),
         out_specs=in_vmem(),
-        out_shape=shape((places, units) + queries.shape[2:]),
+        out_shape=shape(queries.shape),
         scratch_shapes=[pltpu.VMEM((keys, HD), BF16), pltpu.VMEM((keys, 2 * HD), BF16)],
         compiler_params=params(20),
         cost_estimate=cost(pairs * HD * 4, 4 * queries.size + 8 * kv[0].size, pairs),
@@ -329,29 +343,28 @@
 
 
 def fold_kernel(r_ref, own_ref, lse_ref, far_ref):
-    units = r_ref.shape[1]
+    units = own_ref.shape[0]
     rows = 2 * ROWS
     width = lax.axis_size("x")
-    places = [
-        [p for p in range(r_ref.shape[0]) if head_of(p // width, p % width) == h]
-        for h in range(KVH)
-    ]
     lane = lax.broadcasted_iota(jnp.int32, (rows, HD), 1)
     for u in range(units):
         near = jnp.zeros((rows, HD), F32)
         sent = jnp.zeros((rows, HD), F32)
-        for x in range(KVH):
+        for g in range(KVH):
+            places = [p for p in range(r_ref.shape[0]) if head_of(p // width, p % width) == g]
             tails = []
-            for place in places[x]:
-                tail = r_ref[place, u, :, GW:].astype(F32)
-                tails.append(
-                    tail[:, :GRP] + tail[:, GRP:2 * GRP] + tail[:, 2 * GRP:3 * GRP]
+            for place in places:
+                tail = r_ref[place, :, units * GW:].astype(F32)
+                first, second, third = (
+                    tail[:, (3 * u + i) * GRP:(3 * u + i + 1) * GRP] for i in range(3)
                 )
+                tails.append(first + second + third)
             for j in range(GRP):
-                h = x * GRP + j
+                h = g * GRP + j
+                cols = slice(u * GW + j * HD, u * GW + (j + 1) * HD)
                 out, lse = merge([
-                    (r_ref[place, u, :, j * HD:(j + 1) * HD].astype(F32), t[:, j:j + 1])
-                    for place, t in zip(places[x], tails)
+                    (r_ref[place, :, cols].astype(F32), tail[:, j:j + 1])
+                    for place, tail in zip(places, tails)
                 ])
                 own_ref[u, :, h * HD:(h + 1) * HD] = out[:ROWS]
                 far_ref[u, :, h * HD:(h + 1) * HD] = out[ROWS:].astype(BF16)
@@ -362,14 +375,13 @@
         far_ref[u, :, QH * HD:] = sent[ROWS:].astype(BF16)
 
 
-def fold(received):
-    units = received.shape[1]
+def fold(received, units):
     return pl.pallas_call(
         fold_kernel,
         out_shape=(
-            jax.ShapeDtypeStruct((units, ROWS, QH * HD), F32),
-            jax.ShapeDtypeStruct((units, ROWS, HD), F32),
-            jax.ShapeDtypeStruct((units, ROWS, QH * HD + HD), BF16),
+            shape((units, ROWS, QH * HD), F32),
+            shape((units, ROWS, HD), F32),
+            shape((units, ROWS, QH * HD + HD)),
         ),
         compiler_params=params(6),
         cost_estimate=cost(0, 4 * received.size),
@@ -377,9 +389,10 @@
     )(received)
 
 
-def finish_kernel(sending, own_ref, lse_ref, far_ref, o_ref):
+def finish_kernel(own_ref, lse_ref, far_ref, sent_ref, *kept):
     half = QH // 2
-    for u in range(own_ref.shape[0]):
+    units = own_ref.shape[0]
+    for u in reversed(range(units)):
         tail = far_ref[u, :, QH * HD:].astype(F32)
         far_lse = tail[:, :QH] + tail[:, QH:2 * QH] + tail[:, 2 * QH:3 * QH]
         for h in range(QH):
@@ -389,21 +402,22 @@
                 (far_ref[u, :, cols].astype(F32), far_lse[:, h:h + 1]),
             ])
             out = out.astype(BF16)
-            if sending:
-                part = h % half
-                for chip in range(o_ref.shape[0] // 2):
-                    o_ref[2 * chip + h // half, :, part * HD:(part + 1) * HD] = out
+            if u < units - 1:
+                kept[0][u, :, cols] = out
             else:
-                o_ref[u, :, cols] = out
-
-
-def finish(own, lse, far, sending=False):
-    out = shape(own.shape)
-    if sending:
-        out = shape((lax.axis_size("zl") * lax.axis_size("co"), ROWS, QH * HD // 2))
-    return pl.pallas_call(
-        functools.partial(finish_kernel, sending),
-        out_shape=out,
+                n = h % half
+                for chip in range(sent_ref.shape[0] // 2):
+                    sent_ref[2 * chip + h // half, :, n * HD:(n + 1) * HD] = out
+
+
+def finish(own, lse, far):
+    units = own.shape[0]
+    outs = [shape((lax.axis_size("zl") * lax.axis_size("co"), ROWS, QH * HD // 2))]
+    if units > 1:
+        outs.append(shape((units - 1,) + own.shape[1:]))
+    return pl.pallas_call(
+        finish_kernel,
+        out_shape=outs,
         compiler_params=params(4),
         cost_estimate=cost(0, 8 * own.size),
         name="finish",
@@ -457,15 +471,14 @@
         ),
         DP,
     )
-    pieces = cut_by_head(stored_memory)
-    kv = [pieces[0]] + [across(piece, d) for d, piece in enumerate(pieces) if d]
-
     query_first = masked_rows(opening_probe_vectors, opening_hidden_marks, blank_symbol_probe)
     block_first = masked_rows(opening_memory_pairs, opening_hidden_marks, blank_symbol_pairs)
-
-    def second_queries(turn, *aheads):
+    pieces = cut_by_head(stored_memory, block_first)
+    kv = [pieces[0]] + [across(piece, d) for d, piece in enumerate(pieces) if d]
+
+    def second_queries(turn, *ahead):
         kept, lent = pick(plan, slot_halves, (SLOT + turn, OTHER + turn))
-        return join(kept, swap(lent, "co"), (wide, pair), *aheads)
+        return join(kept, swap(lent, "co"), (wide, pair), *ahead)
 
     def second_member(turn):
         return lambda plan_ref: plan_ref[MEMBER + turn]
@@ -478,25 +491,21 @@
     def last_pass(early):
         queries, pairs = second_queries(1)
         second_in = exchange(pack(queries, swap(queries, "zh"), pairs), PLANE)
-        second_part = attend(plan, second_in, kv, 0, [second_member(1)])
-        own, lse, far = fold(exchange(second_part, PLANE))
-        late = hand_back(finish(own, lse, swap(far, "zh"), True))
+        second_part = attend(plan, second_in, kv, [second_member(1)], seqs)
+        own, lse, far = fold(exchange(second_part, PLANE), 1)
+        late = hand_back(finish(own, lse, swap(far, "zh"))[0])
         return tuple(jnp.where(plan[WAITS] > 0, new, old) for new, old in zip(late, early))
 
-    queries, pairs = second_queries(0, query_first, block_first)
+    queries, pairs = second_queries(0, query_first)
     far = swap(queries, "zh")
     everything = exchange(pack(queries, after(far, *kv[1:]), pairs), PLANE)
 
-    second_part = attend(plan, everything, kv, seqs, [second_member(0)])
-    first_part = attend(plan, everything, kv, 0, [lambda plan_ref, n=n: n for n in range(seqs)])
-    second_back = exchange(second_part, PLANE)
-    first_back = exchange(after(first_part, second_back), PLANE)
-    own, lse, far = fold(second_back)
-    home_out = finish(own, lse, swap(far, "zh"), True)
-    own_first, lse_first, far_first = fold(first_back)
-    first_out = finish(own_first, lse_first, swap(far_first, "zh"))
+    members = list(range(seqs)) + [second_member(0)]
+    partial = attend(plan, everything, kv, members, seqs)
+    own, lse, far = fold(exchange(partial, PLANE), len(members))
+    home_halves, first_out = finish(own, lse, swap(far, "zh"))
     shared = plan[SHARED] > 0
-    halves = hand_back(after(home_out, first_back), first_out, shared)
+    halves = hand_back(home_halves, shared)
     halves = lax.cond(shared, last_pass, lambda early: early, halves)
     return first_out, join(*halves, (wide,))[0]
 

time: 160 us -> 158 us (0.988); the launches traced: 157 us -> 157 us
  starting transfers between devices: 81.8 us -> 65.3 us
  blocking collectives: 18.1 us -> 30.9 us
  waiting for transfers between devices: 29.3 us -> 36 us
  Pallas kernels: 23.9 us -> 19.6 us
    all_to_all x1 -> x2, blocking collectives: 18.1 us -> 30.9 us  [exchange(): return lax.all_to_all(value, axes, split_axis=0, concat_axis=0, tiled=True)]
    all_to_all x4 -> x2, starting transfers between devices: 36.6 us -> 25.1 us  [exchange(): return lax.all_to_all(value, axes, split_axis=0, concat_axis=0, tiled=True)]
    all_to_all x4 -> x2, waiting for transfers between devices: 13.7 us -> 23.9 us  [exchange(): return lax.all_to_all(value, axes, split_axis=0, concat_axis=0, tiled=True)]
    ppermute x5 -> x4, starting transfers between devices: 36.8 us -> 31.9 us  [swap(): return lax.ppermute(value, axis, [(0, 1), (1, 0)])]
    pallas_call x7 -> x4, Pallas kernels: 19.1 us -> 14.8 us  [the longest x1 10.9 us: attend(): pl.pallas_call(functools.partial(attend_kernel, members, seqs), in_specs=...]
    ppermute x5 -> x4, waiting for transfers between devices: 15.6 us -> 11.7 us  [swap(): return lax.ppermute(value, axis, [(0, 1), (1, 0)])]
  transfers between devices with their start and end apart: 12 -> 9, of which waited for: 7 -> 7; matrix products, arithmetic and copies ran while one was open for 0% -> 1% of each run, Pallas kernels for 10% -> 2%
where the time goes in v4:
time: 158 us; the launch traced here: 157 us
  starting transfers between devices  65.3 us (41%)
  waiting for transfers between devices  36 us (23%)
  blocking collectives  30.9 us (20%)
  Pallas kernels  19.6 us (12%)
  local copies, waits for them, and re-layouts  2.18 us (1%)
  other arithmetic  1.6 us (1%)
    ppermute x4, starting transfers between devices, swap(): return lax.ppermute(value, axis, [(0, 1), (1, 0)])  31.9 us
    all_to_all x2, blocking collectives, exchange(): return lax.all_to_all(value, axes, split_axis=0, concat_axis=0, tiled=True)  30.9 us
    all_to_all x2, starting transfers between devices, exchange(): return lax.all_to_all(value, axes, split_axis=0, concat_axis=0, tiled=True)  25.1 us
    all_to_all x2, waiting for transfers between devices, exchange(): return lax.all_to_all(value, axes, split_axis=0, concat_axis=0, tiled=True)  23.9 us
    ppermute x4, waiting for transfers between devices, swap(): return lax.ppermute(value, axis, [(0, 1), (1, 0)])  11.7 us
    pallas_call x1, Pallas kernels, attend(): pl.pallas_call(functools.partial(attend_kernel, members, seqs), in_specs=...  10.9 us
    ppermute x3, starting transfers between devices, across(): lax.ppermute(value, PLANE, [(i, i ^ steps) for i in range(width * lax.axi...  8.4 us
  transfers between devices with their start and end apart: 9, of which 7 were waited for; matrix products, arithmetic and copies ran while one was open for 1% of the time, Pallas kernels for 2%

profile of v4, /device:TPU:1, one launch (start us, length us, event | category | flops | bytes accessed | tf_op | source)
XLA Modules:
  0.0 157.0 jit_solution(10917821042446958387)
XLA Ops:
  0.7 1.7 %send_slots.1 = bf16[16,8,1536]{2,1,0:T(8,128)(2,1)} custom-call(bf16[1,8,2048]{2,1,0:T(8,128)(2,1)} %refs_0_.1, bf16[1,8,1024]{2,1,0:T(8,128)(2,1)} %refs_1_.1, s32[1,8]{1,0:T(1,128)} %refs_2_.1, bf16[16,128]{1,0:T(8,128)(2,1)} %bitcast.4, bf16[8,128]{1,0:T(8,128)(2,1)} %bitcast.5), custom_call_target="tpu_custom_call" | custom-call | bytes 393216 | tf_op jit(solution)/shard_map/send_slots/pallas_call | solution.py:171
  2.4 14.1 %all-to-all-start.3 = ((bf16[16,8,1536]{2,1,0:T(8,128)(2,1)}), bf16[16,8,1536]{2,1,0:T(8,128)(2,1)S(1)}, u32[]{:S(2)}, u32[]{:S(2)}) async-start(bf16[16,8,1536]{2,1,0:T(8,128)(2,1)} %send_slots.1), calls=%async_computation.3 | async-start | bytes 786432 | tf_op jit(solution)/shard_map/all_to_all | solution.py:432
  17.1 0.8 broadcast_select_fusion.3.b_ref
  17.9 1.6 %copy-done = bf16[2,512,1024]{2,1,0:T(8,128)(2,1)S(1)} copy-done((bf16[2,512,1024]{2,1,0:T(8,128)(2,1)S(1)}, bf16[2,512,1024]{2,1,0:T(8,128)(2,1)}, u32[]{:S(2)}) %copy-start) | copy-done | bytes 2097176
  20.1 3.1 %collective-permute-start.6 = (bf16[1040,256]{1,0:T(8,128)(2,1)S(1)}, bf16[1040,256]{1,0:T(8,128)(2,1)S(1)}, u32[]{:S(2)}, u32[]{:S(2)}) collective-permute-start(bf16[1040,256]{1,0:T(8,128)(2,1)S(1)} %get-tuple-element.61), channel_id=1, source_target_pairs={{0,1},{1,0},{2,3},{3,2},{4,5},{5,4},{6,7},{7,6},{8,9},{9,8},{10,11... | collective-permute-start | bytes 1597448 | tf_op jit(solution)/shard_map/ppermute | solution.py:438
  23.2 3.2 %collective-permute-start.7 = (bf16[1040,256]{1,0:T(8,128)(2,1)S(1)}, bf16[1040,256]{1,0:T(8,128)(2,1)}, u32[]{:S(2)}, u32[]{:S(2)}) collective-permute-start(bf16[1040,256]{1,0:T(8,128)(2,1)S(1)} %get-tuple-element.62), channel_id=1, source_target_pairs={{0,4},{1,5},{2,6},{3,7},{4,0},{5,1},{6,2},{7,3},{8,12},{9,13},{10,... | collective-permute-start | bytes 1597448 | tf_op jit(solution)/shard_map/ppermute | solution.py:438
  26.4 2.0 %collective-permute-start.8 = (bf16[1040,256]{1,0:T(8,128)(2,1)S(1)}, bf16[1040,256]{1,0:T(8,128)(2,1)}, u32[]{:S(2)}, u32[]{:S(2)}) collective-permute-start(bf16[1040,256]{1,0:T(8,128)(2,1)S(1)} %get-tuple-element.63), channel_id=1, source_target_pairs={{0,5},{1,4},{2,7},{3,6},{4,1},{5,0},{6,3},{7,2},{8,13},{9,12},{10,... | collective-permute-start | bytes 1597448 | tf_op jit(solution)/shard_map/ppermute | solution.py:438
  28.5 1.3 plan.1.plan_ref
  29.9 8.2 %all-to-all-done.3.halves_ref = bf16[16,8,1536]{2,1,0:T(8,128)(2,1)S(1)} async-done(((bf16[16,8,1536]{2,1,0:T(8,128)(2,1)}), bf16[16,8,1536]{2,1,0:T(8,128)(2,1)S(1)}, u32[]{:S(2)}, u32[]{:S(2)}) %all-to-all-start.3) | async-done | bytes 393248 | tf_op jit(solution)/shard_map/all_to_all | solution.py:432
  38.6 1.9 %collective-permute-start.4 = (bf16[1,8,1536]{2,1,0:T(8,128)(2,1)S(1)}, bf16[1,8,1536]{2,1,0:T(8,128)(2,1)S(1)}, u32[]{:S(2)}, u32[]{:S(2)}) collective-permute-start(bf16[1,8,1536]{2,1,0:T(8,128)(2,1)S(1)} %get-tuple-element.59), channel_id=1, source_target_pairs={{0,32},{32,0},{1,33},{33,1},{2,34},{34,2},{3,35},{35,3},{4,36},{36... | collective-permute-start | bytes 73736 | tf_op jit(solution)/shard_map/ppermute | solution.py:428
  40.6 1.1 collective-permute-done.4.got_ref
  41.7 7.9 %collective-permute-start.5 = (bf16[3,8,2048]{2,1,0:T(8,128)(2,1)S(1)}, bf16[3,8,2048]{2,1,0:T(8,128)(2,1)S(1)}, u32[]{:S(2)}, u32[]{:S(2)}) collective-permute-start(bf16[3,8,2048]{2,1,0:T(8,128)(2,1)S(1)} %get-tuple-element.60.own_ref), channel_id=1, source_target_pairs={{0,16},{16,0},{1,17},{17,1},{2,18},{18,2},{3,19},{19,3},{4,20},{20... | collective-permute-start | bytes 294920 | tf_op jit(solution)/shard_map/ppermute | solution.py:428
  50.0 6.6 %collective-permute-done.5.far_ref = bf16[3,8,2048]{2,1,0:T(8,128)(2,1)S(1)} collective-permute-done((bf16[3,8,2048]{2,1,0:T(8,128)(2,1)S(1)}, bf16[3,8,2048]{2,1,0:T(8,128)(2,1)S(1)}, u32[]{:S(2)}, u32[]{:S(2)}) %collective-permute-start.5) | collective-permute-done | bytes 98336 | tf_op jit(solution)/shard_map/ppermute | solution.py:428
  56.6 17.5 %all_to_all.34.q_ref = bf16[16,16,1664]{2,1,0:T(8,128)(2,1)S(1)} all-to-all(bf16[16,16,1664]{2,1,0:T(8,128)(2,1)S(1)} %pack_queries.3), channel_id=1, replica_groups=mesh['zl'=8,'co'=2,'zh'=2,'y'=4,'x'=4] {'y','x'}, dimensions={0} | all-to-all | bytes 1703936 | tf_op jit(solution)/shard_map/all_to_all | solution.py:432
  74.1 10.9 %attend.3 = bf16[16,16,1664]{2,1,0:T(8,128)(2,1)S(1)} custom-call(s32[10]{0:T(128)S(1)} %plan.1.plan_ref, bf16[16,16,1664]{2,1,0:T(8,128)(2,1)S(1)} %all_to_all.34.q_ref, bf16[1040,256]{1,0:T(8,128)(2,1)S(1)} %get-tuple-element.66.refs_0_, bf16[1040,256]{1,0:T(8,128)(2,1)S(1)} %collective-permute-done.6.refs_1_, ...), custom_call_target="tpu_custom_call" | custom-call | flops 3271557120 | bytes 3833856 | tf_op jit(solution)/shard_map/attend/pallas_call | solution.py:320
  85.0 13.4 %all_to_all.35.r_ref = bf16[16,16,1664]{2,1,0:T(8,128)(2,1)S(1)} all-to-all(bf16[16,16,1664]{2,1,0:T(8,128)(2,1)S(1)} %attend.3), channel_id=1, replica_groups=mesh['zl'=8,'co'=2,'zh'=2,'y'=4,'x'=4] {'y','x'}, dimensions={0} | all-to-all | bytes 1703936 | tf_op jit(solution)/shard_map/all_to_all | solution.py:432
  98.4 2.2 %fold_plane.3 = (f32[3,8,2048]{2,1,0:T(8,128)S(1)}, f32[3,8,128]{2,1,0:T(8,128)S(1)}, bf16[3,8,2176]{2,1,0:T(8,128)(2,1)S(1)}) custom-call(bf16[16,16,1664]{2,1,0:T(8,128)(2,1)S(1)} %all_to_all.35.r_ref), custom_call_target="tpu_custom_call" | custom-call | bytes 1703936 | tf_op jit(solution)/shard_map/fold_plane/pallas_call | solution.py:379
  100.5 20.1 %collective-permute-start.9 = (bf16[3,8,2176]{2,1,0:T(8,128)(2,1)S(1)}, bf16[3,8,2176]{2,1,0:T(8,128)(2,1)S(1)}, u32[]{:S(2)}, u32[]{:S(2)}) collective-permute-start(bf16[3,8,2176]{2,1,0:T(8,128)(2,1)S(1)} %get-tuple-element.69), channel_id=1, source_target_pairs={{0,16},{16,0},{1,17},{17,1},{2,18},{18,2},{3,19},{19,3},{4,20},{20... | collective-permute-start | bytes 313352 | tf_op jit(solution)/shard_map/ppermute | solution.py:428
  120.6 3.0 %collective-permute-done.9.far_ref = bf16[3,8,2176]{2,1,0:T(8,128)(2,1)S(1)} collective-permute-done((bf16[3,8,2176]{2,1,0:T(8,128)(2,1)S(1)}, bf16[3,8,2176]{2,1,0:T(8,128)(2,1)S(1)}, u32[]{:S(2)}, u32[]{:S(2)}) %collective-permute-start.9) | collective-permute-done | bytes 104480 | tf_op jit(solution)/shard_map/ppermute | solution.py:428
  123.6 1.2 finish.3
  124.8 11.0 %all-to-all-start.6 = ((bf16[16,8,1024]{2,1,0:T(8,128)(2,1)}), bf16[16,8,1024]{2,1,0:T(8,128)(2,1)S(1)}, u32[]{:S(2)}, u32[]{:S(2)}) async-start(bf16[16,8,1024]{2,1,0:T(8,128)(2,1)} %get-tuple-element.71), calls=%async_computation.6 | async-start | bytes 524288 | tf_op jit(solution)/shard_map/all_to_all | solution.py:432
  137.0 15.8 %all-to-all-done.6.halves_ref = bf16[16,8,1024]{2,1,0:T(8,128)(2,1)S(1)} async-done(((bf16[16,8,1024]{2,1,0:T(8,128)(2,1)}), bf16[16,8,1024]{2,1,0:T(8,128)(2,1)S(1)}, u32[]{:S(2)}, u32[]{:S(2)}) %all-to-all-start.6) | async-done | bytes 262176 | tf_op jit(solution)/shard_map/all_to_all | solution.py:432
  153.3 1.9 %collective-permute-start.10 = (bf16[1,8,1024]{2,1,0:T(8,128)(2,1)S(1)}, bf16[1,8,1024]{2,1,0:T(8,128)(2,1)S(1)}, u32[]{:S(2)}, u32[]{:S(2)}) collective-permute-start(bf16[1,8,1024]{2,1,0:T(8,128)(2,1)S(1)} %get-tuple-element.74), channel_id=1, source_target_pairs={{0,32},{32,0},{1,33},{33,1},{2,34},{34,2},{3,35},{35,3},{4,36},{36... | collective-permute-start | bytes 49160 | tf_op jit(solution)/shard_map/ppermute | solution.py:428
  155.3 1.1 collective-permute-done.10
  (20 shorter events, 4.0 us)
Async XLA Ops:
  0.6 39.9 %copy-start.3 = (bf16[2048]{0:T(1024)(128)(2,1)S(1)}, bf16[2048]{0:T(1024)(128)(2,1)}, u32[]{:S(2)}) copy-start(bf16[2048]{0:T(1024)(128)(2,1)} %param.20) | copy-start | bytes 12292
  0.6 27.9 %copy-start.1 = (s32[16]{0:T(128)S(1)}, s32[16]{0:T(128)}, u32[]{:S(2)}) copy-start(s32[16]{0:T(128)} %ids_ref.1) | copy-start | bytes 196
  0.7 39.9 %copy-start.2 = (bf16[2,8,2048]{2,1,0:T(8,128)(2,1)S(1)}, bf16[2,8,2048]{2,1,0:T(8,128)(2,1)}, u32[]{:S(2)}) copy-start(bf16[2,8,2048]{2,1,0:T(8,128)(2,1)} %param.13) | copy-start | bytes 196612
  2.4 35.7 %all-to-all-start.3 = ((bf16[16,8,1536]{2,1,0:T(8,128)(2,1)}), bf16[16,8,1536]{2,1,0:T(8,128)(2,1)S(1)}, u32[]{:S(2)}, u32[]{:S(2)}) async-start(bf16[16,8,1536]{2,1,0:T(8,128)(2,1)} %send_slots.1), calls=%async_computation.3 | async-start | bytes 786432 | tf_op jit(solution)/shard_map/all_to_all | solution.py:432
  17.9 1.6 %copy-start = (bf16[2,512,1024]{2,1,0:T(8,128)(2,1)S(1)}, bf16[2,512,1024]{2,1,0:T(8,128)(2,1)}, u32[]{:S(2)}) copy-start(bf16[2,512,1024]{2,1,0:T(8,128)(2,1)} %s_ref.1) | copy-start | bytes 6291460
  20.1 29.6 %collective-permute-start.6 = (bf16[1040,256]{1,0:T(8,128)(2,1)S(1)}, bf16[1040,256]{1,0:T(8,128)(2,1)S(1)}, u32[]{:S(2)}, u32[]{:S(2)}) collective-permute-start(bf16[1040,256]{1,0:T(8,128)(2,1)S(1)} %get-tuple-element.61), channel_id=1, source_target_pairs={{0,1},{1,0},{2,3},{3,2},{4,5},{5,4},{6,7},{7,6},{8,9},{9,8},{10,11... | collective-permute-start | bytes 1597448 | tf_op jit(solution)/shard_map/ppermute | solution.py:438
  23.2 26.7 %collective-permute-start.7 = (bf16[1040,256]{1,0:T(8,128)(2,1)S(1)}, bf16[1040,256]{1,0:T(8,128)(2,1)}, u32[]{:S(2)}, u32[]{:S(2)}) collective-permute-start(bf16[1040,256]{1,0:T(8,128)(2,1)S(1)} %get-tuple-element.62), channel_id=1, source_target_pairs={{0,4},{1,5},{2,6},{3,7},{4,0},{5,1},{6,2},{7,3},{8,12},{9,13},{10,... | collective-permute-start | bytes 1597448 | tf_op jit(solution)/shard_map/ppermute | solution.py:438
  26.4 23.5 %collective-permute-start.8 = (bf16[1040,256]{1,0:T(8,128)(2,1)S(1)}, bf16[1040,256]{1,0:T(8,128)(2,1)}, u32[]{:S(2)}, u32[]{:S(2)}) collective-permute-start(bf16[1040,256]{1,0:T(8,128)(2,1)S(1)} %get-tuple-element.63), channel_id=1, source_target_pairs={{0,5},{1,4},{2,7},{3,6},{4,1},{5,0},{6,3},{7,2},{8,13},{9,12},{10,... | collective-permute-start | bytes 1597448 | tf_op jit(solution)/shard_map/ppermute | solution.py:438
  38.6 3.1 %collective-permute-start.4 = (bf16[1,8,1536]{2,1,0:T(8,128)(2,1)S(1)}, bf16[1,8,1536]{2,1,0:T(8,128)(2,1)S(1)}, u32[]{:S(2)}, u32[]{:S(2)}) collective-permute-start(bf16[1,8,1536]{2,1,0:T(8,128)(2,1)S(1)} %get-tuple-element.59), channel_id=1, source_target_pairs={{0,32},{32,0},{1,33},{33,1},{2,34},{34,2},{3,35},{35,3},{4,36},{36... | collective-permute-start | bytes 73736 | tf_op jit(solution)/shard_map/ppermute | solution.py:428
  41.7 14.9 %collective-permute-start.5 = (bf16[3,8,2048]{2,1,0:T(8,128)(2,1)S(1)}, bf16[3,8,2048]{2,1,0:T(8,128)(2,1)S(1)}, u32[]{:S(2)}, u32[]{:S(2)}) collective-permute-start(bf16[3,8,2048]{2,1,0:T(8,128)(2,1)S(1)} %get-tuple-element.60.own_ref), channel_id=1, source_target_pairs={{0,16},{16,0},{1,17},{17,1},{2,18},{18,2},{3,19},{19,3},{4,20},{20... | collective-permute-start | bytes 294920 | tf_op jit(solution)/shard_map/ppermute | solution.py:428
  100.5 23.1 %collective-permute-start.9 = (bf16[3,8,2176]{2,1,0:T(8,128)(2,1)S(1)}, bf16[3,8,2176]{2,1,0:T(8,128)(2,1)S(1)}, u32[]{:S(2)}, u32[]{:S(2)}) collective-permute-start(bf16[3,8,2176]{2,1,0:T(8,128)(2,1)S(1)} %get-tuple-element.69), channel_id=1, source_target_pairs={{0,16},{16,0},{1,17},{17,1},{2,18},{18,2},{3,19},{19,3},{4,20},{20... | collective-permute-start | bytes 313352 | tf_op jit(solution)/shard_map/ppermute | solution.py:428
  124.8 28.0 %all-to-all-start.6 = ((bf16[16,8,1024]{2,1,0:T(8,128)(2,1)}), bf16[16,8,1024]{2,1,0:T(8,128)(2,1)S(1)}, u32[]{:S(2)}, u32[]{:S(2)}) async-start(bf16[16,8,1024]{2,1,0:T(8,128)(2,1)} %get-tuple-element.71), calls=%async_computation.6 | async-start | bytes 524288 | tf_op jit(solution)/shard_map/all_to_all | solution.py:432
  153.3 3.1 %collective-permute-start.10 = (bf16[1,8,1024]{2,1,0:T(8,128)(2,1)S(1)}, bf16[1,8,1024]{2,1,0:T(8,128)(2,1)S(1)}, u32[]{:S(2)}, u32[]{:S(2)}) collective-permute-start(bf16[1,8,1024]{2,1,0:T(8,128)(2,1)S(1)} %get-tuple-element.74), channel_id=1, source_target_pairs={{0,32},{32,0},{1,33},{33,1},{2,34},{34,2},{3,35},{35,3},{4,36},{36... | collective-permute-start | bytes 49160 | tf_op jit(solution)/shard_map/ppermute | solution.py:428

commit v5 on v4

--- a/solution.py
+++ b/solution.py
@@ -232,7 +232,8 @@
     )(kept, got, *aheads)
 
 
-def pack_kernel(own_ref, far_ref, kv_ref, o_ref):
+def pack_kernel(own_ref, both_ref, kv_ref, o_ref):
+    far_ref = both_ref.at[1 - lax.axis_index("zh")]
     width = lax.axis_size("x")
     units = own_ref.shape[0]
     for h in range(KVH):
@@ -389,7 +390,8 @@
     )(received)
 
 
-def finish_kernel(own_ref, lse_ref, far_ref, sent_ref, *kept):
+def finish_kernel(own_ref, lse_ref, both_ref, sent_ref, *kept):
+    far_ref = both_ref.at[1 - lax.axis_index("zh")]
     half = QH // 2
     units = own_ref.shape[0]
     for u in reversed(range(units)):
@@ -436,6 +438,10 @@
     width = lax.axis_size("x")
     steps = (d & 1) + width * (d >> 1)
     return lax.ppermute(value, PLANE, [(i, i ^ steps) for i in range(width * lax.axis_size("y"))])
+
+
+def both_z(value):
+    return lax.all_gather(value, "zh", axis=0)
 
 
 def after(value, *earlier):
@@ -490,20 +496,20 @@
 
     def last_pass(early):
         queries, pairs = second_queries(1)
-        second_in = exchange(pack(queries, swap(queries, "zh"), pairs), PLANE)
+        second_in = exchange(pack(queries, both_z(queries), pairs), PLANE)
         second_part = attend(plan, second_in, kv, [second_member(1)], seqs)
         own, lse, far = fold(exchange(second_part, PLANE), 1)
-        late = hand_back(finish(own, lse, swap(far, "zh"))[0])
+        late = hand_back(finish(own, lse, both_z(far))[0])
         return tuple(jnp.where(plan[WAITS] > 0, new, old) for new, old in zip(late, early))
 
     queries, pairs = second_queries(0, query_first)
-    far = swap(queries, "zh")
+    far = both_z(queries)
     everything = exchange(pack(queries, after(far, *kv[1:]), pairs), PLANE)
 
     members = list(range(seqs)) + [second_member(0)]
     partial = attend(plan, everything, kv, members, seqs)
     own, lse, far = fold(exchange(partial, PLANE), len(members))
-    home_halves, first_out = finish(own, lse, swap(far, "zh"))
+    home_halves, first_out = finish(own, lse, both_z(far))
     shared = plan[SHARED] > 0
     halves = hand_back(home_halves, shared)
     halves = lax.cond(shared, last_pass, lambda early: early, halves)

time: 158 us -> 155 us (0.981)
  blocking collectives: 30.9 us -> 66.4 us
  starting transfers between devices: 65.3 us -> 37.3 us
  waiting for transfers between devices: 36 us -> 26.1 us
    all_gather x0 -> x2, blocking collectives: none -> 35.5 us  [both_z(): return lax.all_gather(value, 'zh', axis=0)]
    ppermute x4 -> x2, starting transfers between devices: 31.9 us -> 3.84 us  [swap(): return lax.ppermute(value, axis, [(0, 1), (1, 0)])]
    ppermute x4 -> x2, waiting for transfers between devices: 11.7 us -> 2.21 us  [swap(): return lax.ppermute(value, axis, [(0, 1), (1, 0)])]
  transfers between devices with their start and end apart: 9 -> 7, of which waited for: 7 -> 4; matrix products, arithmetic and copies ran while one was open for 1% -> 1% of each run, Pallas kernels for 2% -> 2%
where the time goes in v5:
time: 155 us
  blocking collectives  66.4 us (43%)
  starting transfers between devices  37.3 us (24%)
  waiting for transfers between devices  26.1 us (17%)
  Pallas kernels  19.6 us (13%)
  local copies, waits for them, and re-layouts  2.18 us (1%)
  other arithmetic  1.6 us (1%)
    all_gather x2, blocking collectives, both_z(): return lax.all_gather(value, 'zh', axis=0)  35.5 us
    all_to_all x2, blocking collectives, exchange(): return lax.all_to_all(value, axes, split_axis=0, concat_axis=0, tiled=True)  30.9 us
    all_to_all x2, starting transfers between devices, exchange(): return lax.all_to_all(value, axes, split_axis=0, concat_axis=0, tiled=True)  25.1 us
    all_to_all x2, waiting for transfers between devices, exchange(): return lax.all_to_all(value, axes, split_axis=0, concat_axis=0, tiled=True)  23.9 us
    pallas_call x1, Pallas kernels, attend(): pl.pallas_call(functools.partial(attend_kernel, members, seqs), in_specs=...  10.9 us
    ppermute x3, starting transfers between devices, across(): lax.ppermute(value, PLANE, [(i, i ^ steps) for i in range(width * lax.axi...  8.4 us
    ppermute x2, starting transfers between devices, swap(): return lax.ppermute(value, axis, [(0, 1), (1, 0)])  3.84 us
  transfers between devices with their start and end apart: 7, of which 4 were waited for; matrix products, arithmetic and copies ran while one was open for 1% of the time, Pallas kernels for 2%

profile of v5, /device:TPU:1, one launch (start us, length us, event | category | flops | bytes accessed | tf_op | source)
XLA Modules:
  0.0 154.6 jit_solution(1472583303850060895)
XLA Ops:
  0.7 1.7 %send_slots.1 = bf16[16,8,1536]{2,1,0:T(8,128)(2,1)} custom-call(bf16[1,8,2048]{2,1,0:T(8,128)(2,1)} %refs_0_.1, bf16[1,8,1024]{2,1,0:T(8,128)(2,1)} %refs_1_.1, s32[1,8]{1,0:T(1,128)} %refs_2_.1, bf16[16,128]{1,0:T(8,128)(2,1)} %bitcast.12, bf16[8,128]{1,0:T(8,128)(2,1)} %bitcast.13), custom_call_target="tpu_custom_call" | custom-call | bytes 393216 | tf_op jit(solution)/shard_map/send_slots/pallas_call | solution.py:171
  2.4 14.1 %all-to-all-start.3 = ((bf16[16,8,1536]{2,1,0:T(8,128)(2,1)}), bf16[16,8,1536]{2,1,0:T(8,128)(2,1)S(1)}, u32[]{:S(2)}, u32[]{:S(2)}) async-start(bf16[16,8,1536]{2,1,0:T(8,128)(2,1)} %send_slots.1), calls=%async_computation.3 | async-start | bytes 786432 | tf_op jit(solution)/shard_map/all_to_all | solution.py:434
  16.4 0.7 broadcast_compare_fusion
  17.1 0.8 broadcast_select_fusion.3.b_ref
  17.9 1.6 %copy-done = bf16[2,512,1024]{2,1,0:T(8,128)(2,1)S(1)} copy-done((bf16[2,512,1024]{2,1,0:T(8,128)(2,1)S(1)}, bf16[2,512,1024]{2,1,0:T(8,128)(2,1)}, u32[]{:S(2)}) %copy-start) | copy-done | bytes 2097176
  20.1 3.1 %collective-permute-start.3 = (bf16[1040,256]{1,0:T(8,128)(2,1)S(1)}, bf16[1040,256]{1,0:T(8,128)(2,1)S(1)}, u32[]{:S(2)}, u32[]{:S(2)}) collective-permute-start(bf16[1040,256]{1,0:T(8,128)(2,1)S(1)} %get-tuple-element.61), channel_id=1, source_target_pairs={{0,1},{1,0},{2,3},{3,2},{4,5},{5,4},{6,7},{7,6},{8,9},{9,8},{10,11... | collective-permute-start | bytes 1597448 | tf_op jit(solution)/shard_map/ppermute | solution.py:440
  23.2 3.2 %collective-permute-start.4 = (bf16[1040,256]{1,0:T(8,128)(2,1)S(1)}, bf16[1040,256]{1,0:T(8,128)(2,1)}, u32[]{:S(2)}, u32[]{:S(2)}) collective-permute-start(bf16[1040,256]{1,0:T(8,128)(2,1)S(1)} %get-tuple-element.62), channel_id=1, source_target_pairs={{0,4},{1,5},{2,6},{3,7},{4,0},{5,1},{6,2},{7,3},{8,12},{9,13},{10,... | collective-permute-start | bytes 1597448 | tf_op jit(solution)/shard_map/ppermute | solution.py:440
  26.4 2.0 %collective-permute-start.5 = (bf16[1040,256]{1,0:T(8,128)(2,1)S(1)}, bf16[1040,256]{1,0:T(8,128)(2,1)}, u32[]{:S(2)}, u32[]{:S(2)}) collective-permute-start(bf16[1040,256]{1,0:T(8,128)(2,1)S(1)} %get-tuple-element.63), channel_id=1, source_target_pairs={{0,5},{1,4},{2,7},{3,6},{4,1},{5,0},{6,3},{7,2},{8,13},{9,12},{10,... | collective-permute-start | bytes 1597448 | tf_op jit(solution)/shard_map/ppermute | solution.py:440
  28.5 1.3 plan.1.plan_ref
  29.8 8.2 %all-to-all-done.3.halves_ref = bf16[16,8,1536]{2,1,0:T(8,128)(2,1)S(1)} async-done(((bf16[16,8,1536]{2,1,0:T(8,128)(2,1)}), bf16[16,8,1536]{2,1,0:T(8,128)(2,1)S(1)}, u32[]{:S(2)}, u32[]{:S(2)}) %all-to-all-start.3) | async-done | bytes 393248 | tf_op jit(solution)/shard_map/all_to_all | solution.py:434
  38.6 1.9 %collective-permute-start.2 = (bf16[1,8,1536]{2,1,0:T(8,128)(2,1)S(1)}, bf16[1,8,1536]{2,1,0:T(8,128)(2,1)S(1)}, u32[]{:S(2)}, u32[]{:S(2)}) collective-permute-start(bf16[1,8,1536]{2,1,0:T(8,128)(2,1)S(1)} %get-tuple-element.59), channel_id=1, source_target_pairs={{0,32},{32,0},{1,33},{33,1},{2,34},{34,2},{3,35},{35,3},{4,36},{36... | collective-permute-start | bytes 73736 | tf_op jit(solution)/shard_map/ppermute | solution.py:430
  40.6 1.1 collective-permute-done.2.got_ref
  41.7 13.6 %all-gather.2 = bf16[6,8,2048]{2,1,0:T(8,128)(2,1)S(1)} all-gather(bf16[3,8,2048]{2,1,0:T(8,128)(2,1)S(1)} %get-tuple-element.60.own_ref), channel_id=4, replica_groups=mesh['zl'=8,'co'=2,'zh'=2,'y'=4,'x'=4] {'zh'}, dimensions={0}, use_global_device_ids=true | all-gather | bytes 294912 | tf_op jit(solution)/shard_map/all_gather | solution.py:444
  55.4 17.5 %all_to_all.34.q_ref = bf16[16,16,1664]{2,1,0:T(8,128)(2,1)S(1)} all-to-all(bf16[16,16,1664]{2,1,0:T(8,128)(2,1)S(1)} %pack_queries.3), channel_id=1, replica_groups=mesh['zl'=8,'co'=2,'zh'=2,'y'=4,'x'=4] {'y','x'}, dimensions={0} | all-to-all | bytes 1703936 | tf_op jit(solution)/shard_map/all_to_all | solution.py:434
  72.9 10.9 %attend.3 = bf16[16,16,1664]{2,1,0:T(8,128)(2,1)S(1)} custom-call(s32[10]{0:T(128)S(1)} %plan.1.plan_ref, bf16[16,16,1664]{2,1,0:T(8,128)(2,1)S(1)} %all_to_all.34.q_ref, bf16[1040,256]{1,0:T(8,128)(2,1)S(1)} %get-tuple-element.66.refs_0_, bf16[1040,256]{1,0:T(8,128)(2,1)S(1)} %collective-permute-done.3.refs_1_, ...), custom_call_target="tpu_custom_call" | custom-call | flops 3271557120 | bytes 3833856 | tf_op jit(solution)/shard_map/attend/pallas_call | solution.py:321
  83.7 13.4 %all_to_all.35.r_ref = bf16[16,16,1664]{2,1,0:T(8,128)(2,1)S(1)} all-to-all(bf16[16,16,1664]{2,1,0:T(8,128)(2,1)S(1)} %attend.3), channel_id=1, replica_groups=mesh['zl'=8,'co'=2,'zh'=2,'y'=4,'x'=4] {'y','x'}, dimensions={0} | all-to-all | bytes 1703936 | tf_op jit(solution)/shard_map/all_to_all | solution.py:434
  97.1 2.2 %fold_plane.3 = (f32[3,8,2048]{2,1,0:T(8,128)S(1)}, f32[3,8,128]{2,1,0:T(8,128)S(1)}, bf16[3,8,2176]{2,1,0:T(8,128)(2,1)S(1)}) custom-call(bf16[16,16,1664]{2,1,0:T(8,128)(2,1)S(1)} %all_to_all.35.r_ref), custom_call_target="tpu_custom_call" | custom-call | bytes 1703936 | tf_op jit(solution)/shard_map/fold_plane/pallas_call | solution.py:380
  99.3 21.8 %all-gather.3 = bf16[6,8,2176]{2,1,0:T(8,128)(2,1)S(1)} all-gather(bf16[3,8,2176]{2,1,0:T(8,128)(2,1)S(1)} %get-tuple-element.69), channel_id=5, replica_groups=mesh['zl'=8,'co'=2,'zh'=2,'y'=4,'x'=4] {'zh'}, dimensions={0}, use_global_device_ids=true | all-gather | bytes 313344 | tf_op jit(solution)/shard_map/all_gather | solution.py:444
  121.1 1.2 finish.3
  122.4 11.0 %all-to-all-start.6 = ((bf16[16,8,1024]{2,1,0:T(8,128)(2,1)}), bf16[16,8,1024]{2,1,0:T(8,128)(2,1)S(1)}, u32[]{:S(2)}, u32[]{:S(2)}) async-start(bf16[16,8,1024]{2,1,0:T(8,128)(2,1)} %get-tuple-element.71), calls=%async_computation.6 | async-start | bytes 524288 | tf_op jit(solution)/shard_map/all_to_all | solution.py:434
  134.6 15.8 %all-to-all-done.6.halves_ref = bf16[16,8,1024]{2,1,0:T(8,128)(2,1)S(1)} async-done(((bf16[16,8,1024]{2,1,0:T(8,128)(2,1)}), bf16[16,8,1024]{2,1,0:T(8,128)(2,1)S(1)}, u32[]{:S(2)}, u32[]{:S(2)}) %all-to-all-start.6) | async-done | bytes 262176 | tf_op jit(solution)/shard_map/all_to_all | solution.py:434
  150.9 1.9 %collective-permute-start.6 = (bf16[1,8,1024]{2,1,0:T(8,128)(2,1)S(1)}, bf16[1,8,1024]{2,1,0:T(8,128)(2,1)S(1)}, u32[]{:S(2)}, u32[]{:S(2)}) collective-permute-start(bf16[1,8,1024]{2,1,0:T(8,128)(2,1)S(1)} %get-tuple-element.74), channel_id=1, source_target_pairs={{0,32},{32,0},{1,33},{33,1},{2,34},{34,2},{3,35},{35,3},{4,36},{36... | collective-permute-start | bytes 49160 | tf_op jit(solution)/shard_map/ppermute | solution.py:430
  152.9 1.1 collective-permute-done.6
  154.0 0.6 join.5
  (18 shorter events, 2.4 us)
Async XLA Ops:
  0.6 39.9 %copy-start.3 = (bf16[2048]{0:T(1024)(128)(2,1)S(1)}, bf16[2048]{0:T(1024)(128)(2,1)}, u32[]{:S(2)}) copy-start(bf16[2048]{0:T(1024)(128)(2,1)} %param.20) | copy-start | bytes 12292
  0.6 27.9 %copy-start.1 = (s32[16]{0:T(128)S(1)}, s32[16]{0:T(128)}, u32[]{:S(2)}) copy-start(s32[16]{0:T(128)} %ids_ref.1) | copy-start | bytes 196
  0.7 39.9 %copy-start.2 = (bf16[2,8,2048]{2,1,0:T(8,128)(2,1)S(1)}, bf16[2,8,2048]{2,1,0:T(8,128)(2,1)}, u32[]{:S(2)}) copy-start(bf16[2,8,2048]{2,1,0:T(8,128)(2,1)} %param.13) | copy-start | bytes 196612
  2.4 35.7 %all-to-all-start.3 = ((bf16[16,8,1536]{2,1,0:T(8,128)(2,1)}), bf16[16,8,1536]{2,1,0:T(8,128)(2,1)S(1)}, u32[]{:S(2)}, u32[]{:S(2)}) async-start(bf16[16,8,1536]{2,1,0:T(8,128)(2,1)} %send_slots.1), calls=%async_computation.3 | async-start | bytes 786432 | tf_op jit(solution)/shard_map/all_to_all | solution.py:434
  17.9 1.6 %copy-start = (bf16[2,512,1024]{2,1,0:T(8,128)(2,1)S(1)}, bf16[2,512,1024]{2,1,0:T(8,128)(2,1)}, u32[]{:S(2)}) copy-start(bf16[2,512,1024]{2,1,0:T(8,128)(2,1)} %s_ref.1) | copy-start | bytes 6291460
  20.1 35.2 %collective-permute-start.3 = (bf16[1040,256]{1,0:T(8,128)(2,1)S(1)}, bf16[1040,256]{1,0:T(8,128)(2,1)S(1)}, u32[]{:S(2)}, u32[]{:S(2)}) collective-permute-start(bf16[1040,256]{1,0:T(8,128)(2,1)S(1)} %get-tuple-element.61), channel_id=1, source_target_pairs={{0,1},{1,0},{2,3},{3,2},{4,5},{5,4},{6,7},{7,6},{8,9},{9,8},{10,11... | collective-permute-start | bytes 1597448 | tf_op jit(solution)/shard_map/ppermute | solution.py:440
  23.2 32.1 %collective-permute-start.4 = (bf16[1040,256]{1,0:T(8,128)(2,1)S(1)}, bf16[1040,256]{1,0:T(8,128)(2,1)}, u32[]{:S(2)}, u32[]{:S(2)}) collective-permute-start(bf16[1040,256]{1,0:T(8,128)(2,1)S(1)} %get-tuple-element.62), channel_id=1, source_target_pairs={{0,4},{1,5},{2,6},{3,7},{4,0},{5,1},{6,2},{7,3},{8,12},{9,13},{10,... | collective-permute-start | bytes 1597448 | tf_op jit(solution)/shard_map/ppermute | solution.py:440
  26.4 28.9 %collective-permute-start.5 = (bf16[1040,256]{1,0:T(8,128)(2,1)S(1)}, bf16[1040,256]{1,0:T(8,128)(2,1)}, u32[]{:S(2)}, u32[]{:S(2)}) collective-permute-start(bf16[1040,256]{1,0:T(8,128)(2,1)S(1)} %get-tuple-element.63), channel_id=1, source_target_pairs={{0,5},{1,4},{2,7},{3,6},{4,1},{5,0},{6,3},{7,2},{8,13},{9,12},{10,... | collective-permute-start | bytes 1597448 | tf_op jit(solution)/shard_map/ppermute | solution.py:440
  38.6 3.1 %collective-permute-start.2 = (bf16[1,8,1536]{2,1,0:T(8,128)(2,1)S(1)}, bf16[1,8,1536]{2,1,0:T(8,128)(2,1)S(1)}, u32[]{:S(2)}, u32[]{:S(2)}) collective-permute-start(bf16[1,8,1536]{2,1,0:T(8,128)(2,1)S(1)} %get-tuple-element.59), channel_id=1, source_target_pairs={{0,32},{32,0},{1,33},{33,1},{2,34},{34,2},{3,35},{35,3},{4,36},{36... | collective-permute-start | bytes 73736 | tf_op jit(solution)/shard_map/ppermute | solution.py:430
  122.4 28.0 %all-to-all-start.6 = ((bf16[16,8,1024]{2,1,0:T(8,128)(2,1)}), bf16[16,8,1024]{2,1,0:T(8,128)(2,1)S(1)}, u32[]{:S(2)}, u32[]{:S(2)}) async-start(bf16[16,8,1024]{2,1,0:T(8,128)(2,1)} %get-tuple-element.71), calls=%async_computation.6 | async-start | bytes 524288 | tf_op jit(solution)/shard_map/all_to_all | solution.py:434
  150.9 3.1 %collective-permute-start.6 = (bf16[1,8,1024]{2,1,0:T(8,128)(2,1)S(1)}, bf16[1,8,1024]{2,1,0:T(8,128)(2,1)S(1)}, u32[]{:S(2)}, u32[]{:S(2)}) collective-permute-start(bf16[1,8,1024]{2,1,0:T(8,128)(2,1)S(1)} %get-tuple-element.74), channel_id=1, source_target_pairs={{0,32},{32,0},{1,33},{33,1},{2,34},{34,2},{3,35},{35,3},{4,36},{36... | collective-permute-start | bytes 49160 | tf_op jit(solution)/shard_map/ppermute | solution.py:430
